TPU v7x, 32 devices: a whole 2x2x4 slice. The times are simulated.
32 devices in a mesh: blk: 8 (over y, x, core), rep: 4 (over z).
Axes of the slice: x: 2, y: 2, z: 4, core: 2. Of those that a mesh axis runs over, the one named last changes fastest.
Arguments:
- point_pool: bfloat16 [40960, 1024], P(('blk', 'rep')), may hold values from -8 to 8
- batch_rows: int32 [32768], P(('blk', 'rep')), may hold values from 0 to 1279
- targets: bfloat16 [32768, 256], P(('blk', 'rep')), may hold values from -6 to 6
- center_pool: bfloat16 [512, 1024], P('blk'), may hold values from -8 to 8
- center_rows: int32 [256], P('blk'), may hold values from 0 to 63
- coefs: bfloat16 [256, 256], P('blk'), may hold values from -3 to 3
Outputs:
- residual: float32 [32768, 256], P(('blk', 'rep'))
- coef_grad: float32 [256, 256], P('blk')
All inputs are finite; a program needn't handle non-finite values.
Results may differ from a plain program's by a relative error of at most 0.0016.
Values may be sent and summed in bfloat16 or wider, within the bound.
No kernel may reach another device: no remote copies, remote signals or barrier semaphores. Data moves between devices by JAX's collectives and lax.ppermute only.
A program may use at most 64 MiB of HBM per device.

v0:
```python
import jax
import jax.numpy as jnp
from jax import lax
from jax.sharding import PartitionSpec as P


def kernel_block(points, point_norm, center_piece):
    center_norm = jnp.sum(center_piece.astype(jnp.float32) ** 2, axis=1)
    inner = lax.dot_general(
        points, center_piece, (((1,), (1,)), ((), ())), preferred_element_type=jnp.float32
    )
    distance = point_norm[:, None] + center_norm[None, :] - 2.0 * inner
    return jnp.exp(-distance / points.shape[1]).astype(jnp.bfloat16)


def transposed_product(kernel, residual_b):
    return lax.dot_general(
        kernel, residual_b, (((0,), (0,)), ((), ())), preferred_element_type=jnp.float32
    )


def per_device(point_pool, batch_rows, targets, center_pool, center_rows, coefs):
    points = jnp.take(point_pool, batch_rows, axis=0)
    centers = jnp.take(center_pool, center_rows, axis=0)
    point_norm = jnp.sum(points.astype(jnp.float32) ** 2, axis=1)
    kernel = kernel_block(points, point_norm, lax.all_gather(centers, "blk", axis=0, tiled=True))
    residual = jnp.dot(
        kernel, lax.all_gather(coefs, "blk", axis=0, tiled=True), preferred_element_type=jnp.float32
    ) - targets.astype(jnp.float32)
    residual_b = residual.astype(jnp.bfloat16)
    grad_terms = transposed_product(
        kernel_block(points, point_norm, lax.all_gather(centers, "blk", axis=0, tiled=True)),
        residual_b,
    )
    partial_grad = lax.psum_scatter(grad_terms, "blk", scatter_dimension=0, tiled=True)
    coef_grad = lax.psum(partial_grad, "rep")
    return (residual, coef_grad)


def solution(mesh):
    return jax.shard_map(
        per_device,
        mesh=mesh,
        in_specs=(
            P(("blk", "rep"), None),
            P(("blk", "rep")),
            P(("blk", "rep"), None),
            P("blk", None),
            P("blk"),
            P("blk", None),
        ),
        out_specs=(P(("blk", "rep"), None), P("blk", None)),
        check_vma=False,
    )
```

profile of v0, /device:TPU:0, one launch (start us, length us, event | category | flops | bytes accessed | tf_op | source)
XLA Modules:
  0.0 104.8 jit_solution(6035580587863414867)
XLA Ops:
  7.2 0.0 copy-start
  7.2 0.0 reduce-scatter.2.cloned.1.call-start
  7.2 0.8 fusion.7
  8.1 0.7 compare_and_fusion
  8.8 0.7 compare_select_fusion.1
  9.4 0.7 compare_and_fusion.1
  10.1 1.6 %gather_fusion.1 = bf16[32,1024]{1,0:T(8,128)(2,1)S(1)} fusion(bf16[64,1024]{1,0:T(8,128)(2,1)} %param.9, s32[1024]{0:T(1024)S(1)} %pad_clamp_fusion), kind=kCustom, calls=%fused_computation.1 | custom fusion | bytes 131200 | tf_op jit(solution)/shard_map/jit(_take)/gather | solution.py:24
  11.7 0.1 broadcast_select_fusion.2
  11.8 11.3 %all_gather.7 = bf16[256,1024]{1,0:T(8,128)(2,1)S(1)} all-gather(bf16[32,1024]{1,0:T(8,128)(2,1)S(1)} %broadcast_select_fusion.2), channel_id=1, replica_groups=mesh['blk'=8,'rep'=4] {'blk'}, dimensions={0}, use_global_device_ids=true | all-gather | bytes 589824 | tf_op jit(solution)/shard_map/all_gather | solution.py:26
  23.1 0.2 multiply_reduce_fusion.1
  23.3 9.2 %all_gather.8 = bf16[256,256]{1,0:T(8,128)(2,1)S(1)} all-gather(bf16[32,256]{1,0:T(8,128)(2,1)} %param.11), channel_id=1, replica_groups=mesh['blk'=8,'rep'=4] {'blk'}, dimensions={0}, use_global_device_ids=true | all-gather | bytes 147456 | tf_op jit(solution)/shard_map/all_gather | solution.py:28
  32.5 0.0 copy-done
  32.5 5.4 %gather_fusion = bf16[1024,1024]{1,0:T(8,128)(2,1)} fusion(bf16[1280,1024]{1,0:T(8,128)(2,1)S(1)} %copy-done, s32[1024]{0:T(1024)S(1)} %fusion.7), kind=kCustom, calls=%fused_computation | custom fusion | bytes 4198400 | tf_op jit(solution)/shard_map/jit(_take)/gather | solution.py:23
  37.8 2.5 %multiply_reduce_fusion = f32[1024]{0:T(1024)S(1)} fusion(bf16[1024,1024]{1,0:T(8,128)(2,1)} %gather_fusion, pred[1024]{0:T(1024)(128)(4,1)S(1)} %compare_and_fusion), kind=kLoop, calls=%fused_computation.2 | loop fusion | flops 4193280 | bytes 2102272 | tf_op jit(solution)/shard_map/reduce_sum | solution.py:25
  40.3 0.0 copy-start.3
  40.3 0.8 fusion.4
  41.1 0.2 copy-done.3
  41.3 0.3 convolution_subtract_fusion
  41.6 0.0 copy-start.2
  41.7 1.0 copy-done.2
  42.6 1.0 fusion.5
  43.7 0.0 reduce-scatter.2.cloned.1.call-update
  43.7 34.1 %reduce-scatter.2.cloned.1.call-done = f32[32,256]{1,0:T(8,128)} async-done(((f32[256,256]{1,0:T(8,128)}), f32[32,256]{1,0:T(8,128)}) %reduce-scatter.2.cloned.1.call-update) | async-done | bytes 32784 | tf_op jit(solution)/shard_map/reduce_scatter | solution.py:35
  77.7 20.2 %psum.7 = f32[32,256]{1,0:T(8,128)} all-reduce(f32[32,256]{1,0:T(8,128)} %reduce-scatter.2.cloned.1.call-done), channel_id=1, replica_groups=mesh['blk'=8,'rep'=4] {'rep'}, use_global_device_ids=true, to_apply=%region_3.4 | all-reduce | flops 8192 | bytes 65536 | tf_op jit(solution)/shard_map/psum | solution.py:36
  (3 shorter events, 0.0 us)
Async XLA Ops:
  7.2 25.3 %copy-start = (bf16[1280,1024]{1,0:T(8,128)(2,1)S(1)}, bf16[1280,1024]{1,0:T(8,128)(2,1)}, u32[]{:S(2)}) copy-start(bf16[1280,1024]{1,0:T(8,128)(2,1)} %param.6) | copy-start | bytes 7864324
  7.2 70.6 %reduce-scatter.2.cloned.1.call-start = ((), (), s32[]{:S(2)}) async-start(), calls=%async_computation.1 | async-start | bytes 294912 | tf_op jit(solution)/shard_map/reduce_scatter | solution.py:35
  37.8 2.5 %copy-start.1 = (bf16[1024,1024]{1,0:T(8,128)(2,1)S(1)}, bf16[1024,1024]{1,0:T(8,128)(2,1)}, u32[]{:S(2)}) copy-start(bf16[1024,1024]{1,0:T(8,128)(2,1)} %gather_fusion) | copy-start | bytes 6291460
  40.3 1.0 copy-start.3
  41.6 1.0 copy-start.2
Sparse Core Ops, SparseCore 0:
  43.8 33.8 reduce-scatter.1
where the time goes:
time: 105 us
  blocking collectives  40.7 us (39%)
  waiting for transfers between devices  34.1 us (32%)
  between operations  14.1 us (13%)
  local copies, waits for them, and re-layouts  8.14 us (8%)
  other arithmetic  5.6 us (5%)
  matrix products  2.16 us (2%)
    reduce_scatter x1, waiting for transfers between devices, per_device(): lax.psum_scatter(grad_terms, 'blk', scatter_dimension=0, tiled=True)  34.1 us
    psum x1, blocking collectives, per_device(): coef_grad = lax.psum(partial_grad, 'rep')  20.2 us
    all_gather x1, blocking collectives, per_device(): lax.all_gather(centers, 'blk', axis=0, tiled=True)  11.3 us
    all_gather x1, blocking collectives, per_device(): lax.all_gather(coefs, 'blk', axis=0, tiled=True)  9.2 us
    gather x1, local copies, waits for them, and re-layouts, per_device(): points = jnp.take(point_pool, batch_rows, axis=0)  5.35 us
    reduce_sum x1, other arithmetic, per_device(): point_norm = jnp.sum(points.astype(jnp.float32) ** 2, axis=1)  2.48 us
  transfers between devices with their start and end apart: 1, of which 1 were waited for; matrix products, arithmetic and copies ran while one was open for 0% of the time, Pallas kernels for 0%

commit v1 on v0

v1 whole, which is shorter than its diff:
```python
import functools

import jax
import jax.numpy as jnp
from jax import lax
from jax.experimental import pallas as pl
from jax.experimental.pallas import tpu as pltpu
from jax.sharding import PartitionSpec as P

F32, BF16 = jnp.float32, jnp.bfloat16
VMEM = pl.BlockSpec(memory_space=pltpu.VMEM)
ANY = pl.BlockSpec(memory_space=pl.ANY)


def dot(a, b, contract):
    return lax.dot_general(a, b, (contract, ((), ())), preferred_element_type=F32)


def piece_kernel(rows_ref, pool_ref, coefs_ref, piece_ref):
    count, width = pool_ref.shape
    picked = lax.broadcasted_iota(jnp.int32, (count, rows_ref.shape[1]), 0) == rows_ref[...]
    piece_ref[:, :width] = dot(picked.astype(F32).astype(BF16), pool_ref[...], ((0,), (0,))).astype(BF16)
    piece_ref[:, width:] = coefs_ref[...]


def points_kernel(rows_ref, pool_ref, points_ref, norm_ref, picks, squares):
    count, width = pool_ref.shape
    lane = lax.broadcasted_iota(jnp.int32, (128, 128), 1)
    for j in range(rows_ref.shape[0]):
        row = jnp.broadcast_to(rows_ref[j : j + 1, :], (128, 128)).T
        for g in range(count // 128):
            picks[j * 128 : (j + 1) * 128, g * 128 : (g + 1) * 128] = (
                (row == lane + g * 128).astype(F32).astype(BF16)
            )
    for n in range(width // 256):
        block = dot(picks[...], pool_ref[:, n * 256 : (n + 1) * 256], ((1,), (0,)))
        points_ref[:, n * 256 : (n + 1) * 256] = block.astype(BF16)
        square = block[:, :128] * block[:, :128] + block[:, 128:] * block[:, 128:]
        squares[...] = square if n == 0 else squares[...] + square
    norm_ref[...] = jnp.sum(squares[...], axis=1, keepdims=True)


def residual_kernel(pieces, width, points_ref, norm_ref, targets_ref, *refs):
    piece_refs, (residual_hbm, kept_ref, sent_ref), (centers, coefs, residual, sem) = (
        refs[:pieces],
        refs[pieces : pieces + 3],
        refs[pieces + 3 :],
    )
    each = piece_refs[0].shape[0]
    for i, ref in enumerate(piece_refs):
        centers[i * each : (i + 1) * each, :] = ref[:, :width]
        coefs[i * each : (i + 1) * each, :] = ref[:, width:]
    squares = jnp.zeros((pieces * each, 128), F32)
    for g in range(width // 128):
        part = centers[:, g * 128 : (g + 1) * 128].astype(F32)
        squares = squares + part * part
    center_norm = jnp.sum(squares.T, axis=0, keepdims=True)
    rows = 256
    grad = jnp.zeros((pieces * each, coefs.shape[1]), F32)
    copies = []
    for m in range(points_ref.shape[0] // rows):
        at = slice(m * rows, (m + 1) * rows)
        inner = dot(points_ref[at, :], centers[...], ((1,), (1,)))
        distance = norm_ref[at, :] + center_norm - 2.0 * inner
        kernel = jnp.exp(distance * (-1.0 / width)).astype(BF16)
        left = dot(kernel, coefs[...], ((1,), (0,))) - targets_ref[at, :].astype(F32)
        residual[at, :] = left
        copy = pltpu.make_async_copy(residual.at[at, :], residual_hbm.at[at, :], sem.at[m])
        copy.start()
        copies.append(copy)
        grad = grad + dot(kernel, left.astype(BF16), ((0,), (0,)))
    half = pieces * each // 2
    kept_ref[...] = grad[:half]
    sent_ref[...] = grad[half:]
    for copy in copies:
        copy.wait()


def swap(x, axes, sizes, flips):
    blk, rep = sizes
    pairs = [
        (b * rep + r, (b ^ flips[0]) * rep + (r ^ flips[1])) for b in range(blk) for r in range(rep)
    ]
    return lax.ppermute(x, axes, pairs)


def digits(size, low):
    groups = []
    while 1 << low < size:
        high = min(low + 2, size.bit_length() - 1)
        groups.append([d << low for d in range(1, 1 << (high - low))])
        low = high
    return groups


def pair_sum(parts):
    while len(parts) > 1:
        parts = [parts[i] + parts[i + 1] for i in range(0, len(parts), 2)]
    return parts[0]


def per_device(sizes, point_pool, batch_rows, targets, center_pool, center_rows, coefs):
    send = functools.partial(swap, axes=("blk", "rep"), sizes=sizes)
    each, outs = coefs.shape
    width = point_pool.shape[1]
    count = batch_rows.shape[0]

    piece = pl.pallas_call(
        piece_kernel,
        out_shape=jax.ShapeDtypeStruct((each, width + outs), BF16),
        in_specs=[VMEM] * 3,
        out_specs=VMEM,
        name="piece",
    )(center_rows.reshape(1, each), center_pool, coefs)

    chips, reps = digits(sizes[0], 1), digits(sizes[1], 0)
    held = {0: piece}
    for group in chips:
        for s, x in list(held.items()):
            for d in reversed(group):
                held[s ^ d] = send(x, flips=(d, 0))
    for s, x in list(held.items()):
        held[s ^ 1] = send(x, flips=(1, 0))

    points, point_norm = pl.pallas_call(
        points_kernel,
        out_shape=(
            jax.ShapeDtypeStruct((count, width), BF16),
            jax.ShapeDtypeStruct((count, 1), F32),
        ),
        in_specs=[VMEM] * 2,
        out_specs=(VMEM, VMEM),
        scratch_shapes=[
            pltpu.VMEM((count, point_pool.shape[0]), BF16),
            pltpu.VMEM((count, 128), F32),
        ],
        compiler_params=pltpu.CompilerParams(vmem_limit_bytes=32 << 20),
        cost_estimate=pl.CostEstimate(flops=2 << 30, bytes_accessed=5 << 20, transcendentals=0),
        name="points",
    )(batch_rows.reshape(count // 128, 128), point_pool)

    near = [0] + [d for d in chips[0]]
    far = [0]
    for group in chips[1:]:
        far = [f ^ d for d in [0] + group for f in far]
    kept_slots = [f ^ (n if n else 1) for f in far for n in near]
    slots = kept_slots + [s ^ 1 for s in kept_slots]
    residual, kept, sent = pl.pallas_call(
        functools.partial(residual_kernel, len(slots), width),
        out_shape=(
            jax.ShapeDtypeStruct((count, outs), F32),
            jax.ShapeDtypeStruct((len(kept_slots) * each, outs), F32),
            jax.ShapeDtypeStruct((len(kept_slots) * each, outs), F32),
        ),
        in_specs=[VMEM] * (3 + len(slots)),
        out_specs=(ANY, VMEM, VMEM),
        scratch_shapes=[
            pltpu.VMEM((len(slots) * each, width), BF16),
            pltpu.VMEM((len(slots) * each, outs), BF16),
            pltpu.VMEM((count, outs), F32),
            pltpu.SemaphoreType.DMA((count // 256,)),
        ],
        compiler_params=pltpu.CompilerParams(vmem_limit_bytes=32 << 20),
        name="residual",
    )(points, point_norm, targets, *[held[s] for s in slots])

    total = (kept + send(sent, flips=(1, 0))).reshape(len(far), len(near), each, outs)
    blocks = {f: total[i] for i, f in enumerate(far)}
    for group in reversed(chips[1:]):
        low = [f for f in blocks if f < group[0]]
        got = {d: {f: send(blocks[f ^ d], flips=(d, 0)) for f in low} for d in reversed(group)}
        blocks = {f: pair_sum([blocks[f]] + [got[d][f] for d in group]) for f in low}
    rows = blocks[0]
    got = {d: send(rows[i + 1], flips=(d ^ 1, 0)) for i, d in reversed(list(enumerate(chips[0])))}
    mine = pair_sum([rows[0]] + [got[d] for d in chips[0]])
    flip = 1
    for group in reps:
        got = {d: send(mine, flips=(flip, d)) for d in reversed(group)}
        first = send(mine, flips=(1, 0)) if flip else mine
        mine, flip = pair_sum([first] + [got[d] for d in group]), 0
    return residual, mine


def solution(mesh):
    return jax.shard_map(
        functools.partial(per_device, (mesh.shape["blk"], mesh.shape["rep"])),
        mesh=mesh,
        in_specs=(
            P(("blk", "rep"), None),
            P(("blk", "rep")),
            P(("blk", "rep"), None),
            P("blk", None),
            P("blk"),
            P("blk", None),
        ),
        out_specs=(P(("blk", "rep"), None), P("blk", None)),
        check_vma=False,
    )
```

time: 105 us -> 36 us (0.34)
  blocking collectives: 40.7 us -> 0 us
  waiting for transfers between devices: 34.1 us -> 11.6 us
  between operations: 14.1 us -> 0.71 us
  starting transfers between devices: 0.04 us -> 12.6 us
  Pallas kernels: 0 us -> 7.75 us
  local copies, waits for them, and re-layouts: 8.14 us -> 2.44 us
  other arithmetic: 5.6 us -> 0.65 us
  matrix products: 2.16 us -> 0 us
    reduce_scatter x1 -> x0, waiting for transfers between devices: 34.1 us -> none  [per_device(): lax.psum_scatter(grad_terms, 'blk', scatter_dimension=0, tiled=True)]
    all_gather x2 -> x0, blocking collectives: 20.5 us -> none  [the longest x1 11.3 us: per_device(): lax.all_gather(centers, 'blk', axis=0, tiled=True)]
    psum x1 -> x0, blocking collectives: 20.2 us -> none  [per_device(): coef_grad = lax.psum(partial_grad, 'rep')]
    ppermute x0 -> x15, starting transfers between devices: none -> 12.6 us  [swap(): return lax.ppermute(x, axes, pairs)]
    ppermute x0 -> x15, waiting for transfers between devices: none -> 11.6 us  [swap(): return lax.ppermute(x, axes, pairs)]
    pallas_call x0 -> x3, Pallas kernels: none -> 7.75 us  [the longest x1 3.32 us: per_device(): pl.pallas_call(points_kernel, out_shape=(jax.ShapeDtypeStruct((count, wid...]
    gather x2 -> x0, local copies, waits for them, and re-layouts: 6.95 us -> none  [the longest x1 5.35 us: per_device(): points = jnp.take(point_pool, batch_rows, axis=0)]
    reduce_sum x2 -> x0, other arithmetic: 2.66 us -> none  [the longest x1 2.48 us: per_device(): point_norm = jnp.sum(points.astype(jnp.float32) ** 2, axis=1)]
  transfers between devices with their start and end apart: 1 -> 15, of which waited for: 1 -> 9; matrix products, arithmetic and copies ran while one was open for 0% -> 0% of each run, Pallas kernels for 0% -> 9%
where the time goes in v1:
time: 36 us; the launch traced here: 35.8 us
  starting transfers between devices  12.6 us (35%)
  waiting for transfers between devices  11.6 us (32%)
  Pallas kernels  7.75 us (22%)
  local copies, waits for them, and re-layouts  2.44 us (7%)
  between operations  0.71 us (2%)
  other arithmetic  0.65 us (2%)
    ppermute x15, starting transfers between devices, swap(): return lax.ppermute(x, axes, pairs)  12.6 us
    ppermute x15, waiting for transfers between devices, swap(): return lax.ppermute(x, axes, pairs)  11.6 us
    pallas_call x1, Pallas kernels, per_device(): pl.pallas_call(points_kernel, out_shape=(jax.ShapeDtypeStruct((count, wid...  3.32 us
    pallas_call x1, Pallas kernels, per_device(): pl.pallas_call(functools.partial(residual_kernel, len(slots), width), out...  2.69 us
    unnamed x8, local copies, waits for them, and re-layouts  2.43 us
    pallas_call x1, Pallas kernels, per_device(): pl.pallas_call(piece_kernel, out_shape=jax.ShapeDtypeStruct((each, width...  1.73 us
  transfers between devices with their start and end apart: 15, of which 9 were waited for; matrix products, arithmetic and copies ran while one was open for 0% of the time, Pallas kernels for 9%

profile of v1, /device:TPU:0, one launch (start us, length us, event | category | flops | bytes accessed | tf_op | source)
XLA Modules:
  0.0 35.8 jit_solution(9378391514850399622)
XLA Ops:
  0.6 1.7 %piece.1.refs_4_ = bf16[32,1280]{1,0:T(8,128)(2,1)} custom-call(s32[1,32]{1,0:T(1,128)} %bitcast.3, bf16[64,1024]{1,0:T(8,128)(2,1)} %pool_ref.3, bf16[32,256]{1,0:T(8,128)(2,1)} %coefs_ref.1), custom_call_target="tpu_custom_call" | custom-call | tf_op jit(solution)/shard_map/piece/pallas_call | solution.py:108
  2.4 3.9 %collective-permute-start.3 = (bf16[32,1280]{1,0:T(8,128)(2,1)}, bf16[32,1280]{1,0:T(8,128)(2,1)S(1)}, u32[]{:S(2)}, u32[]{:S(2)}) collective-permute-start(bf16[32,1280]{1,0:T(8,128)(2,1)} %piece.1.refs_4_), channel_id=1, source_target_pairs={{0,24},{1,25},{2,26},{3,27},{4,28},{5,29},{6,30},{7,31},{8,16},{9,... | collective-permute-start | bytes 245768 | tf_op jit(solution)/shard_map/ppermute | solution.py:84
  6.3 0.5 %collective-permute-start.2 = (bf16[32,1280]{1,0:T(8,128)(2,1)}, bf16[32,1280]{1,0:T(8,128)(2,1)S(1)}, u32[]{:S(2)}, u32[]{:S(2)}) collective-permute-start(bf16[32,1280]{1,0:T(8,128)(2,1)} %piece.1.refs_4_), channel_id=1, source_target_pairs={{0,16},{1,17},{2,18},{3,19},{4,20},{5,21},{6,22},{7,23},{8,24},{9,... | collective-permute-start | bytes 245768 | tf_op jit(solution)/shard_map/ppermute | solution.py:84
  6.8 2.3 %collective-permute-done.3.refs_3_ = bf16[32,1280]{1,0:T(8,128)(2,1)S(1)} collective-permute-done((bf16[32,1280]{1,0:T(8,128)(2,1)}, bf16[32,1280]{1,0:T(8,128)(2,1)S(1)}, u32[]{:S(2)}, u32[]{:S(2)}) %collective-permute-start.3) | collective-permute-done | bytes 81952 | tf_op jit(solution)/shard_map/ppermute | solution.py:84
  9.2 1.8 %collective-permute-done.2.refs_2_ = bf16[32,1280]{1,0:T(8,128)(2,1)S(1)} collective-permute-done((bf16[32,1280]{1,0:T(8,128)(2,1)}, bf16[32,1280]{1,0:T(8,128)(2,1)S(1)}, u32[]{:S(2)}, u32[]{:S(2)}) %collective-permute-start.2) | collective-permute-done | bytes 81952 | tf_op jit(solution)/shard_map/ppermute | solution.py:84
  10.9 0.5 %collective-permute-done.1.refs_1_ = bf16[32,1280]{1,0:T(8,128)(2,1)S(1)} collective-permute-done((bf16[32,1280]{1,0:T(8,128)(2,1)}, bf16[32,1280]{1,0:T(8,128)(2,1)S(1)}, u32[]{:S(2)}, u32[]{:S(2)}) %collective-permute-start.1) | collective-permute-done | bytes 81952 | tf_op jit(solution)/shard_map/ppermute | solution.py:84
  11.4 1.7 %copy-done.2 = bf16[1280,1024]{1,0:T(8,128)(2,1)S(1)} copy-done((bf16[1280,1024]{1,0:T(8,128)(2,1)S(1)}, bf16[1280,1024]{1,0:T(8,128)(2,1)}, u32[]{:S(2)}) %copy-start.2) | copy-done | bytes 2621464
  13.2 0.7 %copy-done.3 = s32[1024]{0:T(1024)S(1)} copy-done((s32[1024]{0:T(1024)S(1)}, s32[1024]{0:T(1024)}, u32[]{:S(2)}) %copy-start.3) | copy-done | bytes 4120
  13.9 3.3 %points.1 = (bf16[1024,1024]{1,0:T(8,128)(2,1)S(1)}, f32[1024,1]{1,0:T(8,128)S(1)}) custom-call(s32[8,128]{1,0:T(8,128)S(1)} %bitcast.2, bf16[1280,1024]{1,0:T(8,128)(2,1)S(1)} %copy-done.2), custom_call_target="tpu_custom_call" | custom-call | flops 2147483648 | bytes 5242880 | tf_op jit(solution)/shard_map/points/pallas_call | solution.py:125
  17.2 2.7 %residual.1 = (f32[1024,256]{1,0:T(8,128)}, f32[128,256]{1,0:T(8,128)S(1)}, f32[128,256]{1,0:T(8,128)S(1)}) custom-call(bf16[1024,1024]{1,0:T(8,128)(2,1)S(1)} %get-tuple-element.7.points_ref, f32[1024,1]{1,0:T(8,128)S(1)} %get-tuple-element.8.norm_ref, bf16[1024,256]{1,0:T(8,128)(2,1)S(1)} %copy-done, bf16[32,1280]{1,0:T(8,128)(2,1)S(1)} %collective-permute-done.refs_0_, ...), custom_call_target="tpu_custom_call" | custom-call | tf_op jit(solution)/shard_map/residual/pallas_call | solution.py:148
  19.9 0.6 %collective-permute-start.7 = (f32[128,256]{1,0:T(8,128)S(1)}, f32[128,256]{1,0:T(8,128)S(1)}, u32[]{:S(2)}, u32[]{:S(2)}) collective-permute-start(f32[128,256]{1,0:T(8,128)S(1)} %get-tuple-element.11), channel_id=1, source_target_pairs={{0,4},{1,5},{2,6},{3,7},{4,0},{5,1},{6,2},{7,3},{8,12},{9,13},{10,... | collective-permute-start | bytes 393224 | tf_op jit(solution)/shard_map/ppermute | solution.py:84
  20.5 1.0 %collective-permute-done.7 = f32[128,256]{1,0:T(8,128)S(1)} collective-permute-done((f32[128,256]{1,0:T(8,128)S(1)}, f32[128,256]{1,0:T(8,128)S(1)}, u32[]{:S(2)}, u32[]{:S(2)}) %collective-permute-start.7) | collective-permute-done | bytes 131104 | tf_op jit(solution)/shard_map/ppermute | solution.py:84
  21.5 1.6 %collective-permute-start.10 = (f32[32,256]{1,0:T(8,128)S(1)}, f32[32,256]{1,0:T(8,128)S(1)}, u32[]{:S(2)}, u32[]{:S(2)}) collective-permute-start(f32[32,256]{1,0:T(8,128)S(1)} %get-tuple-element.12), channel_id=1, source_target_pairs={{0,28},{1,29},{2,30},{3,31},{4,24},{5,25},{6,26},{7,27},{8,20},{9,... | collective-permute-start | bytes 98312 | tf_op jit(solution)/shard_map/ppermute | solution.py:84
  23.1 1.0 %collective-permute-start.9 = (f32[32,256]{1,0:T(8,128)S(1)}, f32[32,256]{1,0:T(8,128)S(1)}, u32[]{:S(2)}, u32[]{:S(2)}) collective-permute-start(f32[32,256]{1,0:T(8,128)S(1)} %get-tuple-element.13), channel_id=1, source_target_pairs={{0,20},{1,21},{2,22},{3,23},{4,16},{5,17},{6,18},{7,19},{8,28},{9,... | collective-permute-start | bytes 98312 | tf_op jit(solution)/shard_map/ppermute | solution.py:84
  24.1 0.7 %collective-permute-start.8 = (f32[32,256]{1,0:T(8,128)S(1)}, f32[32,256]{1,0:T(8,128)S(1)}, u32[]{:S(2)}, u32[]{:S(2)}) collective-permute-start(f32[32,256]{1,0:T(8,128)S(1)} %get-tuple-element.14), channel_id=1, source_target_pairs={{0,12},{1,13},{2,14},{3,15},{4,8},{5,9},{6,10},{7,11},{8,4},{9,5},... | collective-permute-start | bytes 98312 | tf_op jit(solution)/shard_map/ppermute | solution.py:84
  24.8 1.1 %collective-permute-done.10 = f32[32,256]{1,0:T(8,128)S(1)} collective-permute-done((f32[32,256]{1,0:T(8,128)S(1)}, f32[32,256]{1,0:T(8,128)S(1)}, u32[]{:S(2)}, u32[]{:S(2)}) %collective-permute-start.10) | collective-permute-done | bytes 32800 | tf_op jit(solution)/shard_map/ppermute | solution.py:84
  25.8 1.2 %collective-permute-done.9 = f32[32,256]{1,0:T(8,128)S(1)} collective-permute-done((f32[32,256]{1,0:T(8,128)S(1)}, f32[32,256]{1,0:T(8,128)S(1)}, u32[]{:S(2)}, u32[]{:S(2)}) %collective-permute-start.9) | collective-permute-done | bytes 32800 | tf_op jit(solution)/shard_map/ppermute | solution.py:84
  27.0 0.4 %collective-permute-done.8 = f32[32,256]{1,0:T(8,128)S(1)} collective-permute-done((f32[32,256]{1,0:T(8,128)S(1)}, f32[32,256]{1,0:T(8,128)S(1)}, u32[]{:S(2)}, u32[]{:S(2)}) %collective-permute-start.8) | collective-permute-done | bytes 32800 | tf_op jit(solution)/shard_map/ppermute | solution.py:84
  27.4 3.4 %collective-permute-start.14 = (f32[32,256]{1,0:T(8,128)S(1)}, f32[32,256]{1,0:T(8,128)S(1)}, u32[]{:S(2)}, u32[]{:S(2)}) collective-permute-start(f32[32,256]{1,0:T(8,128)S(1)} %fusion), channel_id=1, source_target_pairs={{0,7},{1,6},{2,5},{3,4},{4,3},{5,2},{6,1},{7,0},{8,15},{9,14},{10,... | collective-permute-start | bytes 98312 | tf_op jit(solution)/shard_map/ppermute | solution.py:84
  30.9 0.6 %collective-permute-start.12 = (f32[32,256]{1,0:T(8,128)S(1)}, f32[32,256]{1,0:T(8,128)S(1)}, u32[]{:S(2)}, u32[]{:S(2)}) collective-permute-start(f32[32,256]{1,0:T(8,128)S(1)} %fusion), channel_id=1, source_target_pairs={{0,5},{1,4},{2,7},{3,6},{4,1},{5,0},{6,3},{7,2},{8,13},{9,12},{10,... | collective-permute-start | bytes 98312 | tf_op jit(solution)/shard_map/ppermute | solution.py:84
  31.5 0.3 collective-permute-start.11
  31.7 0.9 %collective-permute-done.14 = f32[32,256]{1,0:T(8,128)S(1)} collective-permute-done((f32[32,256]{1,0:T(8,128)S(1)}, f32[32,256]{1,0:T(8,128)S(1)}, u32[]{:S(2)}, u32[]{:S(2)}) %collective-permute-start.14) | collective-permute-done | bytes 32800 | tf_op jit(solution)/shard_map/ppermute | solution.py:84
  32.6 2.5 %collective-permute-done.13 = f32[32,256]{1,0:T(8,128)S(1)} collective-permute-done((f32[32,256]{1,0:T(8,128)S(1)}, f32[32,256]{1,0:T(8,128)S(1)}, u32[]{:S(2)}, u32[]{:S(2)}) %collective-permute-start.13) | collective-permute-done | bytes 32800 | tf_op jit(solution)/shard_map/ppermute | solution.py:84
  35.1 0.6 %add_add_fusion = f32[32,256]{1,0:T(8,128)} fusion(f32[32,256]{1,0:T(8,128)S(1)} %collective-permute-done.13, f32[32,256]{1,0:T(8,128)S(1)} %collective-permute-done.14, f32[32,256]{1,0:T(8,128)S(1)} %collective-permute-done.11, f32[32,256]{1,0:T(8,128)S(1)} %collective-permute-done.12), kind=kLoop, calls=%fused_computation.2 | loop fusion | flops 24576 | bytes 163840 | tf_op jit(solution)/shard_map/add | solution.py:98
  (21 shorter events, 0.1 us)
Async XLA Ops:
  2.4 6.8 %collective-permute-start.3 = (bf16[32,1280]{1,0:T(8,128)(2,1)}, bf16[32,1280]{1,0:T(8,128)(2,1)S(1)}, u32[]{:S(2)}, u32[]{:S(2)}) collective-permute-start(bf16[32,1280]{1,0:T(8,128)(2,1)} %piece.1.refs_4_), channel_id=1, source_target_pairs={{0,24},{1,25},{2,26},{3,27},{4,28},{5,29},{6,30},{7,31},{8,16},{9,... | collective-permute-start | bytes 245768 | tf_op jit(solution)/shard_map/ppermute | solution.py:84
  6.3 4.7 %collective-permute-start.2 = (bf16[32,1280]{1,0:T(8,128)(2,1)}, bf16[32,1280]{1,0:T(8,128)(2,1)S(1)}, u32[]{:S(2)}, u32[]{:S(2)}) collective-permute-start(bf16[32,1280]{1,0:T(8,128)(2,1)} %piece.1.refs_4_), channel_id=1, source_target_pairs={{0,16},{1,17},{2,18},{3,19},{4,20},{5,21},{6,22},{7,23},{8,24},{9,... | collective-permute-start | bytes 245768 | tf_op jit(solution)/shard_map/ppermute | solution.py:84
  6.8 4.7 %collective-permute-start.1 = (bf16[32,1280]{1,0:T(8,128)(2,1)}, bf16[32,1280]{1,0:T(8,128)(2,1)S(1)}, u32[]{:S(2)}, u32[]{:S(2)}) collective-permute-start(bf16[32,1280]{1,0:T(8,128)(2,1)} %piece.1.refs_4_), channel_id=1, source_target_pairs={{0,8},{1,9},{2,10},{3,11},{4,12},{5,13},{6,14},{7,15},{8,0},{9,1},... | collective-permute-start | bytes 245768 | tf_op jit(solution)/shard_map/ppermute | solution.py:84
  6.8 10.4 %collective-permute-start = (bf16[32,1280]{1,0:T(8,128)(2,1)}, bf16[32,1280]{1,0:T(8,128)(2,1)S(1)}, u32[]{:S(2)}, u32[]{:S(2)}) collective-permute-start(bf16[32,1280]{1,0:T(8,128)(2,1)} %piece.1.refs_4_), channel_id=1, source_target_pairs={{0,4},{1,5},{2,6},{3,7},{4,0},{5,1},{6,2},{7,3},{8,12},{9,13},{10,... | collective-permute-start | bytes 245768 | tf_op jit(solution)/shard_map/ppermute | solution.py:84
  9.2 8.0 %collective-permute-start.6 = (bf16[32,1280]{1,0:T(8,128)(2,1)S(1)}, bf16[32,1280]{1,0:T(8,128)(2,1)S(1)}, u32[]{:S(2)}, u32[]{:S(2)}) collective-permute-start(bf16[32,1280]{1,0:T(8,128)(2,1)S(1)} %collective-permute-done.3.refs_3_), channel_id=1, source_target_pairs={{0,4},{1,5},{2,6},{3,7},{4,0},{5,1},{6,2},{7,3},{8,12},{9,13},{10,... | collective-permute-start | bytes 245768 | tf_op jit(solution)/shard_map/ppermute | solution.py:84
  10.9 6.3 %collective-permute-start.5 = (bf16[32,1280]{1,0:T(8,128)(2,1)S(1)}, bf16[32,1280]{1,0:T(8,128)(2,1)S(1)}, u32[]{:S(2)}, u32[]{:S(2)}) collective-permute-start(bf16[32,1280]{1,0:T(8,128)(2,1)S(1)} %collective-permute-done.2.refs_2_), channel_id=1, source_target_pairs={{0,4},{1,5},{2,6},{3,7},{4,0},{5,1},{6,2},{7,3},{8,12},{9,13},{10,... | collective-permute-start | bytes 245768 | tf_op jit(solution)/shard_map/ppermute | solution.py:84
  11.4 5.8 %collective-permute-start.4 = (bf16[32,1280]{1,0:T(8,128)(2,1)S(1)}, bf16[32,1280]{1,0:T(8,128)(2,1)S(1)}, u32[]{:S(2)}, u32[]{:S(2)}) collective-permute-start(bf16[32,1280]{1,0:T(8,128)(2,1)S(1)} %collective-permute-done.1.refs_1_), channel_id=1, source_target_pairs={{0,4},{1,5},{2,6},{3,7},{4,0},{5,1},{6,2},{7,3},{8,12},{9,13},{10,... | collective-permute-start | bytes 245768 | tf_op jit(solution)/shard_map/ppermute | solution.py:84
  11.4 1.7 %copy-start.2 = (bf16[1280,1024]{1,0:T(8,128)(2,1)S(1)}, bf16[1280,1024]{1,0:T(8,128)(2,1)}, u32[]{:S(2)}) copy-start(bf16[1280,1024]{1,0:T(8,128)(2,1)} %pool_ref.2) | copy-start | bytes 7864324
  13.2 0.7 %copy-start.3 = (s32[1024]{0:T(1024)S(1)}, s32[1024]{0:T(1024)}, u32[]{:S(2)}) copy-start(s32[1024]{0:T(1024)} %param.7) | copy-start | bytes 12292
  13.8 3.4 %copy-start = (bf16[1024,256]{1,0:T(8,128)(2,1)S(1)}, bf16[1024,256]{1,0:T(8,128)(2,1)}, u32[]{:S(2)}) copy-start(bf16[1024,256]{1,0:T(8,128)(2,1)} %targets_ref.1) | copy-start | bytes 1572868
  13.9 3.4 %copy-start.1 = (bf16[32,1280]{1,0:T(8,128)(2,1)S(1)}, bf16[32,1280]{1,0:T(8,128)(2,1)}, u32[]{:S(2)}) copy-start(bf16[32,1280]{1,0:T(8,128)(2,1)} %piece.1.refs_4_) | copy-start | bytes 245764
  19.9 1.6 %collective-permute-start.7 = (f32[128,256]{1,0:T(8,128)S(1)}, f32[128,256]{1,0:T(8,128)S(1)}, u32[]{:S(2)}, u32[]{:S(2)}) collective-permute-start(f32[128,256]{1,0:T(8,128)S(1)} %get-tuple-element.11), channel_id=1, source_target_pairs={{0,4},{1,5},{2,6},{3,7},{4,0},{5,1},{6,2},{7,3},{8,12},{9,13},{10,... | collective-permute-start | bytes 393224 | tf_op jit(solution)/shard_map/ppermute | solution.py:84
  21.5 4.3 %collective-permute-start.10 = (f32[32,256]{1,0:T(8,128)S(1)}, f32[32,256]{1,0:T(8,128)S(1)}, u32[]{:S(2)}, u32[]{:S(2)}) collective-permute-start(f32[32,256]{1,0:T(8,128)S(1)} %get-tuple-element.12), channel_id=1, source_target_pairs={{0,28},{1,29},{2,30},{3,31},{4,24},{5,25},{6,26},{7,27},{8,20},{9,... | collective-permute-start | bytes 98312 | tf_op jit(solution)/shard_map/ppermute | solution.py:84
  23.1 3.9 %collective-permute-start.9 = (f32[32,256]{1,0:T(8,128)S(1)}, f32[32,256]{1,0:T(8,128)S(1)}, u32[]{:S(2)}, u32[]{:S(2)}) collective-permute-start(f32[32,256]{1,0:T(8,128)S(1)} %get-tuple-element.13), channel_id=1, source_target_pairs={{0,20},{1,21},{2,22},{3,23},{4,16},{5,17},{6,18},{7,19},{8,28},{9,... | collective-permute-start | bytes 98312 | tf_op jit(solution)/shard_map/ppermute | solution.py:84
  24.1 3.3 %collective-permute-start.8 = (f32[32,256]{1,0:T(8,128)S(1)}, f32[32,256]{1,0:T(8,128)S(1)}, u32[]{:S(2)}, u32[]{:S(2)}) collective-permute-start(f32[32,256]{1,0:T(8,128)S(1)} %get-tuple-element.14), channel_id=1, source_target_pairs={{0,12},{1,13},{2,14},{3,15},{4,8},{5,9},{6,10},{7,11},{8,4},{9,5},... | collective-permute-start | bytes 98312 | tf_op jit(solution)/shard_map/ppermute | solution.py:84
  27.4 5.2 %collective-permute-start.14 = (f32[32,256]{1,0:T(8,128)S(1)}, f32[32,256]{1,0:T(8,128)S(1)}, u32[]{:S(2)}, u32[]{:S(2)}) collective-permute-start(f32[32,256]{1,0:T(8,128)S(1)} %fusion), channel_id=1, source_target_pairs={{0,7},{1,6},{2,5},{3,4},{4,3},{5,2},{6,1},{7,0},{8,15},{9,14},{10,... | collective-permute-start | bytes 98312 | tf_op jit(solution)/shard_map/ppermute | solution.py:84
  30.9 4.2 %collective-permute-start.13 = (f32[32,256]{1,0:T(8,128)S(1)}, f32[32,256]{1,0:T(8,128)S(1)}, u32[]{:S(2)}, u32[]{:S(2)}) collective-permute-start(f32[32,256]{1,0:T(8,128)S(1)} %fusion), channel_id=1, source_target_pairs={{0,6},{1,7},{2,4},{3,5},{4,2},{5,3},{6,0},{7,1},{8,14},{9,15},{10,... | collective-permute-start | bytes 98312 | tf_op jit(solution)/shard_map/ppermute | solution.py:84
  30.9 4.2 %collective-permute-start.12 = (f32[32,256]{1,0:T(8,128)S(1)}, f32[32,256]{1,0:T(8,128)S(1)}, u32[]{:S(2)}, u32[]{:S(2)}) collective-permute-start(f32[32,256]{1,0:T(8,128)S(1)} %fusion), channel_id=1, source_target_pairs={{0,5},{1,4},{2,7},{3,6},{4,1},{5,0},{6,3},{7,2},{8,13},{9,12},{10,... | collective-permute-start | bytes 98312 | tf_op jit(solution)/shard_map/ppermute | solution.py:84
  31.5 3.7 %collective-permute-start.11 = (f32[32,256]{1,0:T(8,128)S(1)}, f32[32,256]{1,0:T(8,128)S(1)}, u32[]{:S(2)}, u32[]{:S(2)}) collective-permute-start(f32[32,256]{1,0:T(8,128)S(1)} %fusion), channel_id=1, source_target_pairs={{0,4},{1,5},{2,6},{3,7},{4,0},{5,1},{6,2},{7,3},{8,12},{9,13},{10,... | collective-permute-start | bytes 98312 | tf_op jit(solution)/shard_map/ppermute | solution.py:84

commit v2 on v1

v2 whole, which is shorter than its diff:
```python
import functools

import jax
import jax.numpy as jnp
from jax import lax
from jax.experimental import pallas as pl
from jax.experimental.pallas import tpu as pltpu
from jax.sharding import PartitionSpec as P

F32, BF16 = jnp.float32, jnp.bfloat16
STEPS = 2
VMEM = pl.BlockSpec(memory_space=pltpu.VMEM)
ANY = pl.BlockSpec(memory_space=pl.ANY)


def in_hbm(x):
    return pltpu.with_memory_space_constraint(x, pltpu.HBM)


def dot(a, b, contract):
    return lax.dot_general(a, b, (contract, ((), ())), preferred_element_type=F32)


def start_copies(source, target, sem, parts):
    step = source.shape[0] // parts
    copies = []
    for p in range(parts):
        at = slice(p * step, (p + 1) * step)
        copies.append(pltpu.make_async_copy(source.at[at, :], target.at[at, :], sem.at[p]))
        copies[-1].start()
    return copies


def piece_kernel(rows_hbm, centers_hbm, coefs_hbm, picks_hbm, pool_hbm, piece_ref, picks_ref, pool_ref, rows_ref, centers_ref, sem, pool_sem):
    candidates, width = centers_ref.shape
    copies = [
        pltpu.make_async_copy(rows_hbm, rows_ref, sem.at[0]),
        pltpu.make_async_copy(centers_hbm, centers_ref, sem.at[1]),
        pltpu.make_async_copy(coefs_hbm, piece_ref.at[:, width:], sem.at[2]),
        pltpu.make_async_copy(picks_hbm, picks_ref, sem.at[3]),
    ]
    for copy in copies:
        copy.start()
    first = pool_ref.shape[0]
    copies += start_copies(pool_hbm.at[:first, :], pool_ref, pool_sem, pool_sem.shape[0])
    copies[0].wait()
    picked = lax.broadcasted_iota(jnp.int32, (candidates, rows_ref.shape[1]), 0) == rows_ref[...]
    picked = picked.astype(F32).astype(BF16)
    copies[1].wait()
    piece_ref[:, :width] = dot(picked, centers_ref[...], ((0,), (0,))).astype(BF16)
    for copy in copies[2:]:
        copy.wait()


def points_kernel(rows_ref, first_ref, pool_hbm, targets_hbm, points_ref, norm_ref, targets_ref, rest_ref, picks, partial, squares, sem):
    first, width = first_ref.shape
    count = first + rest_ref.shape[0]
    parts = sem.shape[0] // 2
    copies = start_copies(pool_hbm.at[first:, :], rest_ref, sem, parts)
    later = start_copies(targets_hbm, targets_ref, sem.at[parts:], parts)
    lane = lax.broadcasted_iota(jnp.int32, (128, 128), 1).astype(jnp.int16)
    one, zero = jnp.ones((128, 128), BF16), jnp.zeros((128, 128), BF16)
    for j in range(rows_ref.shape[0]):
        row = jnp.broadcast_to(rows_ref[j : j + 1, :], (128, 128)).T.astype(jnp.int16)
        for g in range(count // 128):
            picks[j * 128 : (j + 1) * 128, g * 128 : (g + 1) * 128] = (
                jnp.where(row == lane + jnp.int16(g * 128), one, zero)
            )
    for n in range(width // 256):
        at = slice(n * 256, (n + 1) * 256)
        partial[:, at] = dot(picks[:, :first], first_ref[:, at], ((1,), (0,)))
    for copy in copies:
        copy.wait()
    for n in range(width // 256):
        at = slice(n * 256, (n + 1) * 256)
        block = partial[:, at] + dot(picks[:, first:], rest_ref[:, at], ((1,), (0,)))
        points_ref[:, at] = block.astype(BF16)
        square = block[:, :128] * block[:, :128] + block[:, 128:] * block[:, 128:]
        squares[...] = square if n == 0 else squares[...] + square
    norm_ref[...] = jnp.sum(squares[...], axis=1, keepdims=True)
    for copy in later:
        copy.wait()


def residual_kernel(far, each, points_ref, norm_ref, targets_ref, own_ref, other_ref, residual_hbm, kept_ref, sent_ref, centers, coefs, kernel, rounded, residual, sem):
    half = own_ref.shape[0]
    count, width = points_ref.shape
    for i, ref in enumerate((own_ref, other_ref)):
        centers[i * half : (i + 1) * half, :] = ref[:, :width]
        coefs[i * half : (i + 1) * half, :] = ref[:, width:]
    squares = jnp.zeros((2 * half, 128), F32)
    for g in range(width // 128):
        part = centers[:, g * 128 : (g + 1) * 128].astype(F32)
        squares = squares + part * part
    center_norm = jnp.sum(squares.T, axis=0, keepdims=True)
    rows = count // STEPS
    copies = []
    for m in range(STEPS):
        at = slice(m * rows, (m + 1) * rows)
        inner = dot(points_ref[at, :], centers[...], ((1,), (1,)))
        distance = norm_ref[at, :] + center_norm - 2.0 * inner
        kernel[at, :] = jnp.exp(distance * (-1.0 / width)).astype(BF16)
    for m in range(STEPS):
        at = slice(m * rows, (m + 1) * rows)
        left = dot(kernel[at, :], coefs[...], ((1,), (0,))) - targets_ref[at, :].astype(F32)
        residual[at, :] = left
        rounded[at, :] = left.astype(BF16)
        copies.append(pltpu.make_async_copy(residual.at[at, :], residual_hbm.at[at, :], sem.at[m]))
        copies[-1].start()
    grad = dot(kernel[...], rounded[...], ((0,), (0,)))
    step = half // far
    for f in range(far):
        at = f * step
        kept_ref[at : at + each, :] = grad[half + at : half + at + each]
        kept_ref[at + each : at + step, :] = grad[at + each : at + step]
        sent_ref[at : at + each, :] = grad[at : at + each]
        sent_ref[at + each : at + step, :] = grad[half + at + each : half + at + step]
    for copy in copies:
        copy.wait()


def swap(x, axes, sizes, flips):
    blk, rep = sizes
    pairs = [
        (b * rep + r, (b ^ flips[0]) * rep + (r ^ flips[1])) for b in range(blk) for r in range(rep)
    ]
    return lax.ppermute(x, axes, pairs)


def digits(size, low):
    groups = []
    while 1 << low < size:
        high = min(low + 2, size.bit_length() - 1)
        groups.append([d << low for d in range(1, 1 << (high - low))])
        low = high
    return groups


def pair_sum(parts):
    while len(parts) > 1:
        parts = [parts[i] + parts[i + 1] for i in range(0, len(parts), 2)]
    return parts[0]


def per_device(sizes, point_pool, batch_rows, targets, center_pool, center_rows, coefs):
    send = functools.partial(swap, axes=("blk", "rep"), sizes=sizes)
    each, outs = coefs.shape
    width = point_pool.shape[1]
    count = batch_rows.shape[0]

    rows = batch_rows.reshape(count // 128, 128)
    pool = in_hbm(point_pool)
    first = point_pool.shape[0] // 512 * 256
    piece, rows, resident = pl.pallas_call(
        piece_kernel,
        out_shape=(
            pltpu.VMEM((each, width + outs), BF16),
            pltpu.VMEM(rows.shape, rows.dtype),
            pltpu.VMEM((first, width), BF16),
        ),
        in_specs=[ANY] * 5,
        out_specs=(VMEM,) * 3,
        scratch_shapes=[
            pltpu.VMEM((1, each), jnp.int32),
            pltpu.VMEM(center_pool.shape, BF16),
            pltpu.SemaphoreType.DMA((4,)),
            pltpu.SemaphoreType.DMA((4,)),
        ],
        compiler_params=pltpu.CompilerParams(vmem_limit_bytes=8 << 20),
        name="piece",
    )(in_hbm(center_rows.reshape(1, each)), in_hbm(center_pool), in_hbm(coefs), in_hbm(rows), pool)

    chips, reps = digits(sizes[0], 1), digits(sizes[1], 0)
    block = piece
    parts = [block] + [send(block, flips=(d, 0)) for d in chips[0]]
    points, point_norm, goals = pl.pallas_call(
        points_kernel,
        out_shape=(
            pltpu.VMEM((count, width), BF16),
            pltpu.VMEM((count, 1), F32),
            pltpu.VMEM(targets.shape, BF16),
        ),
        in_specs=[VMEM, VMEM, ANY, ANY],
        out_specs=(VMEM,) * 3,
        scratch_shapes=[
            pltpu.VMEM((point_pool.shape[0] - first, width), BF16),
            pltpu.VMEM((count, point_pool.shape[0]), BF16),
            pltpu.VMEM((count, width), F32),
            pltpu.VMEM((count, 128), F32),
            pltpu.SemaphoreType.DMA((8,)),
        ],
        compiler_params=pltpu.CompilerParams(vmem_limit_bytes=32 << 20),
        cost_estimate=pl.CostEstimate(flops=2 << 30, bytes_accessed=5 << 20, transcendentals=0),
        name="points",
    )(rows, resident, pool, in_hbm(targets))
    parts, points, point_norm, goals = lax.optimization_barrier((parts, points, point_norm, goals))
    block = jnp.concatenate(parts, axis=0)
    near = len(parts)
    for group in chips[1:]:
        block = jnp.concatenate([block] + [send(block, flips=(d, 0)) for d in group], axis=0)
    half = block.shape[0]
    far = half // (near * each)
    residual, kept, sent = pl.pallas_call(
        functools.partial(residual_kernel, far, each),
        out_shape=(
            jax.ShapeDtypeStruct((count, outs), F32),
            pltpu.VMEM((half, outs), F32),
            pltpu.VMEM((half, outs), F32),
        ),
        in_specs=[VMEM] * 5,
        out_specs=(ANY, VMEM, VMEM),
        scratch_shapes=[
            pltpu.VMEM((2 * half, width), BF16),
            pltpu.VMEM((2 * half, outs), BF16),
            pltpu.VMEM((count, 2 * half), BF16),
            pltpu.VMEM((count, outs), BF16),
            pltpu.VMEM((count, outs), F32),
            pltpu.SemaphoreType.DMA((STEPS,)),
        ],
        compiler_params=pltpu.CompilerParams(vmem_limit_bytes=32 << 20),
        name="residual",
    )(points, point_norm, goals, block, send(block, flips=(1, 0)))

    total = (kept + send(sent, flips=(1, 0))).reshape(far, near, each, outs)
    for group in reversed(chips[1:]):
        low = total.shape[0] // (len(group) + 1)
        blocks = [total[i * low : (i + 1) * low] for i in range(len(group) + 1)]
        total = pair_sum(blocks[:1] + [send(x, flips=(d, 0)) for x, d in zip(blocks[1:], group)])
    mine = pair_sum([total[0, 0]] + [send(total[0, i + 1], flips=(d ^ 1, 0)) for i, d in enumerate(chips[0])])
    flip = 1
    for group in reps:
        first = send(mine, flips=(1, 0)) if flip else mine
        mine, flip = pair_sum([first] + [send(mine, flips=(flip, d)) for d in group]), 0
    return residual, mine


def solution(mesh):
    return jax.shard_map(
        functools.partial(per_device, (mesh.shape["blk"], mesh.shape["rep"])),
        mesh=mesh,
        in_specs=(
            P(("blk", "rep"), None),
            P(("blk", "rep")),
            P(("blk", "rep"), None),
            P("blk", None),
            P("blk"),
            P("blk", None),
        ),
        out_specs=(P(("blk", "rep"), None), P("blk", None)),
        check_vma=False,
    )
```

time: 36 us -> 30.1 us (0.84)
  local copies, waits for them, and re-layouts: 2.44 us -> 0.04 us
  waiting for transfers between devices: 11.6 us -> 9.7 us
  Pallas kernels: 7.75 us -> 6.66 us
  starting transfers between devices: 12.6 us -> 12.2 us
    unnamed x8 -> x3, local copies, waits for them, and re-layouts: 2.43 us -> 0.02 us
    ppermute x15 -> x12, waiting for transfers between devices: 11.6 us -> 9.7 us  [swap(): return lax.ppermute(x, axes, pairs)]
    pallas_call x3, Pallas kernels: 7.75 us -> 6.66 us  [the longest x1 3.42 us: per_device(): pl.pallas_call(points_kernel, out_shape=(pltpu.VMEM((count, width), BF16)...]
    ppermute x15 -> x12, starting transfers between devices: 12.6 us -> 12.2 us  [swap(): return lax.ppermute(x, axes, pairs)]
  transfers between devices with their start and end apart: 15 -> 12, of which waited for: 9 -> 9; matrix products, arithmetic and copies ran while one was open for 0% -> 0% of each run, Pallas kernels for 9% -> 11%
where the time goes in v2:
time: 30.1 us; the launch traced here: 30 us
  starting transfers between devices  12.2 us (41%)
  waiting for transfers between devices  9.7 us (32%)
  Pallas kernels  6.66 us (22%)
  between operations  0.72 us (2%)
  other arithmetic  0.65 us (2%)
    ppermute x12, starting transfers between devices, swap(): return lax.ppermute(x, axes, pairs)  12.2 us
    ppermute x12, waiting for transfers between devices, swap(): return lax.ppermute(x, axes, pairs)  9.7 us
    pallas_call x1, Pallas kernels, per_device(): pl.pallas_call(points_kernel, out_shape=(pltpu.VMEM((count, width), BF16)...  3.42 us
    pallas_call x1, Pallas kernels, per_device(): pl.pallas_call(functools.partial(residual_kernel, far, each), out_shape=(...  1.88 us
    pallas_call x1, Pallas kernels, per_device(): pl.pallas_call(piece_kernel, out_shape=(pltpu.VMEM((each, width + outs),...  1.37 us
    add x2, other arithmetic, pair_sum(): parts = [parts[i] + parts[i + 1] for i in range(0, len(parts), 2)]  0.64 us
  transfers between devices with their start and end apart: 12, of which 9 were waited for; matrix products, arithmetic and copies ran while one was open for 0% of the time, Pallas kernels for 11%

profile of v2, /device:TPU:0, one launch (start us, length us, event | category | flops | bytes accessed | tf_op | source)
XLA Modules:
  0.0 30.0 jit_solution(11631944764609677912)
XLA Ops:
  0.6 1.4 %piece.1 = (bf16[32,1280]{1,0:T(8,128)(2,1)S(1)}, s32[8,128]{1,0:T(8,128)S(1)}, bf16[512,1024]{1,0:T(8,128)(2,1)S(1)}) custom-call(s32[1,32]{1,0:T(1,128)} %bitcast.18, bf16[64,1024]{1,0:T(8,128)(2,1)} %centers_hbm.1, bf16[32,256]{1,0:T(8,128)(2,1)} %coefs_hbm.1, s32[8,128]{1,0:T(8,128)} %bitcast.17, bf16[1280,1024]{1,0:T(8,128)(2,1)} %pool_hbm.3), custom_call_target="tpu_custom_call" | custom-call | tf_op jit(solution)/shard_map/piece/pallas_call | solution.py:154
  2.0 4.0 %collective-permute-start.2 = (bf16[32,1280]{1,0:T(8,128)(2,1)S(1)}, bf16[32,1280]{1,0:T(8,128)(2,1)S(1)}, u32[]{:S(2)}, u32[]{:S(2)}) collective-permute-start(bf16[32,1280]{1,0:T(8,128)(2,1)S(1)} %get-tuple-element.27), channel_id=1, source_target_pairs={{0,24},{1,25},{2,26},{3,27},{4,28},{5,29},{6,30},{7,31},{8,16},{9,... | collective-permute-start | bytes 245768 | tf_op jit(solution)/shard_map/ppermute | solution.py:127
  6.0 0.5 %collective-permute-start.1 = (bf16[32,1280]{1,0:T(8,128)(2,1)S(1)}, bf16[32,1280]{1,0:T(8,128)(2,1)S(1)}, u32[]{:S(2)}, u32[]{:S(2)}) collective-permute-start(bf16[32,1280]{1,0:T(8,128)(2,1)S(1)} %get-tuple-element.27), channel_id=1, source_target_pairs={{0,16},{1,17},{2,18},{3,19},{4,20},{5,21},{6,22},{7,23},{8,24},{9,... | collective-permute-start | bytes 245768 | tf_op jit(solution)/shard_map/ppermute | solution.py:127
  6.5 0.1 collective-permute-start
  6.6 3.4 %points.1 = (bf16[1024,1024]{1,0:T(8,128)(2,1)S(1)}, f32[1024,1]{1,0:T(8,128)S(1)}, bf16[1024,256]{1,0:T(8,128)(2,1)S(1)}) custom-call(s32[8,128]{1,0:T(8,128)S(1)} %get-tuple-element.19.rows_ref, bf16[512,1024]{1,0:T(8,128)(2,1)S(1)} %get-tuple-element.20.first_ref, bf16[1280,1024]{1,0:T(8,128)(2,1)} %pool_hbm.3, bf16[1024,256]{1,0:T(8,128)(2,1)} %targets_hbm.1), custom_call_target="tpu_custom_call" | custom-call | flops 2147483648 | bytes 5242880 | tf_op jit(solution)/shard_map/points/pallas_call | solution.py:176
  10.0 0.4 %collective-permute-done.1 = bf16[32,1280]{1,0:T(8,128)(2,1)S(1)} collective-permute-done((bf16[32,1280]{1,0:T(8,128)(2,1)S(1)}, bf16[32,1280]{1,0:T(8,128)(2,1)S(1)}, u32[]{:S(2)}, u32[]{:S(2)}) %collective-permute-start.1) | collective-permute-done | bytes 81952 | tf_op jit(solution)/shard_map/ppermute | solution.py:127
  10.4 0.5 %collective-permute-done = bf16[32,1280]{1,0:T(8,128)(2,1)S(1)} collective-permute-done((bf16[32,1280]{1,0:T(8,128)(2,1)S(1)}, bf16[32,1280]{1,0:T(8,128)(2,1)S(1)}, u32[]{:S(2)}, u32[]{:S(2)}) %collective-permute-start) | collective-permute-done | bytes 81952 | tf_op jit(solution)/shard_map/ppermute | solution.py:127
  11.0 0.1 collective-permute-start.3
  11.0 1.6 %collective-permute-done.3.other_ref = bf16[128,1280]{1,0:T(8,128)(2,1)S(1)} collective-permute-done((bf16[128,1280]{1,0:T(8,128)(2,1)S(1)}, bf16[128,1280]{1,0:T(8,128)(2,1)S(1)}, u32[]{:S(2)}, u32[]{:S(2)}) %collective-permute-start.3) | collective-permute-done | bytes 327712 | tf_op jit(solution)/shard_map/ppermute | solution.py:127
  12.7 1.9 %residual.1 = (f32[1024,256]{1,0:T(8,128)}, f32[128,256]{1,0:T(8,128)S(1)}, f32[128,256]{1,0:T(8,128)S(1)}) custom-call(bf16[1024,1024]{1,0:T(8,128)(2,1)S(1)} %get-tuple-element.24.points_ref, f32[1024,1]{1,0:T(8,128)S(1)} %get-tuple-element.25.norm_ref, bf16[1024,256]{1,0:T(8,128)(2,1)S(1)} %get-tuple-element.26.targets_ref, ...), custom_call_target="tpu_custom_call" | custom-call | tf_op jit(solution)/shard_map/residual/pallas_call | solution.py:203
  14.5 0.2 collective-permute-start.4
  14.7 1.2 %collective-permute-done.4 = f32[128,256]{1,0:T(8,128)S(1)} collective-permute-done((f32[128,256]{1,0:T(8,128)S(1)}, f32[128,256]{1,0:T(8,128)S(1)}, u32[]{:S(2)}, u32[]{:S(2)}) %collective-permute-start.4) | collective-permute-done | bytes 131104 | tf_op jit(solution)/shard_map/ppermute | solution.py:127
  16.0 1.8 %collective-permute-start.7 = (f32[32,256]{1,0:T(8,128)S(1)}, f32[32,256]{1,0:T(8,128)S(1)}, u32[]{:S(2)}, u32[]{:S(2)}) collective-permute-start(f32[32,256]{1,0:T(8,128)S(1)} %get-tuple-element.34), channel_id=1, source_target_pairs={{0,28},{1,29},{2,30},{3,31},{4,24},{5,25},{6,26},{7,27},{8,20},{9,... | collective-permute-start | bytes 98312 | tf_op jit(solution)/shard_map/ppermute | solution.py:127
  17.8 0.5 %collective-permute-start.6 = (f32[32,256]{1,0:T(8,128)S(1)}, f32[32,256]{1,0:T(8,128)S(1)}, u32[]{:S(2)}, u32[]{:S(2)}) collective-permute-start(f32[32,256]{1,0:T(8,128)S(1)} %get-tuple-element.35), channel_id=1, source_target_pairs={{0,20},{1,21},{2,22},{3,23},{4,16},{5,17},{6,18},{7,19},{8,28},{9,... | collective-permute-start | bytes 98312 | tf_op jit(solution)/shard_map/ppermute | solution.py:127
  18.3 0.7 %collective-permute-start.5 = (f32[32,256]{1,0:T(8,128)S(1)}, f32[32,256]{1,0:T(8,128)S(1)}, u32[]{:S(2)}, u32[]{:S(2)}) collective-permute-start(f32[32,256]{1,0:T(8,128)S(1)} %get-tuple-element.36), channel_id=1, source_target_pairs={{0,12},{1,13},{2,14},{3,15},{4,8},{5,9},{6,10},{7,11},{8,4},{9,5},... | collective-permute-start | bytes 98312 | tf_op jit(solution)/shard_map/ppermute | solution.py:127
  19.0 1.3 %collective-permute-done.7 = f32[32,256]{1,0:T(8,128)S(1)} collective-permute-done((f32[32,256]{1,0:T(8,128)S(1)}, f32[32,256]{1,0:T(8,128)S(1)}, u32[]{:S(2)}, u32[]{:S(2)}) %collective-permute-start.7) | collective-permute-done | bytes 32800 | tf_op jit(solution)/shard_map/ppermute | solution.py:127
  20.3 0.9 %collective-permute-done.6 = f32[32,256]{1,0:T(8,128)S(1)} collective-permute-done((f32[32,256]{1,0:T(8,128)S(1)}, f32[32,256]{1,0:T(8,128)S(1)}, u32[]{:S(2)}, u32[]{:S(2)}) %collective-permute-start.6) | collective-permute-done | bytes 32800 | tf_op jit(solution)/shard_map/ppermute | solution.py:127
  21.2 0.5 %collective-permute-done.5 = f32[32,256]{1,0:T(8,128)S(1)} collective-permute-done((f32[32,256]{1,0:T(8,128)S(1)}, f32[32,256]{1,0:T(8,128)S(1)}, u32[]{:S(2)}, u32[]{:S(2)}) %collective-permute-start.5) | collective-permute-done | bytes 32800 | tf_op jit(solution)/shard_map/ppermute | solution.py:127
  21.7 3.4 %collective-permute-start.11 = (f32[32,256]{1,0:T(8,128)S(1)}, f32[32,256]{1,0:T(8,128)S(1)}, u32[]{:S(2)}, u32[]{:S(2)}) collective-permute-start(f32[32,256]{1,0:T(8,128)S(1)} %fusion.1), channel_id=1, source_target_pairs={{0,7},{1,6},{2,5},{3,4},{4,3},{5,2},{6,1},{7,0},{8,15},{9,14},{10,... | collective-permute-start | bytes 98312 | tf_op jit(solution)/shard_map/ppermute | solution.py:127
  25.1 0.6 %collective-permute-start.9 = (f32[32,256]{1,0:T(8,128)S(1)}, f32[32,256]{1,0:T(8,128)S(1)}, u32[]{:S(2)}, u32[]{:S(2)}) collective-permute-start(f32[32,256]{1,0:T(8,128)S(1)} %fusion.1), channel_id=1, source_target_pairs={{0,5},{1,4},{2,7},{3,6},{4,1},{5,0},{6,3},{7,2},{8,13},{9,12},{10,... | collective-permute-start | bytes 98312 | tf_op jit(solution)/shard_map/ppermute | solution.py:127
  25.7 0.3 collective-permute-start.8
  25.9 0.9 %collective-permute-done.11 = f32[32,256]{1,0:T(8,128)S(1)} collective-permute-done((f32[32,256]{1,0:T(8,128)S(1)}, f32[32,256]{1,0:T(8,128)S(1)}, u32[]{:S(2)}, u32[]{:S(2)}) %collective-permute-start.11) | collective-permute-done | bytes 32800 | tf_op jit(solution)/shard_map/ppermute | solution.py:127
  26.9 2.5 %collective-permute-done.10 = f32[32,256]{1,0:T(8,128)S(1)} collective-permute-done((f32[32,256]{1,0:T(8,128)S(1)}, f32[32,256]{1,0:T(8,128)S(1)}, u32[]{:S(2)}, u32[]{:S(2)}) %collective-permute-start.10) | collective-permute-done | bytes 32800 | tf_op jit(solution)/shard_map/ppermute | solution.py:127
  29.3 0.6 %add_add_fusion = f32[32,256]{1,0:T(8,128)} fusion(f32[32,256]{1,0:T(8,128)S(1)} %collective-permute-done.10, f32[32,256]{1,0:T(8,128)S(1)} %collective-permute-done.11, f32[32,256]{1,0:T(8,128)S(1)} %collective-permute-done.8, f32[32,256]{1,0:T(8,128)S(1)} %collective-permute-done.9), kind=kLoop, calls=%fused_computation.6 | loop fusion | flops 24576 | bytes 163840 | tf_op jit(solution)/shard_map/add | solution.py:141
  (11 shorter events, 0.1 us)
Async XLA Ops:
  2.0 8.0 %collective-permute-start.2 = (bf16[32,1280]{1,0:T(8,128)(2,1)S(1)}, bf16[32,1280]{1,0:T(8,128)(2,1)S(1)}, u32[]{:S(2)}, u32[]{:S(2)}) collective-permute-start(bf16[32,1280]{1,0:T(8,128)(2,1)S(1)} %get-tuple-element.27), channel_id=1, source_target_pairs={{0,24},{1,25},{2,26},{3,27},{4,28},{5,29},{6,30},{7,31},{8,16},{9,... | collective-permute-start | bytes 245768 | tf_op jit(solution)/shard_map/ppermute | solution.py:127
  6.0 4.4 %collective-permute-start.1 = (bf16[32,1280]{1,0:T(8,128)(2,1)S(1)}, bf16[32,1280]{1,0:T(8,128)(2,1)S(1)}, u32[]{:S(2)}, u32[]{:S(2)}) collective-permute-start(bf16[32,1280]{1,0:T(8,128)(2,1)S(1)} %get-tuple-element.27), channel_id=1, source_target_pairs={{0,16},{1,17},{2,18},{3,19},{4,20},{5,21},{6,22},{7,23},{8,24},{9,... | collective-permute-start | bytes 245768 | tf_op jit(solution)/shard_map/ppermute | solution.py:127
  6.5 4.4 %collective-permute-start = (bf16[32,1280]{1,0:T(8,128)(2,1)S(1)}, bf16[32,1280]{1,0:T(8,128)(2,1)S(1)}, u32[]{:S(2)}, u32[]{:S(2)}) collective-permute-start(bf16[32,1280]{1,0:T(8,128)(2,1)S(1)} %get-tuple-element.27), channel_id=1, source_target_pairs={{0,8},{1,9},{2,10},{3,11},{4,12},{5,13},{6,14},{7,15},{8,0},{9,1},... | collective-permute-start | bytes 245768 | tf_op jit(solution)/shard_map/ppermute | solution.py:127
  11.0 1.7 %collective-permute-start.3 = (bf16[128,1280]{1,0:T(8,128)(2,1)S(1)}, bf16[128,1280]{1,0:T(8,128)(2,1)S(1)}, u32[]{:S(2)}, u32[]{:S(2)}) collective-permute-start(bf16[128,1280]{1,0:T(8,128)(2,1)S(1)} %constant_dynamic-update-slice_fusion.own_ref), channel_id=1, source_target_pairs={{0,4},{1,5},{2,6},{3,7},{4,0},{5,1},{6,2},{7,3},{8,12},{9,13},{10,... | collective-permute-start | bytes 983048 | tf_op jit(solution)/shard_map/ppermute | solution.py:127
  14.5 1.4 %collective-permute-start.4 = (f32[128,256]{1,0:T(8,128)S(1)}, f32[128,256]{1,0:T(8,128)S(1)}, u32[]{:S(2)}, u32[]{:S(2)}) collective-permute-start(f32[128,256]{1,0:T(8,128)S(1)} %get-tuple-element.33), channel_id=1, source_target_pairs={{0,4},{1,5},{2,6},{3,7},{4,0},{5,1},{6,2},{7,3},{8,12},{9,13},{10,... | collective-permute-start | bytes 393224 | tf_op jit(solution)/shard_map/ppermute | solution.py:127
  16.0 4.3 %collective-permute-start.7 = (f32[32,256]{1,0:T(8,128)S(1)}, f32[32,256]{1,0:T(8,128)S(1)}, u32[]{:S(2)}, u32[]{:S(2)}) collective-permute-start(f32[32,256]{1,0:T(8,128)S(1)} %get-tuple-element.34), channel_id=1, source_target_pairs={{0,28},{1,29},{2,30},{3,31},{4,24},{5,25},{6,26},{7,27},{8,20},{9,... | collective-permute-start | bytes 98312 | tf_op jit(solution)/shard_map/ppermute | solution.py:127
  17.8 3.4 %collective-permute-start.6 = (f32[32,256]{1,0:T(8,128)S(1)}, f32[32,256]{1,0:T(8,128)S(1)}, u32[]{:S(2)}, u32[]{:S(2)}) collective-permute-start(f32[32,256]{1,0:T(8,128)S(1)} %get-tuple-element.35), channel_id=1, source_target_pairs={{0,20},{1,21},{2,22},{3,23},{4,16},{5,17},{6,18},{7,19},{8,28},{9,... | collective-permute-start | bytes 98312 | tf_op jit(solution)/shard_map/ppermute | solution.py:127
  18.3 3.3 %collective-permute-start.5 = (f32[32,256]{1,0:T(8,128)S(1)}, f32[32,256]{1,0:T(8,128)S(1)}, u32[]{:S(2)}, u32[]{:S(2)}) collective-permute-start(f32[32,256]{1,0:T(8,128)S(1)} %get-tuple-element.36), channel_id=1, source_target_pairs={{0,12},{1,13},{2,14},{3,15},{4,8},{5,9},{6,10},{7,11},{8,4},{9,5},... | collective-permute-start | bytes 98312 | tf_op jit(solution)/shard_map/ppermute | solution.py:127
  21.7 5.2 %collective-permute-start.11 = (f32[32,256]{1,0:T(8,128)S(1)}, f32[32,256]{1,0:T(8,128)S(1)}, u32[]{:S(2)}, u32[]{:S(2)}) collective-permute-start(f32[32,256]{1,0:T(8,128)S(1)} %fusion.1), channel_id=1, source_target_pairs={{0,7},{1,6},{2,5},{3,4},{4,3},{5,2},{6,1},{7,0},{8,15},{9,14},{10,... | collective-permute-start | bytes 98312 | tf_op jit(solution)/shard_map/ppermute | solution.py:127
  25.1 4.2 %collective-permute-start.10 = (f32[32,256]{1,0:T(8,128)S(1)}, f32[32,256]{1,0:T(8,128)S(1)}, u32[]{:S(2)}, u32[]{:S(2)}) collective-permute-start(f32[32,256]{1,0:T(8,128)S(1)} %fusion.1), channel_id=1, source_target_pairs={{0,6},{1,7},{2,4},{3,5},{4,2},{5,3},{6,0},{7,1},{8,14},{9,15},{10,... | collective-permute-start | bytes 98312 | tf_op jit(solution)/shard_map/ppermute | solution.py:127
  25.1 4.2 %collective-permute-start.9 = (f32[32,256]{1,0:T(8,128)S(1)}, f32[32,256]{1,0:T(8,128)S(1)}, u32[]{:S(2)}, u32[]{:S(2)}) collective-permute-start(f32[32,256]{1,0:T(8,128)S(1)} %fusion.1), channel_id=1, source_target_pairs={{0,5},{1,4},{2,7},{3,6},{4,1},{5,0},{6,3},{7,2},{8,13},{9,12},{10,... | collective-permute-start | bytes 98312 | tf_op jit(solution)/shard_map/ppermute | solution.py:127
  25.7 3.7 %collective-permute-start.8 = (f32[32,256]{1,0:T(8,128)S(1)}, f32[32,256]{1,0:T(8,128)S(1)}, u32[]{:S(2)}, u32[]{:S(2)}) collective-permute-start(f32[32,256]{1,0:T(8,128)S(1)} %fusion.1), channel_id=1, source_target_pairs={{0,4},{1,5},{2,6},{3,7},{4,0},{5,1},{6,2},{7,3},{8,12},{9,13},{10,... | collective-permute-start | bytes 98312 | tf_op jit(solution)/shard_map/ppermute | solution.py:127

commit v3 on v2

--- a/solution.py
+++ b/solution.py
@@ -82,7 +82,7 @@
         copy.wait()
 
 
-def residual_kernel(far, each, points_ref, norm_ref, targets_ref, own_ref, other_ref, residual_hbm, kept_ref, sent_ref, centers, coefs, kernel, rounded, residual, sem):
+def residual_kernel(far, each, points_ref, norm_ref, targets_ref, own_ref, other_ref, residual_ref, kept_ref, sent_ref, centers, coefs, kernel, rounded):
     half = own_ref.shape[0]
     count, width = points_ref.shape
     for i, ref in enumerate((own_ref, other_ref)):
@@ -94,7 +94,6 @@
         squares = squares + part * part
     center_norm = jnp.sum(squares.T, axis=0, keepdims=True)
     rows = count // STEPS
-    copies = []
     for m in range(STEPS):
         at = slice(m * rows, (m + 1) * rows)
         inner = dot(points_ref[at, :], centers[...], ((1,), (1,)))
@@ -103,10 +102,8 @@
     for m in range(STEPS):
         at = slice(m * rows, (m + 1) * rows)
         left = dot(kernel[at, :], coefs[...], ((1,), (0,))) - targets_ref[at, :].astype(F32)
-        residual[at, :] = left
+        residual_ref[at, :] = left
         rounded[at, :] = left.astype(BF16)
-        copies.append(pltpu.make_async_copy(residual.at[at, :], residual_hbm.at[at, :], sem.at[m]))
-        copies[-1].start()
     grad = dot(kernel[...], rounded[...], ((0,), (0,)))
     step = half // far
     for f in range(far):
@@ -115,7 +112,10 @@
         kept_ref[at + each : at + step, :] = grad[at + each : at + step]
         sent_ref[at : at + each, :] = grad[at : at + each]
         sent_ref[at + each : at + step, :] = grad[half + at + each : half + at + step]
-    for copy in copies:
+
+
+def write_kernel(source, target, sem):
+    for copy in start_copies(source, target, sem, sem.shape[0]):
         copy.wait()
 
 
@@ -172,7 +172,8 @@
 
     chips, reps = digits(sizes[0], 1), digits(sizes[1], 0)
     block = piece
-    parts = [block] + [send(block, flips=(d, 0)) for d in chips[0]]
+    near = [0] + chips[0]
+    parts = [block] + [send(block, flips=(d, 0)) for d in near[1:]]
     points, point_norm, goals = pl.pallas_call(
         points_kernel,
         out_shape=(
@@ -195,38 +196,48 @@
     )(rows, resident, pool, in_hbm(targets))
     parts, points, point_norm, goals = lax.optimization_barrier((parts, points, point_norm, goals))
     block = jnp.concatenate(parts, axis=0)
-    near = len(parts)
     for group in chips[1:]:
         block = jnp.concatenate([block] + [send(block, flips=(d, 0)) for d in group], axis=0)
     half = block.shape[0]
-    far = half // (near * each)
+    far = half // (len(near) * each)
     residual, kept, sent = pl.pallas_call(
         functools.partial(residual_kernel, far, each),
         out_shape=(
-            jax.ShapeDtypeStruct((count, outs), F32),
+            pltpu.VMEM((count, outs), F32),
             pltpu.VMEM((half, outs), F32),
             pltpu.VMEM((half, outs), F32),
         ),
         in_specs=[VMEM] * 5,
-        out_specs=(ANY, VMEM, VMEM),
+        out_specs=(VMEM,) * 3,
         scratch_shapes=[
             pltpu.VMEM((2 * half, width), BF16),
             pltpu.VMEM((2 * half, outs), BF16),
             pltpu.VMEM((count, 2 * half), BF16),
             pltpu.VMEM((count, outs), BF16),
-            pltpu.VMEM((count, outs), F32),
-            pltpu.SemaphoreType.DMA((STEPS,)),
         ],
         compiler_params=pltpu.CompilerParams(vmem_limit_bytes=32 << 20),
         name="residual",
     )(points, point_norm, goals, block, send(block, flips=(1, 0)))
 
-    total = (kept + send(sent, flips=(1, 0))).reshape(far, near, each, outs)
+    total = (kept + send(sent, flips=(1, 0))).reshape(far, len(near), each, outs)
     for group in reversed(chips[1:]):
         low = total.shape[0] // (len(group) + 1)
         blocks = [total[i * low : (i + 1) * low] for i in range(len(group) + 1)]
         total = pair_sum(blocks[:1] + [send(x, flips=(d, 0)) for x, d in zip(blocks[1:], group)])
-    mine = pair_sum([total[0, 0]] + [send(total[0, i + 1], flips=(d ^ 1, 0)) for i, d in enumerate(chips[0])])
+    rows = {d: total[0, i] for i, d in enumerate(near)}
+    parts = [rows[0]] + [send(rows[d], flips=(d ^ 1, 0)) for d in chips[0]]
+    residual = pl.pallas_call(
+        write_kernel,
+        out_shape=jax.ShapeDtypeStruct(residual.shape, F32),
+        in_specs=[VMEM],
+        out_specs=ANY,
+        scratch_shapes=[pltpu.SemaphoreType.DMA((4,))],
+        compiler_params=pltpu.CompilerParams(vmem_limit_bytes=8 << 20),
+        cost_estimate=pl.CostEstimate(flops=0, bytes_accessed=4 << 20, transcendentals=0),
+        name="write",
+    )(residual)
+    parts, residual = lax.optimization_barrier((parts, residual))
+    mine = pair_sum(parts)
     flip = 1
     for group in reps:
         first = send(mine, flips=(1, 0)) if flip else mine

time: 30.1 us -> 29.5 us (0.980)
  waiting for transfers between devices: 9.7 us -> 8.7 us
  Pallas kernels: 6.66 us -> 7.01 us
    ppermute x12, waiting for transfers between devices: 9.7 us -> 8.7 us  [swap(): return lax.ppermute(x, axes, pairs)]
    pallas_call x0 -> x1, Pallas kernels: none -> 0.99 us  [per_device(): pl.pallas_call(write_kernel, out_shape=jax.ShapeDtypeStruct(residual.shap...]
    pallas_call x1, Pallas kernels: 1.88 us -> 1.24 us  [per_device(): pl.pallas_call(functools.partial(residual_kernel, far, each), out_shape=(...]
  transfers between devices with their start and end apart: 12 -> 12, of which waited for: 9 -> 9; matrix products, arithmetic and copies ran while one was open for 0% -> 0% of each run, Pallas kernels for 11% -> 15%
where the time goes in v3:
time: 29.5 us; the launch traced here: 29.3 us
  starting transfers between devices  12.2 us (41%)
  waiting for transfers between devices  8.7 us (29%)
  Pallas kernels  7.01 us (24%)
  between operations  0.72 us (2%)
  other arithmetic  0.65 us (2%)
    ppermute x12, starting transfers between devices, swap(): return lax.ppermute(x, axes, pairs)  12.2 us
    ppermute x12, waiting for transfers between devices, swap(): return lax.ppermute(x, axes, pairs)  8.7 us
    pallas_call x1, Pallas kernels, per_device(): pl.pallas_call(points_kernel, out_shape=(pltpu.VMEM((count, width), BF16)...  3.42 us
    pallas_call x1, Pallas kernels, per_device(): pl.pallas_call(piece_kernel, out_shape=(pltpu.VMEM((each, width + outs),...  1.37 us
    pallas_call x1, Pallas kernels, per_device(): pl.pallas_call(functools.partial(residual_kernel, far, each), out_shape=(...  1.24 us
    pallas_call x1, Pallas kernels, per_device(): pl.pallas_call(write_kernel, out_shape=jax.ShapeDtypeStruct(residual.shap...  0.99 us
    add x2, other arithmetic, pair_sum(): parts = [parts[i] + parts[i + 1] for i in range(0, len(parts), 2)]  0.64 us
  transfers between devices with their start and end apart: 12, of which 9 were waited for; matrix products, arithmetic and copies ran while one was open for 0% of the time, Pallas kernels for 15%

profile of v3, /device:TPU:0, one launch (start us, length us, event | category | flops | bytes accessed | tf_op | source)
XLA Modules:
  0.0 29.3 jit_solution(12191191108506998766)
XLA Ops:
  0.6 1.4 %piece.1 = (bf16[32,1280]{1,0:T(8,128)(2,1)S(1)}, s32[8,128]{1,0:T(8,128)S(1)}, bf16[512,1024]{1,0:T(8,128)(2,1)S(1)}) custom-call(s32[1,32]{1,0:T(1,128)} %bitcast.13, bf16[64,1024]{1,0:T(8,128)(2,1)} %centers_hbm.1, bf16[32,256]{1,0:T(8,128)(2,1)} %coefs_hbm.1, s32[8,128]{1,0:T(8,128)} %bitcast.12, bf16[1280,1024]{1,0:T(8,128)(2,1)} %pool_hbm.3), custom_call_target="tpu_custom_call" | custom-call | tf_op jit(solution)/shard_map/piece/pallas_call | solution.py:154
  2.0 4.0 %collective-permute-start.2 = (bf16[32,1280]{1,0:T(8,128)(2,1)S(1)}, bf16[32,1280]{1,0:T(8,128)(2,1)S(1)}, u32[]{:S(2)}, u32[]{:S(2)}) collective-permute-start(bf16[32,1280]{1,0:T(8,128)(2,1)S(1)} %get-tuple-element.32), channel_id=1, source_target_pairs={{0,24},{1,25},{2,26},{3,27},{4,28},{5,29},{6,30},{7,31},{8,16},{9,... | collective-permute-start | bytes 245768 | tf_op jit(solution)/shard_map/ppermute | solution.py:127
  6.0 0.5 %collective-permute-start.1 = (bf16[32,1280]{1,0:T(8,128)(2,1)S(1)}, bf16[32,1280]{1,0:T(8,128)(2,1)S(1)}, u32[]{:S(2)}, u32[]{:S(2)}) collective-permute-start(bf16[32,1280]{1,0:T(8,128)(2,1)S(1)} %get-tuple-element.32), channel_id=1, source_target_pairs={{0,16},{1,17},{2,18},{3,19},{4,20},{5,21},{6,22},{7,23},{8,24},{9,... | collective-permute-start | bytes 245768 | tf_op jit(solution)/shard_map/ppermute | solution.py:127
  6.5 0.1 collective-permute-start
  6.6 3.4 %points.1 = (bf16[1024,1024]{1,0:T(8,128)(2,1)S(1)}, f32[1024,1]{1,0:T(8,128)S(1)}, bf16[1024,256]{1,0:T(8,128)(2,1)S(1)}) custom-call(s32[8,128]{1,0:T(8,128)S(1)} %get-tuple-element.24.rows_ref, bf16[512,1024]{1,0:T(8,128)(2,1)S(1)} %get-tuple-element.25.first_ref, bf16[1280,1024]{1,0:T(8,128)(2,1)} %pool_hbm.3, bf16[1024,256]{1,0:T(8,128)(2,1)} %targets_hbm.1), custom_call_target="tpu_custom_call" | custom-call | flops 2147483648 | bytes 5242880 | tf_op jit(solution)/shard_map/points/pallas_call | solution.py:177
  10.0 0.4 %collective-permute-done.1 = bf16[32,1280]{1,0:T(8,128)(2,1)S(1)} collective-permute-done((bf16[32,1280]{1,0:T(8,128)(2,1)S(1)}, bf16[32,1280]{1,0:T(8,128)(2,1)S(1)}, u32[]{:S(2)}, u32[]{:S(2)}) %collective-permute-start.1) | collective-permute-done | bytes 81952 | tf_op jit(solution)/shard_map/ppermute | solution.py:127
  10.4 0.5 %collective-permute-done = bf16[32,1280]{1,0:T(8,128)(2,1)S(1)} collective-permute-done((bf16[32,1280]{1,0:T(8,128)(2,1)S(1)}, bf16[32,1280]{1,0:T(8,128)(2,1)S(1)}, u32[]{:S(2)}, u32[]{:S(2)}) %collective-permute-start) | collective-permute-done | bytes 81952 | tf_op jit(solution)/shard_map/ppermute | solution.py:127
  11.0 1.6 %collective-permute-done.3.other_ref = bf16[128,1280]{1,0:T(8,128)(2,1)S(1)} collective-permute-done((bf16[128,1280]{1,0:T(8,128)(2,1)S(1)}, bf16[128,1280]{1,0:T(8,128)(2,1)S(1)}, u32[]{:S(2)}, u32[]{:S(2)}) %collective-permute-start.3) | collective-permute-done | bytes 327712 | tf_op jit(solution)/shard_map/ppermute | solution.py:127
  12.7 1.2 %residual.1 = (f32[1024,256]{1,0:T(8,128)S(1)}, f32[128,256]{1,0:T(8,128)S(1)}, f32[128,256]{1,0:T(8,128)S(1)}) custom-call(bf16[1024,1024]{1,0:T(8,128)(2,1)S(1)} %get-tuple-element.29.points_ref, f32[1024,1]{1,0:T(8,128)S(1)} %get-tuple-element.30.norm_ref, bf16[1024,256]{1,0:T(8,128)(2,1)S(1)} %get-tuple-element.31.targets_ref, ...), custom_call_target="tpu_custom_call" | custom-call | tf_op jit(solution)/shard_map/residual/pallas_call | solution.py:203
  13.9 0.2 collective-permute-start.4
  14.1 1.2 %collective-permute-done.4 = f32[128,256]{1,0:T(8,128)S(1)} collective-permute-done((f32[128,256]{1,0:T(8,128)S(1)}, f32[128,256]{1,0:T(8,128)S(1)}, u32[]{:S(2)}, u32[]{:S(2)}) %collective-permute-start.4) | collective-permute-done | bytes 131104 | tf_op jit(solution)/shard_map/ppermute | solution.py:127
  15.4 1.8 %collective-permute-start.7 = (f32[32,256]{1,0:T(8,128)S(1)}, f32[32,256]{1,0:T(8,128)S(1)}, u32[]{:S(2)}, u32[]{:S(2)}) collective-permute-start(f32[32,256]{1,0:T(8,128)S(1)} %get-tuple-element.44), channel_id=1, source_target_pairs={{0,28},{1,29},{2,30},{3,31},{4,24},{5,25},{6,26},{7,27},{8,20},{9,... | collective-permute-start | bytes 98312 | tf_op jit(solution)/shard_map/ppermute | solution.py:127
  17.2 0.5 %collective-permute-start.6 = (f32[32,256]{1,0:T(8,128)S(1)}, f32[32,256]{1,0:T(8,128)S(1)}, u32[]{:S(2)}, u32[]{:S(2)}) collective-permute-start(f32[32,256]{1,0:T(8,128)S(1)} %get-tuple-element.45), channel_id=1, source_target_pairs={{0,20},{1,21},{2,22},{3,23},{4,16},{5,17},{6,18},{7,19},{8,28},{9,... | collective-permute-start | bytes 98312 | tf_op jit(solution)/shard_map/ppermute | solution.py:127
  17.7 0.7 %collective-permute-start.5 = (f32[32,256]{1,0:T(8,128)S(1)}, f32[32,256]{1,0:T(8,128)S(1)}, u32[]{:S(2)}, u32[]{:S(2)}) collective-permute-start(f32[32,256]{1,0:T(8,128)S(1)} %get-tuple-element.46), channel_id=1, source_target_pairs={{0,12},{1,13},{2,14},{3,15},{4,8},{5,9},{6,10},{7,11},{8,4},{9,5},... | collective-permute-start | bytes 98312 | tf_op jit(solution)/shard_map/ppermute | solution.py:127
  18.4 1.0 %write.1 = f32[1024,256]{1,0:T(8,128)} custom-call(f32[1024,256]{1,0:T(8,128)S(1)} %get-tuple-element.38.source), custom_call_target="tpu_custom_call" | custom-call | bytes 4194304 | tf_op jit(solution)/shard_map/write/pallas_call | solution.py:229
  19.4 0.3 collective-permute-done.7
  19.7 0.9 %collective-permute-done.6 = f32[32,256]{1,0:T(8,128)S(1)} collective-permute-done((f32[32,256]{1,0:T(8,128)S(1)}, f32[32,256]{1,0:T(8,128)S(1)}, u32[]{:S(2)}, u32[]{:S(2)}) %collective-permute-start.6) | collective-permute-done | bytes 32800 | tf_op jit(solution)/shard_map/ppermute | solution.py:127
  20.5 0.5 %collective-permute-done.5 = f32[32,256]{1,0:T(8,128)S(1)} collective-permute-done((f32[32,256]{1,0:T(8,128)S(1)}, f32[32,256]{1,0:T(8,128)S(1)}, u32[]{:S(2)}, u32[]{:S(2)}) %collective-permute-start.5) | collective-permute-done | bytes 32800 | tf_op jit(solution)/shard_map/ppermute | solution.py:127
  21.0 3.4 %collective-permute-start.11 = (f32[32,256]{1,0:T(8,128)S(1)}, f32[32,256]{1,0:T(8,128)S(1)}, u32[]{:S(2)}, u32[]{:S(2)}) collective-permute-start(f32[32,256]{1,0:T(8,128)S(1)} %add_add_fusion.1), channel_id=1, source_target_pairs={{0,7},{1,6},{2,5},{3,4},{4,3},{5,2},{6,1},{7,0},{8,15},{9,14},{10,... | collective-permute-start | bytes 98312 | tf_op jit(solution)/shard_map/ppermute | solution.py:127
  24.5 0.6 %collective-permute-start.9 = (f32[32,256]{1,0:T(8,128)S(1)}, f32[32,256]{1,0:T(8,128)S(1)}, u32[]{:S(2)}, u32[]{:S(2)}) collective-permute-start(f32[32,256]{1,0:T(8,128)S(1)} %add_add_fusion.1), channel_id=1, source_target_pairs={{0,5},{1,4},{2,7},{3,6},{4,1},{5,0},{6,3},{7,2},{8,13},{9,12},{10,... | collective-permute-start | bytes 98312 | tf_op jit(solution)/shard_map/ppermute | solution.py:127
  25.1 0.3 collective-permute-start.8
  25.3 0.9 %collective-permute-done.11 = f32[32,256]{1,0:T(8,128)S(1)} collective-permute-done((f32[32,256]{1,0:T(8,128)S(1)}, f32[32,256]{1,0:T(8,128)S(1)}, u32[]{:S(2)}, u32[]{:S(2)}) %collective-permute-start.11) | collective-permute-done | bytes 32800 | tf_op jit(solution)/shard_map/ppermute | solution.py:127
  26.2 2.5 %collective-permute-done.10 = f32[32,256]{1,0:T(8,128)S(1)} collective-permute-done((f32[32,256]{1,0:T(8,128)S(1)}, f32[32,256]{1,0:T(8,128)S(1)}, u32[]{:S(2)}, u32[]{:S(2)}) %collective-permute-start.10) | collective-permute-done | bytes 32800 | tf_op jit(solution)/shard_map/ppermute | solution.py:127
  28.7 0.6 %add_add_fusion = f32[32,256]{1,0:T(8,128)} fusion(f32[32,256]{1,0:T(8,128)S(1)} %collective-permute-done.10, f32[32,256]{1,0:T(8,128)S(1)} %collective-permute-done.11, f32[32,256]{1,0:T(8,128)S(1)} %collective-permute-done.8, f32[32,256]{1,0:T(8,128)S(1)} %collective-permute-done.9), kind=kLoop, calls=%fused_computation.4 | loop fusion | flops 24576 | bytes 163840 | tf_op jit(solution)/shard_map/add | solution.py:141
  (12 shorter events, 0.1 us)
Async XLA Ops:
  2.0 8.0 %collective-permute-start.2 = (bf16[32,1280]{1,0:T(8,128)(2,1)S(1)}, bf16[32,1280]{1,0:T(8,128)(2,1)S(1)}, u32[]{:S(2)}, u32[]{:S(2)}) collective-permute-start(bf16[32,1280]{1,0:T(8,128)(2,1)S(1)} %get-tuple-element.32), channel_id=1, source_target_pairs={{0,24},{1,25},{2,26},{3,27},{4,28},{5,29},{6,30},{7,31},{8,16},{9,... | collective-permute-start | bytes 245768 | tf_op jit(solution)/shard_map/ppermute | solution.py:127
  6.0 4.4 %collective-permute-start.1 = (bf16[32,1280]{1,0:T(8,128)(2,1)S(1)}, bf16[32,1280]{1,0:T(8,128)(2,1)S(1)}, u32[]{:S(2)}, u32[]{:S(2)}) collective-permute-start(bf16[32,1280]{1,0:T(8,128)(2,1)S(1)} %get-tuple-element.32), channel_id=1, source_target_pairs={{0,16},{1,17},{2,18},{3,19},{4,20},{5,21},{6,22},{7,23},{8,24},{9,... | collective-permute-start | bytes 245768 | tf_op jit(solution)/shard_map/ppermute | solution.py:127
  6.5 4.4 %collective-permute-start = (bf16[32,1280]{1,0:T(8,128)(2,1)S(1)}, bf16[32,1280]{1,0:T(8,128)(2,1)S(1)}, u32[]{:S(2)}, u32[]{:S(2)}) collective-permute-start(bf16[32,1280]{1,0:T(8,128)(2,1)S(1)} %get-tuple-element.32), channel_id=1, source_target_pairs={{0,8},{1,9},{2,10},{3,11},{4,12},{5,13},{6,14},{7,15},{8,0},{9,1},... | collective-permute-start | bytes 245768 | tf_op jit(solution)/shard_map/ppermute | solution.py:127
  11.0 1.7 %collective-permute-start.3 = (bf16[128,1280]{1,0:T(8,128)(2,1)S(1)}, bf16[128,1280]{1,0:T(8,128)(2,1)S(1)}, u32[]{:S(2)}, u32[]{:S(2)}) collective-permute-start(bf16[128,1280]{1,0:T(8,128)(2,1)S(1)} %constant_dynamic-update-slice_fusion.own_ref), channel_id=1, source_target_pairs={{0,4},{1,5},{2,6},{3,7},{4,0},{5,1},{6,2},{7,3},{8,12},{9,13},{10,... | collective-permute-start | bytes 983048 | tf_op jit(solution)/shard_map/ppermute | solution.py:127
  13.9 1.4 %collective-permute-start.4 = (f32[128,256]{1,0:T(8,128)S(1)}, f32[128,256]{1,0:T(8,128)S(1)}, u32[]{:S(2)}, u32[]{:S(2)}) collective-permute-start(f32[128,256]{1,0:T(8,128)S(1)} %get-tuple-element.37), channel_id=1, source_target_pairs={{0,4},{1,5},{2,6},{3,7},{4,0},{5,1},{6,2},{7,3},{8,12},{9,13},{10,... | collective-permute-start | bytes 393224 | tf_op jit(solution)/shard_map/ppermute | solution.py:127
  15.4 4.3 %collective-permute-start.7 = (f32[32,256]{1,0:T(8,128)S(1)}, f32[32,256]{1,0:T(8,128)S(1)}, u32[]{:S(2)}, u32[]{:S(2)}) collective-permute-start(f32[32,256]{1,0:T(8,128)S(1)} %get-tuple-element.44), channel_id=1, source_target_pairs={{0,28},{1,29},{2,30},{3,31},{4,24},{5,25},{6,26},{7,27},{8,20},{9,... | collective-permute-start | bytes 98312 | tf_op jit(solution)/shard_map/ppermute | solution.py:127
  17.2 3.4 %collective-permute-start.6 = (f32[32,256]{1,0:T(8,128)S(1)}, f32[32,256]{1,0:T(8,128)S(1)}, u32[]{:S(2)}, u32[]{:S(2)}) collective-permute-start(f32[32,256]{1,0:T(8,128)S(1)} %get-tuple-element.45), channel_id=1, source_target_pairs={{0,20},{1,21},{2,22},{3,23},{4,16},{5,17},{6,18},{7,19},{8,28},{9,... | collective-permute-start | bytes 98312 | tf_op jit(solution)/shard_map/ppermute | solution.py:127
  17.7 3.3 %collective-permute-start.5 = (f32[32,256]{1,0:T(8,128)S(1)}, f32[32,256]{1,0:T(8,128)S(1)}, u32[]{:S(2)}, u32[]{:S(2)}) collective-permute-start(f32[32,256]{1,0:T(8,128)S(1)} %get-tuple-element.46), channel_id=1, source_target_pairs={{0,12},{1,13},{2,14},{3,15},{4,8},{5,9},{6,10},{7,11},{8,4},{9,5},... | collective-permute-start | bytes 98312 | tf_op jit(solution)/shard_map/ppermute | solution.py:127
  21.0 5.2 %collective-permute-start.11 = (f32[32,256]{1,0:T(8,128)S(1)}, f32[32,256]{1,0:T(8,128)S(1)}, u32[]{:S(2)}, u32[]{:S(2)}) collective-permute-start(f32[32,256]{1,0:T(8,128)S(1)} %add_add_fusion.1), channel_id=1, source_target_pairs={{0,7},{1,6},{2,5},{3,4},{4,3},{5,2},{6,1},{7,0},{8,15},{9,14},{10,... | collective-permute-start | bytes 98312 | tf_op jit(solution)/shard_map/ppermute | solution.py:127
  24.5 4.2 %collective-permute-start.10 = (f32[32,256]{1,0:T(8,128)S(1)}, f32[32,256]{1,0:T(8,128)S(1)}, u32[]{:S(2)}, u32[]{:S(2)}) collective-permute-start(f32[32,256]{1,0:T(8,128)S(1)} %add_add_fusion.1), channel_id=1, source_target_pairs={{0,6},{1,7},{2,4},{3,5},{4,2},{5,3},{6,0},{7,1},{8,14},{9,15},{10,... | collective-permute-start | bytes 98312 | tf_op jit(solution)/shard_map/ppermute | solution.py:127
  24.5 4.2 %collective-permute-start.9 = (f32[32,256]{1,0:T(8,128)S(1)}, f32[32,256]{1,0:T(8,128)S(1)}, u32[]{:S(2)}, u32[]{:S(2)}) collective-permute-start(f32[32,256]{1,0:T(8,128)S(1)} %add_add_fusion.1), channel_id=1, source_target_pairs={{0,5},{1,4},{2,7},{3,6},{4,1},{5,0},{6,3},{7,2},{8,13},{9,12},{10,... | collective-permute-start | bytes 98312 | tf_op jit(solution)/shard_map/ppermute | solution.py:127
  25.1 3.7 %collective-permute-start.8 = (f32[32,256]{1,0:T(8,128)S(1)}, f32[32,256]{1,0:T(8,128)S(1)}, u32[]{:S(2)}, u32[]{:S(2)}) collective-permute-start(f32[32,256]{1,0:T(8,128)S(1)} %add_add_fusion.1), channel_id=1, source_target_pairs={{0,4},{1,5},{2,6},{3,7},{4,0},{5,1},{6,2},{7,3},{8,12},{9,13},{10,... | collective-permute-start | bytes 98312 | tf_op jit(solution)/shard_map/ppermute | solution.py:127

commit v4 on v3

--- a/solution.py
+++ b/solution.py
@@ -119,21 +119,27 @@
         copy.wait()
 
 
-def swap(x, axes, sizes, flips):
+def sum_kernel(*refs):
+    *parts, total_ref = [ref[...] for ref in refs[:-1]] + [refs[-1]]
+    parts = parts[:1] + parts[:0:-1]
+    while len(parts) > 1:
+        parts = [a + b for a, b in zip(parts[: len(parts) // 2], parts[len(parts) // 2 :])]
+    total_ref[...] = parts[0]
+
+
+def send(x, sizes, flip, shift=0, step=1, size=1):
     blk, rep = sizes
-    pairs = [
-        (b * rep + r, (b ^ flips[0]) * rep + (r ^ flips[1])) for b in range(blk) for r in range(rep)
-    ]
-    return lax.ppermute(x, axes, pairs)
+    pairs = []
+    for b in range(blk):
+        for r in range(rep):
+            digit = r // step % size
+            pairs.append((b * rep + r, (b ^ flip) * rep + r + ((digit + shift) % size - digit) * step))
+    return lax.ppermute(x, ("blk", "rep"), pairs)
 
 
 def digits(size, low):
-    groups = []
-    while 1 << low < size:
-        high = min(low + 2, size.bit_length() - 1)
-        groups.append([d << low for d in range(1, 1 << (high - low))])
-        low = high
-    return groups
+    end = size.bit_length() - 1
+    return [(bit, min(bit + 2, end)) for bit in range(low, end, 2)]
 
 
 def pair_sum(parts):
@@ -143,7 +149,7 @@
 
 
 def per_device(sizes, point_pool, batch_rows, targets, center_pool, center_rows, coefs):
-    send = functools.partial(swap, axes=("blk", "rep"), sizes=sizes)
+    to = functools.partial(send, sizes=sizes)
     each, outs = coefs.shape
     width = point_pool.shape[1]
     count = batch_rows.shape[0]
@@ -170,10 +176,11 @@
         name="piece",
     )(in_hbm(center_rows.reshape(1, each)), in_hbm(center_pool), in_hbm(coefs), in_hbm(rows), pool)
 
-    chips, reps = digits(sizes[0], 1), digits(sizes[1], 0)
+    chips = [[d << low for d in range(1, 1 << (high - low))] for low, high in digits(sizes[0], 1)]
+    reps = digits(sizes[1], 0)
     block = piece
     near = [0] + chips[0]
-    parts = [block] + [send(block, flips=(d, 0)) for d in near[1:]]
+    parts = [block] + [to(block, flip=d) for d in near[1:]]
     points, point_norm, goals = pl.pallas_call(
         points_kernel,
         out_shape=(
@@ -197,7 +204,7 @@
     parts, points, point_norm, goals = lax.optimization_barrier((parts, points, point_norm, goals))
     block = jnp.concatenate(parts, axis=0)
     for group in chips[1:]:
-        block = jnp.concatenate([block] + [send(block, flips=(d, 0)) for d in group], axis=0)
+        block = jnp.concatenate([block] + [to(block, flip=d) for d in group], axis=0)
     half = block.shape[0]
     far = half // (len(near) * each)
     residual, kept, sent = pl.pallas_call(
@@ -217,15 +224,15 @@
         ],
         compiler_params=pltpu.CompilerParams(vmem_limit_bytes=32 << 20),
         name="residual",
-    )(points, point_norm, goals, block, send(block, flips=(1, 0)))
-
-    total = (kept + send(sent, flips=(1, 0))).reshape(far, len(near), each, outs)
+    )(points, point_norm, goals, block, to(block, flip=1))
+
+    total = (kept + to(sent, flip=1)).reshape(far, len(near), each, outs)
     for group in reversed(chips[1:]):
         low = total.shape[0] // (len(group) + 1)
         blocks = [total[i * low : (i + 1) * low] for i in range(len(group) + 1)]
-        total = pair_sum(blocks[:1] + [send(x, flips=(d, 0)) for x, d in zip(blocks[1:], group)])
+        total = pair_sum(blocks[:1] + [to(x, flip=d) for x, d in zip(blocks[1:], group)])
     rows = {d: total[0, i] for i, d in enumerate(near)}
-    parts = [rows[0]] + [send(rows[d], flips=(d ^ 1, 0)) for d in chips[0]]
+    parts = [rows[0]] + [to(rows[d], flip=d ^ 1) for d in chips[0]]
     residual = pl.pallas_call(
         write_kernel,
         out_shape=jax.ShapeDtypeStruct(residual.shape, F32),
@@ -239,9 +246,18 @@
     parts, residual = lax.optimization_barrier((parts, residual))
     mine = pair_sum(parts)
     flip = 1
-    for group in reps:
-        first = send(mine, flips=(1, 0)) if flip else mine
-        mine, flip = pair_sum([first] + [send(mine, flips=(flip, d)) for d in group]), 0
+    for low, high in reps:
+        size = 1 << (high - low)
+        around = [to(mine, flip=flip, shift=k, step=1 << low, size=size) for k in range(1, size)]
+        mine = pl.pallas_call(
+            sum_kernel,
+            out_shape=jax.ShapeDtypeStruct(mine.shape, F32),
+            in_specs=[VMEM] * size,
+            out_specs=VMEM,
+            compiler_params=pltpu.CompilerParams(vmem_limit_bytes=4 << 20),
+            name="sum",
+        )(to(mine, flip=1) if flip else mine, *around[::-1])
+        flip = 0
     return residual, mine
 
 

time: 29.5 us -> 29.1 us (0.986)
  waiting for transfers between devices: 8.7 us -> 7.18 us
  starting transfers between devices: 12.2 us -> 13.3 us
  Pallas kernels: 7.01 us -> 7.64 us
  other arithmetic: 0.65 us -> 0.03 us
    ppermute x12, waiting for transfers between devices: 8.7 us -> 7.18 us  [send(): return lax.ppermute(x, ('blk', 'rep'), pairs)]
    ppermute x12, starting transfers between devices: 12.2 us -> 13.3 us  [send(): return lax.ppermute(x, ('blk', 'rep'), pairs)]
    add x2 -> x1, other arithmetic: 0.64 us -> 0.01 us  [pair_sum(): parts = [parts[i] + parts[i + 1] for i in range(0, len(parts), 2)]]
    pallas_call x0 -> x1, Pallas kernels: none -> 0.62 us  [per_device(): pl.pallas_call(sum_kernel, out_shape=jax.ShapeDtypeStruct(mine.shape, F32...]
where the time goes in v4:
time: 29.1 us; the launch traced here: 28.9 us
  starting transfers between devices  13.3 us (46%)
  Pallas kernels  7.64 us (26%)
  waiting for transfers between devices  7.18 us (25%)
  between operations  0.72 us (2%)
    ppermute x12, starting transfers between devices, send(): return lax.ppermute(x, ('blk', 'rep'), pairs)  13.3 us
    ppermute x12, waiting for transfers between devices, send(): return lax.ppermute(x, ('blk', 'rep'), pairs)  7.18 us
    pallas_call x1, Pallas kernels, per_device(): pl.pallas_call(points_kernel, out_shape=(pltpu.VMEM((count, width), BF16)...  3.42 us
    pallas_call x1, Pallas kernels, per_device(): pl.pallas_call(piece_kernel, out_shape=(pltpu.VMEM((each, width + outs),...  1.37 us
    pallas_call x1, Pallas kernels, per_device(): pl.pallas_call(functools.partial(residual_kernel, far, each), out_shape=(...  1.24 us
    pallas_call x1, Pallas kernels, per_device(): pl.pallas_call(write_kernel, out_shape=jax.ShapeDtypeStruct(residual.shap...  0.99 us
    pallas_call x1, Pallas kernels, per_device(): pl.pallas_call(sum_kernel, out_shape=jax.ShapeDtypeStruct(mine.shape, F32...  0.62 us
  transfers between devices with their start and end apart: 12, of which 9 were waited for; matrix products, arithmetic and copies ran while one was open for 0% of the time, Pallas kernels for 15%

profile of v4, /device:TPU:0, one launch (start us, length us, event | category | flops | bytes accessed | tf_op | source)
XLA Modules:
  0.0 28.9 jit_solution(10259604108828277147)
XLA Ops:
  0.6 1.4 %piece.1 = (bf16[32,1280]{1,0:T(8,128)(2,1)S(1)}, s32[8,128]{1,0:T(8,128)S(1)}, bf16[512,1024]{1,0:T(8,128)(2,1)S(1)}) custom-call(s32[1,32]{1,0:T(1,128)} %bitcast.13, bf16[64,1024]{1,0:T(8,128)(2,1)} %centers_hbm.1, bf16[32,256]{1,0:T(8,128)(2,1)} %coefs_hbm.1, s32[8,128]{1,0:T(8,128)} %bitcast.12, bf16[1280,1024]{1,0:T(8,128)(2,1)} %pool_hbm.3), custom_call_target="tpu_custom_call" | custom-call | tf_op jit(solution)/shard_map/piece/pallas_call | solution.py:160
  2.0 4.0 %collective-permute-start.2 = (bf16[32,1280]{1,0:T(8,128)(2,1)S(1)}, bf16[32,1280]{1,0:T(8,128)(2,1)S(1)}, u32[]{:S(2)}, u32[]{:S(2)}) collective-permute-start(bf16[32,1280]{1,0:T(8,128)(2,1)S(1)} %get-tuple-element.32), channel_id=1, source_target_pairs={{0,24},{1,25},{2,26},{3,27},{4,28},{5,29},{6,30},{7,31},{8,16},{9,... | collective-permute-start | bytes 245768 | tf_op jit(solution)/shard_map/ppermute | solution.py:137
  6.0 0.5 %collective-permute-start.1 = (bf16[32,1280]{1,0:T(8,128)(2,1)S(1)}, bf16[32,1280]{1,0:T(8,128)(2,1)S(1)}, u32[]{:S(2)}, u32[]{:S(2)}) collective-permute-start(bf16[32,1280]{1,0:T(8,128)(2,1)S(1)} %get-tuple-element.32), channel_id=1, source_target_pairs={{0,16},{1,17},{2,18},{3,19},{4,20},{5,21},{6,22},{7,23},{8,24},{9,... | collective-permute-start | bytes 245768 | tf_op jit(solution)/shard_map/ppermute | solution.py:137
  6.6 3.4 %points.1 = (bf16[1024,1024]{1,0:T(8,128)(2,1)S(1)}, f32[1024,1]{1,0:T(8,128)S(1)}, bf16[1024,256]{1,0:T(8,128)(2,1)S(1)}) custom-call(s32[8,128]{1,0:T(8,128)S(1)} %get-tuple-element.24.rows_ref, bf16[512,1024]{1,0:T(8,128)(2,1)S(1)} %get-tuple-element.25.first_ref, bf16[1280,1024]{1,0:T(8,128)(2,1)} %pool_hbm.3, bf16[1024,256]{1,0:T(8,128)(2,1)} %targets_hbm.1), custom_call_target="tpu_custom_call" | custom-call | flops 2147483648 | bytes 5242880 | tf_op jit(solution)/shard_map/points/pallas_call | solution.py:184
  10.0 0.4 %collective-permute-done.1 = bf16[32,1280]{1,0:T(8,128)(2,1)S(1)} collective-permute-done((bf16[32,1280]{1,0:T(8,128)(2,1)S(1)}, bf16[32,1280]{1,0:T(8,128)(2,1)S(1)}, u32[]{:S(2)}, u32[]{:S(2)}) %collective-permute-start.1) | collective-permute-done | bytes 81952 | tf_op jit(solution)/shard_map/ppermute | solution.py:137
  10.4 0.5 %collective-permute-done = bf16[32,1280]{1,0:T(8,128)(2,1)S(1)} collective-permute-done((bf16[32,1280]{1,0:T(8,128)(2,1)S(1)}, bf16[32,1280]{1,0:T(8,128)(2,1)S(1)}, u32[]{:S(2)}, u32[]{:S(2)}) %collective-permute-start) | collective-permute-done | bytes 81952 | tf_op jit(solution)/shard_map/ppermute | solution.py:137
  11.0 1.6 %collective-permute-done.3.other_ref = bf16[128,1280]{1,0:T(8,128)(2,1)S(1)} collective-permute-done((bf16[128,1280]{1,0:T(8,128)(2,1)S(1)}, bf16[128,1280]{1,0:T(8,128)(2,1)S(1)}, u32[]{:S(2)}, u32[]{:S(2)}) %collective-permute-start.3) | collective-permute-done | bytes 327712 | tf_op jit(solution)/shard_map/ppermute | solution.py:137
  12.7 1.2 %residual.1 = (f32[1024,256]{1,0:T(8,128)S(1)}, f32[128,256]{1,0:T(8,128)S(1)}, f32[128,256]{1,0:T(8,128)S(1)}) custom-call(bf16[1024,1024]{1,0:T(8,128)(2,1)S(1)} %get-tuple-element.29.points_ref, f32[1024,1]{1,0:T(8,128)S(1)} %get-tuple-element.30.norm_ref, bf16[1024,256]{1,0:T(8,128)(2,1)S(1)} %get-tuple-element.31.targets_ref, ...), custom_call_target="tpu_custom_call" | custom-call | tf_op jit(solution)/shard_map/residual/pallas_call | solution.py:210
  13.9 0.2 collective-permute-start.4
  14.1 1.2 %collective-permute-done.4 = f32[128,256]{1,0:T(8,128)S(1)} collective-permute-done((f32[128,256]{1,0:T(8,128)S(1)}, f32[128,256]{1,0:T(8,128)S(1)}, u32[]{:S(2)}, u32[]{:S(2)}) %collective-permute-start.4) | collective-permute-done | bytes 131104 | tf_op jit(solution)/shard_map/ppermute | solution.py:137
  15.4 1.8 %collective-permute-start.7 = (f32[32,256]{1,0:T(8,128)S(1)}, f32[32,256]{1,0:T(8,128)S(1)}, u32[]{:S(2)}, u32[]{:S(2)}) collective-permute-start(f32[32,256]{1,0:T(8,128)S(1)} %get-tuple-element.44), channel_id=1, source_target_pairs={{0,28},{1,29},{2,30},{3,31},{4,24},{5,25},{6,26},{7,27},{8,20},{9,... | collective-permute-start | bytes 98312 | tf_op jit(solution)/shard_map/ppermute | solution.py:137
  17.2 0.5 %collective-permute-start.6 = (f32[32,256]{1,0:T(8,128)S(1)}, f32[32,256]{1,0:T(8,128)S(1)}, u32[]{:S(2)}, u32[]{:S(2)}) collective-permute-start(f32[32,256]{1,0:T(8,128)S(1)} %get-tuple-element.45), channel_id=1, source_target_pairs={{0,20},{1,21},{2,22},{3,23},{4,16},{5,17},{6,18},{7,19},{8,28},{9,... | collective-permute-start | bytes 98312 | tf_op jit(solution)/shard_map/ppermute | solution.py:137
  17.7 0.7 %collective-permute-start.5 = (f32[32,256]{1,0:T(8,128)S(1)}, f32[32,256]{1,0:T(8,128)S(1)}, u32[]{:S(2)}, u32[]{:S(2)}) collective-permute-start(f32[32,256]{1,0:T(8,128)S(1)} %get-tuple-element.46), channel_id=1, source_target_pairs={{0,12},{1,13},{2,14},{3,15},{4,8},{5,9},{6,10},{7,11},{8,4},{9,5},... | collective-permute-start | bytes 98312 | tf_op jit(solution)/shard_map/ppermute | solution.py:137
  18.4 1.0 %write.1 = f32[1024,256]{1,0:T(8,128)} custom-call(f32[1024,256]{1,0:T(8,128)S(1)} %get-tuple-element.38.source), custom_call_target="tpu_custom_call" | custom-call | bytes 4194304 | tf_op jit(solution)/shard_map/write/pallas_call | solution.py:236
  19.4 0.3 collective-permute-done.7
  19.7 0.9 %collective-permute-done.6 = f32[32,256]{1,0:T(8,128)S(1)} collective-permute-done((f32[32,256]{1,0:T(8,128)S(1)}, f32[32,256]{1,0:T(8,128)S(1)}, u32[]{:S(2)}, u32[]{:S(2)}) %collective-permute-start.6) | collective-permute-done | bytes 32800 | tf_op jit(solution)/shard_map/ppermute | solution.py:137
  20.5 0.5 %collective-permute-done.5 = f32[32,256]{1,0:T(8,128)S(1)} collective-permute-done((f32[32,256]{1,0:T(8,128)S(1)}, f32[32,256]{1,0:T(8,128)S(1)}, u32[]{:S(2)}, u32[]{:S(2)}) %collective-permute-start.5) | collective-permute-done | bytes 32800 | tf_op jit(solution)/shard_map/ppermute | solution.py:137
  21.0 1.4 %collective-permute-start.11 = (f32[32,256]{1,0:T(8,128)S(1)}, f32[32,256]{1,0:T(8,128)S(1)}, u32[]{:S(2)}, u32[]{:S(2)}) collective-permute-start(f32[32,256]{1,0:T(8,128)S(1)} %add_add_fusion), channel_id=1, source_target_pairs={{0,5},{1,6},{2,7},{3,4},{4,1},{5,2},{6,3},{7,0},{8,13},{9,14},{10,... | collective-permute-start | bytes 98312 | tf_op jit(solution)/shard_map/ppermute | solution.py:137
  22.4 2.5 %collective-permute-start.10 = (f32[32,256]{1,0:T(8,128)S(1)}, f32[32,256]{1,0:T(8,128)S(1)}, u32[]{:S(2)}, u32[]{:S(2)}) collective-permute-start(f32[32,256]{1,0:T(8,128)S(1)} %add_add_fusion), channel_id=1, source_target_pairs={{0,6},{1,7},{2,4},{3,5},{4,2},{5,3},{6,0},{7,1},{8,14},{9,15},{10,... | collective-permute-start | bytes 98312 | tf_op jit(solution)/shard_map/ppermute | solution.py:137
  25.0 1.1 %collective-permute-start.9 = (f32[32,256]{1,0:T(8,128)S(1)}, f32[32,256]{1,0:T(8,128)S(1)}, u32[]{:S(2)}, u32[]{:S(2)}) collective-permute-start(f32[32,256]{1,0:T(8,128)S(1)} %add_add_fusion), channel_id=1, source_target_pairs={{0,7},{1,4},{2,5},{3,6},{4,3},{5,0},{6,1},{7,2},{8,15},{9,12},{10,... | collective-permute-start | bytes 98312 | tf_op jit(solution)/shard_map/ppermute | solution.py:137
  26.1 0.3 %collective-permute-start.8 = (f32[32,256]{1,0:T(8,128)S(1)}, f32[32,256]{1,0:T(8,128)S(1)}, u32[]{:S(2)}, u32[]{:S(2)}) collective-permute-start(f32[32,256]{1,0:T(8,128)S(1)} %add_add_fusion), channel_id=1, source_target_pairs={{0,4},{1,5},{2,6},{3,7},{4,0},{5,1},{6,2},{7,3},{8,12},{9,13},{10,... | collective-permute-start | bytes 98312 | tf_op jit(solution)/shard_map/ppermute | solution.py:137
  26.4 0.6 %collective-permute-done.10.refs_2_ = f32[32,256]{1,0:T(8,128)S(1)} collective-permute-done((f32[32,256]{1,0:T(8,128)S(1)}, f32[32,256]{1,0:T(8,128)S(1)}, u32[]{:S(2)}, u32[]{:S(2)}) %collective-permute-start.10) | collective-permute-done | bytes 32800 | tf_op jit(solution)/shard_map/ppermute | solution.py:137
  27.0 1.3 %collective-permute-done.9.refs_1_ = f32[32,256]{1,0:T(8,128)S(1)} collective-permute-done((f32[32,256]{1,0:T(8,128)S(1)}, f32[32,256]{1,0:T(8,128)S(1)}, u32[]{:S(2)}, u32[]{:S(2)}) %collective-permute-start.9) | collective-permute-done | bytes 32800 | tf_op jit(solution)/shard_map/ppermute | solution.py:137
  28.3 0.6 %sum.1 = f32[32,256]{1,0:T(8,128)} custom-call(f32[32,256]{1,0:T(8,128)S(1)} %collective-permute-done.8.refs_0_, f32[32,256]{1,0:T(8,128)S(1)} %collective-permute-done.9.refs_1_, f32[32,256]{1,0:T(8,128)S(1)} %collective-permute-done.10.refs_2_, f32[32,256]{1,0:T(8,128)S(1)} %collective-permute-done.11.refs_3_), custom_call_target="tpu_custom_call" | custom-call | tf_op jit(solution)/shard_map/sum/pallas_call | solution.py:252
  (12 shorter events, 0.3 us)
Async XLA Ops:
  2.0 8.0 %collective-permute-start.2 = (bf16[32,1280]{1,0:T(8,128)(2,1)S(1)}, bf16[32,1280]{1,0:T(8,128)(2,1)S(1)}, u32[]{:S(2)}, u32[]{:S(2)}) collective-permute-start(bf16[32,1280]{1,0:T(8,128)(2,1)S(1)} %get-tuple-element.32), channel_id=1, source_target_pairs={{0,24},{1,25},{2,26},{3,27},{4,28},{5,29},{6,30},{7,31},{8,16},{9,... | collective-permute-start | bytes 245768 | tf_op jit(solution)/shard_map/ppermute | solution.py:137
  6.0 4.4 %collective-permute-start.1 = (bf16[32,1280]{1,0:T(8,128)(2,1)S(1)}, bf16[32,1280]{1,0:T(8,128)(2,1)S(1)}, u32[]{:S(2)}, u32[]{:S(2)}) collective-permute-start(bf16[32,1280]{1,0:T(8,128)(2,1)S(1)} %get-tuple-element.32), channel_id=1, source_target_pairs={{0,16},{1,17},{2,18},{3,19},{4,20},{5,21},{6,22},{7,23},{8,24},{9,... | collective-permute-start | bytes 245768 | tf_op jit(solution)/shard_map/ppermute | solution.py:137
  6.5 4.4 %collective-permute-start = (bf16[32,1280]{1,0:T(8,128)(2,1)S(1)}, bf16[32,1280]{1,0:T(8,128)(2,1)S(1)}, u32[]{:S(2)}, u32[]{:S(2)}) collective-permute-start(bf16[32,1280]{1,0:T(8,128)(2,1)S(1)} %get-tuple-element.32), channel_id=1, source_target_pairs={{0,8},{1,9},{2,10},{3,11},{4,12},{5,13},{6,14},{7,15},{8,0},{9,1},... | collective-permute-start | bytes 245768 | tf_op jit(solution)/shard_map/ppermute | solution.py:137
  11.0 1.7 %collective-permute-start.3 = (bf16[128,1280]{1,0:T(8,128)(2,1)S(1)}, bf16[128,1280]{1,0:T(8,128)(2,1)S(1)}, u32[]{:S(2)}, u32[]{:S(2)}) collective-permute-start(bf16[128,1280]{1,0:T(8,128)(2,1)S(1)} %constant_dynamic-update-slice_fusion.own_ref), channel_id=1, source_target_pairs={{0,4},{1,5},{2,6},{3,7},{4,0},{5,1},{6,2},{7,3},{8,12},{9,13},{10,... | collective-permute-start | bytes 983048 | tf_op jit(solution)/shard_map/ppermute | solution.py:137
  13.9 1.4 %collective-permute-start.4 = (f32[128,256]{1,0:T(8,128)S(1)}, f32[128,256]{1,0:T(8,128)S(1)}, u32[]{:S(2)}, u32[]{:S(2)}) collective-permute-start(f32[128,256]{1,0:T(8,128)S(1)} %get-tuple-element.37), channel_id=1, source_target_pairs={{0,4},{1,5},{2,6},{3,7},{4,0},{5,1},{6,2},{7,3},{8,12},{9,13},{10,... | collective-permute-start | bytes 393224 | tf_op jit(solution)/shard_map/ppermute | solution.py:137
  15.4 4.3 %collective-permute-start.7 = (f32[32,256]{1,0:T(8,128)S(1)}, f32[32,256]{1,0:T(8,128)S(1)}, u32[]{:S(2)}, u32[]{:S(2)}) collective-permute-start(f32[32,256]{1,0:T(8,128)S(1)} %get-tuple-element.44), channel_id=1, source_target_pairs={{0,28},{1,29},{2,30},{3,31},{4,24},{5,25},{6,26},{7,27},{8,20},{9,... | collective-permute-start | bytes 98312 | tf_op jit(solution)/shard_map/ppermute | solution.py:137
  17.2 3.4 %collective-permute-start.6 = (f32[32,256]{1,0:T(8,128)S(1)}, f32[32,256]{1,0:T(8,128)S(1)}, u32[]{:S(2)}, u32[]{:S(2)}) collective-permute-start(f32[32,256]{1,0:T(8,128)S(1)} %get-tuple-element.45), channel_id=1, source_target_pairs={{0,20},{1,21},{2,22},{3,23},{4,16},{5,17},{6,18},{7,19},{8,28},{9,... | collective-permute-start | bytes 98312 | tf_op jit(solution)/shard_map/ppermute | solution.py:137
  17.7 3.3 %collective-permute-start.5 = (f32[32,256]{1,0:T(8,128)S(1)}, f32[32,256]{1,0:T(8,128)S(1)}, u32[]{:S(2)}, u32[]{:S(2)}) collective-permute-start(f32[32,256]{1,0:T(8,128)S(1)} %get-tuple-element.46), channel_id=1, source_target_pairs={{0,12},{1,13},{2,14},{3,15},{4,8},{5,9},{6,10},{7,11},{8,4},{9,5},... | collective-permute-start | bytes 98312 | tf_op jit(solution)/shard_map/ppermute | solution.py:137
  21.0 5.4 %collective-permute-start.11 = (f32[32,256]{1,0:T(8,128)S(1)}, f32[32,256]{1,0:T(8,128)S(1)}, u32[]{:S(2)}, u32[]{:S(2)}) collective-permute-start(f32[32,256]{1,0:T(8,128)S(1)} %add_add_fusion), channel_id=1, source_target_pairs={{0,5},{1,6},{2,7},{3,4},{4,1},{5,2},{6,3},{7,0},{8,13},{9,14},{10,... | collective-permute-start | bytes 98312 | tf_op jit(solution)/shard_map/ppermute | solution.py:137
  22.4 4.6 %collective-permute-start.10 = (f32[32,256]{1,0:T(8,128)S(1)}, f32[32,256]{1,0:T(8,128)S(1)}, u32[]{:S(2)}, u32[]{:S(2)}) collective-permute-start(f32[32,256]{1,0:T(8,128)S(1)} %add_add_fusion), channel_id=1, source_target_pairs={{0,6},{1,7},{2,4},{3,5},{4,2},{5,3},{6,0},{7,1},{8,14},{9,15},{10,... | collective-permute-start | bytes 98312 | tf_op jit(solution)/shard_map/ppermute | solution.py:137
  25.0 3.3 %collective-permute-start.9 = (f32[32,256]{1,0:T(8,128)S(1)}, f32[32,256]{1,0:T(8,128)S(1)}, u32[]{:S(2)}, u32[]{:S(2)}) collective-permute-start(f32[32,256]{1,0:T(8,128)S(1)} %add_add_fusion), channel_id=1, source_target_pairs={{0,7},{1,4},{2,5},{3,6},{4,3},{5,0},{6,1},{7,2},{8,15},{9,12},{10,... | collective-permute-start | bytes 98312 | tf_op jit(solution)/shard_map/ppermute | solution.py:137
  26.1 2.2 %collective-permute-start.8 = (f32[32,256]{1,0:T(8,128)S(1)}, f32[32,256]{1,0:T(8,128)S(1)}, u32[]{:S(2)}, u32[]{:S(2)}) collective-permute-start(f32[32,256]{1,0:T(8,128)S(1)} %add_add_fusion), channel_id=1, source_target_pairs={{0,4},{1,5},{2,6},{3,7},{4,0},{5,1},{6,2},{7,3},{8,12},{9,13},{10,... | collective-permute-start | bytes 98312 | tf_op jit(solution)/shard_map/ppermute | solution.py:137

commit v5 on v4

--- a/solution.py
+++ b/solution.py
@@ -1,4 +1,5 @@
 import functools
+import math
 
 import jax
 import jax.numpy as jnp
@@ -9,6 +10,7 @@
 
 F32, BF16 = jnp.float32, jnp.bfloat16
 STEPS = 2
+ACROSS = (1, 1, 0, 0)
 VMEM = pl.BlockSpec(memory_space=pltpu.VMEM)
 ANY = pl.BlockSpec(memory_space=pl.ANY)
 
@@ -92,26 +94,26 @@
     for g in range(width // 128):
         part = centers[:, g * 128 : (g + 1) * 128].astype(F32)
         squares = squares + part * part
-    center_norm = jnp.sum(squares.T, axis=0, keepdims=True)
+    scale = 1.0 / (width * math.log(2.0))
+    center_norm = jnp.sum(squares.T, axis=0, keepdims=True) * -scale
     rows = count // STEPS
     for m in range(STEPS):
         at = slice(m * rows, (m + 1) * rows)
         inner = dot(points_ref[at, :], centers[...], ((1,), (1,)))
-        distance = norm_ref[at, :] + center_norm - 2.0 * inner
-        kernel[at, :] = jnp.exp(distance * (-1.0 / width)).astype(BF16)
+        norms = norm_ref[at, :] * -scale + center_norm
+        kernel[at, :] = jnp.exp2(norms + inner * (2.0 * scale)).astype(BF16)
     for m in range(STEPS):
         at = slice(m * rows, (m + 1) * rows)
         left = dot(kernel[at, :], coefs[...], ((1,), (0,))) - targets_ref[at, :].astype(F32)
         residual_ref[at, :] = left
         rounded[at, :] = left.astype(BF16)
     grad = dot(kernel[...], rounded[...], ((0,), (0,)))
-    step = half // far
     for f in range(far):
-        at = f * step
-        kept_ref[at : at + each, :] = grad[half + at : half + at + each]
-        kept_ref[at + each : at + step, :] = grad[at + each : at + step]
-        sent_ref[at : at + each, :] = grad[at : at + each]
-        sent_ref[at + each : at + step, :] = grad[half + at + each : half + at + step]
+        for i, swapped in enumerate(ACROSS):
+            at = (f * len(ACROSS) + i) * each
+            here, there = grad[at : at + each], grad[half + at : half + at + each]
+            kept_ref[at : at + each, :] = there if swapped else here
+            sent_ref[at : at + each, :] = here if swapped else there
 
 
 def write_kernel(source, target, sem):
@@ -178,9 +180,8 @@
 
     chips = [[d << low for d in range(1, 1 << (high - low))] for low, high in digits(sizes[0], 1)]
     reps = digits(sizes[1], 0)
-    block = piece
     near = [0] + chips[0]
-    parts = [block] + [to(block, flip=d) for d in near[1:]]
+    parts = [piece] + [to(piece, flip=d ^ across) for d, across in zip(near[1:], ACROSS[1:])]
     points, point_norm, goals = pl.pallas_call(
         points_kernel,
         out_shape=(

time: 29.1 us -> 29 us (level)
  no operation moved by 1% of the time
where the time goes in v5:
time: 29 us; the launch traced here: 28.8 us
  starting transfers between devices  13.2 us (46%)
  Pallas kernels  7.64 us (26%)
  waiting for transfers between devices  7.2 us (25%)
  between operations  0.72 us (2%)
    ppermute x12, starting transfers between devices, send(): return lax.ppermute(x, ('blk', 'rep'), pairs)  13.2 us
    ppermute x12, waiting for transfers between devices, send(): return lax.ppermute(x, ('blk', 'rep'), pairs)  7.2 us
    pallas_call x1, Pallas kernels, per_device(): pl.pallas_call(points_kernel, out_shape=(pltpu.VMEM((count, width), BF16)...  3.42 us
    pallas_call x1, Pallas kernels, per_device(): pl.pallas_call(piece_kernel, out_shape=(pltpu.VMEM((each, width + outs),...  1.37 us
    pallas_call x1, Pallas kernels, per_device(): pl.pallas_call(functools.partial(residual_kernel, far, each), out_shape=(...  1.24 us
    pallas_call x1, Pallas kernels, per_device(): pl.pallas_call(write_kernel, out_shape=jax.ShapeDtypeStruct(residual.shap...  0.99 us
    pallas_call x1, Pallas kernels, per_device(): pl.pallas_call(sum_kernel, out_shape=jax.ShapeDtypeStruct(mine.shape, F32...  0.62 us
  transfers between devices with their start and end apart: 12, of which 9 were waited for; matrix products, arithmetic and copies ran while one was open for 0% of the time, Pallas kernels for 15%

profile of v5, /device:TPU:0, one launch (start us, length us, event | category | flops | bytes accessed | tf_op | source)
XLA Modules:
  0.0 28.8 jit_solution(10876610174909544308)
XLA Ops:
  0.6 1.4 %piece.1 = (bf16[32,1280]{1,0:T(8,128)(2,1)S(1)}, s32[8,128]{1,0:T(8,128)S(1)}, bf16[512,1024]{1,0:T(8,128)(2,1)S(1)}) custom-call(s32[1,32]{1,0:T(1,128)} %bitcast.13, bf16[64,1024]{1,0:T(8,128)(2,1)} %centers_hbm.1, bf16[32,256]{1,0:T(8,128)(2,1)} %coefs_hbm.1, s32[8,128]{1,0:T(8,128)} %bitcast.12, bf16[1280,1024]{1,0:T(8,128)(2,1)} %pool_hbm.3), custom_call_target="tpu_custom_call" | custom-call | tf_op jit(solution)/shard_map/piece/pallas_call | solution.py:162
  2.0 4.0 %collective-permute-start.2 = (bf16[32,1280]{1,0:T(8,128)(2,1)S(1)}, bf16[32,1280]{1,0:T(8,128)(2,1)S(1)}, u32[]{:S(2)}, u32[]{:S(2)}) collective-permute-start(bf16[32,1280]{1,0:T(8,128)(2,1)S(1)} %get-tuple-element.32), channel_id=1, source_target_pairs={{0,24},{1,25},{2,26},{3,27},{4,28},{5,29},{6,30},{7,31},{8,16},{9,... | collective-permute-start | bytes 245768 | tf_op jit(solution)/shard_map/ppermute | solution.py:139
  6.0 0.5 %collective-permute-start.1 = (bf16[32,1280]{1,0:T(8,128)(2,1)S(1)}, bf16[32,1280]{1,0:T(8,128)(2,1)S(1)}, u32[]{:S(2)}, u32[]{:S(2)}) collective-permute-start(bf16[32,1280]{1,0:T(8,128)(2,1)S(1)} %get-tuple-element.32), channel_id=1, source_target_pairs={{0,16},{1,17},{2,18},{3,19},{4,20},{5,21},{6,22},{7,23},{8,24},{9,... | collective-permute-start | bytes 245768 | tf_op jit(solution)/shard_map/ppermute | solution.py:139
  6.5 3.4 %points.1 = (bf16[1024,1024]{1,0:T(8,128)(2,1)S(1)}, f32[1024,1]{1,0:T(8,128)S(1)}, bf16[1024,256]{1,0:T(8,128)(2,1)S(1)}) custom-call(s32[8,128]{1,0:T(8,128)S(1)} %get-tuple-element.24.rows_ref, bf16[512,1024]{1,0:T(8,128)(2,1)S(1)} %get-tuple-element.25.first_ref, bf16[1280,1024]{1,0:T(8,128)(2,1)} %pool_hbm.3, bf16[1024,256]{1,0:T(8,128)(2,1)} %targets_hbm.1), custom_call_target="tpu_custom_call" | custom-call | flops 2147483648 | bytes 5242880 | tf_op jit(solution)/shard_map/points/pallas_call | solution.py:185
  9.9 0.5 %collective-permute-done.1 = bf16[32,1280]{1,0:T(8,128)(2,1)S(1)} collective-permute-done((bf16[32,1280]{1,0:T(8,128)(2,1)S(1)}, bf16[32,1280]{1,0:T(8,128)(2,1)S(1)}, u32[]{:S(2)}, u32[]{:S(2)}) %collective-permute-start.1) | collective-permute-done | bytes 81952 | tf_op jit(solution)/shard_map/ppermute | solution.py:139
  10.4 0.3 collective-permute-done
  10.8 1.6 %collective-permute-done.3.other_ref = bf16[128,1280]{1,0:T(8,128)(2,1)S(1)} collective-permute-done((bf16[128,1280]{1,0:T(8,128)(2,1)S(1)}, bf16[128,1280]{1,0:T(8,128)(2,1)S(1)}, u32[]{:S(2)}, u32[]{:S(2)}) %collective-permute-start.3) | collective-permute-done | bytes 327712 | tf_op jit(solution)/shard_map/ppermute | solution.py:139
  12.4 1.2 %residual.1 = (f32[1024,256]{1,0:T(8,128)S(1)}, f32[128,256]{1,0:T(8,128)S(1)}, f32[128,256]{1,0:T(8,128)S(1)}) custom-call(bf16[1024,1024]{1,0:T(8,128)(2,1)S(1)} %get-tuple-element.29.points_ref, f32[1024,1]{1,0:T(8,128)S(1)} %get-tuple-element.30.norm_ref, bf16[1024,256]{1,0:T(8,128)(2,1)S(1)} %get-tuple-element.31.targets_ref, ...), custom_call_target="tpu_custom_call" | custom-call | tf_op jit(solution)/shard_map/residual/pallas_call | solution.py:211
  13.7 0.2 collective-permute-start.4
  13.9 1.2 %collective-permute-done.4 = f32[128,256]{1,0:T(8,128)S(1)} collective-permute-done((f32[128,256]{1,0:T(8,128)S(1)}, f32[128,256]{1,0:T(8,128)S(1)}, u32[]{:S(2)}, u32[]{:S(2)}) %collective-permute-start.4) | collective-permute-done | bytes 131104 | tf_op jit(solution)/shard_map/ppermute | solution.py:139
  15.1 2.0 %collective-permute-start.7 = (f32[32,256]{1,0:T(8,128)S(1)}, f32[32,256]{1,0:T(8,128)S(1)}, u32[]{:S(2)}, u32[]{:S(2)}) collective-permute-start(f32[32,256]{1,0:T(8,128)S(1)} %get-tuple-element.44), channel_id=1, source_target_pairs={{0,28},{1,29},{2,30},{3,31},{4,24},{5,25},{6,26},{7,27},{8,20},{9,... | collective-permute-start | bytes 98312 | tf_op jit(solution)/shard_map/ppermute | solution.py:139
  17.2 0.4 %collective-permute-start.6 = (f32[32,256]{1,0:T(8,128)S(1)}, f32[32,256]{1,0:T(8,128)S(1)}, u32[]{:S(2)}, u32[]{:S(2)}) collective-permute-start(f32[32,256]{1,0:T(8,128)S(1)} %get-tuple-element.45), channel_id=1, source_target_pairs={{0,20},{1,21},{2,22},{3,23},{4,16},{5,17},{6,18},{7,19},{8,28},{9,... | collective-permute-start | bytes 98312 | tf_op jit(solution)/shard_map/ppermute | solution.py:139
  17.5 0.6 %collective-permute-start.5 = (f32[32,256]{1,0:T(8,128)S(1)}, f32[32,256]{1,0:T(8,128)S(1)}, u32[]{:S(2)}, u32[]{:S(2)}) collective-permute-start(f32[32,256]{1,0:T(8,128)S(1)} %get-tuple-element.46), channel_id=1, source_target_pairs={{0,12},{1,13},{2,14},{3,15},{4,8},{5,9},{6,10},{7,11},{8,4},{9,5},... | collective-permute-start | bytes 98312 | tf_op jit(solution)/shard_map/ppermute | solution.py:139
  18.2 1.0 %write.1 = f32[1024,256]{1,0:T(8,128)} custom-call(f32[1024,256]{1,0:T(8,128)S(1)} %get-tuple-element.38.source), custom_call_target="tpu_custom_call" | custom-call | bytes 4194304 | tf_op jit(solution)/shard_map/write/pallas_call | solution.py:237
  19.2 0.3 collective-permute-done.7
  19.4 1.1 %collective-permute-done.6 = f32[32,256]{1,0:T(8,128)S(1)} collective-permute-done((f32[32,256]{1,0:T(8,128)S(1)}, f32[32,256]{1,0:T(8,128)S(1)}, u32[]{:S(2)}, u32[]{:S(2)}) %collective-permute-start.6) | collective-permute-done | bytes 32800 | tf_op jit(solution)/shard_map/ppermute | solution.py:139
  20.5 0.4 %collective-permute-done.5 = f32[32,256]{1,0:T(8,128)S(1)} collective-permute-done((f32[32,256]{1,0:T(8,128)S(1)}, f32[32,256]{1,0:T(8,128)S(1)}, u32[]{:S(2)}, u32[]{:S(2)}) %collective-permute-start.5) | collective-permute-done | bytes 32800 | tf_op jit(solution)/shard_map/ppermute | solution.py:139
  20.9 1.5 %collective-permute-start.11 = (f32[32,256]{1,0:T(8,128)S(1)}, f32[32,256]{1,0:T(8,128)S(1)}, u32[]{:S(2)}, u32[]{:S(2)}) collective-permute-start(f32[32,256]{1,0:T(8,128)S(1)} %add_add_fusion), channel_id=1, source_target_pairs={{0,5},{1,6},{2,7},{3,4},{4,1},{5,2},{6,3},{7,0},{8,13},{9,14},{10,... | collective-permute-start | bytes 98312 | tf_op jit(solution)/shard_map/ppermute | solution.py:139
  22.4 2.5 %collective-permute-start.10 = (f32[32,256]{1,0:T(8,128)S(1)}, f32[32,256]{1,0:T(8,128)S(1)}, u32[]{:S(2)}, u32[]{:S(2)}) collective-permute-start(f32[32,256]{1,0:T(8,128)S(1)} %add_add_fusion), channel_id=1, source_target_pairs={{0,6},{1,7},{2,4},{3,5},{4,2},{5,3},{6,0},{7,1},{8,14},{9,15},{10,... | collective-permute-start | bytes 98312 | tf_op jit(solution)/shard_map/ppermute | solution.py:139
  24.8 1.2 %collective-permute-start.9 = (f32[32,256]{1,0:T(8,128)S(1)}, f32[32,256]{1,0:T(8,128)S(1)}, u32[]{:S(2)}, u32[]{:S(2)}) collective-permute-start(f32[32,256]{1,0:T(8,128)S(1)} %add_add_fusion), channel_id=1, source_target_pairs={{0,7},{1,4},{2,5},{3,6},{4,3},{5,0},{6,1},{7,2},{8,15},{9,12},{10,... | collective-permute-start | bytes 98312 | tf_op jit(solution)/shard_map/ppermute | solution.py:139
  26.0 0.3 %collective-permute-start.8 = (f32[32,256]{1,0:T(8,128)S(1)}, f32[32,256]{1,0:T(8,128)S(1)}, u32[]{:S(2)}, u32[]{:S(2)}) collective-permute-start(f32[32,256]{1,0:T(8,128)S(1)} %add_add_fusion), channel_id=1, source_target_pairs={{0,4},{1,5},{2,6},{3,7},{4,0},{5,1},{6,2},{7,3},{8,12},{9,13},{10,... | collective-permute-start | bytes 98312 | tf_op jit(solution)/shard_map/ppermute | solution.py:139
  26.3 0.7 %collective-permute-done.10.refs_2_ = f32[32,256]{1,0:T(8,128)S(1)} collective-permute-done((f32[32,256]{1,0:T(8,128)S(1)}, f32[32,256]{1,0:T(8,128)S(1)}, u32[]{:S(2)}, u32[]{:S(2)}) %collective-permute-start.10) | collective-permute-done | bytes 32800 | tf_op jit(solution)/shard_map/ppermute | solution.py:139
  27.0 1.2 %collective-permute-done.9.refs_1_ = f32[32,256]{1,0:T(8,128)S(1)} collective-permute-done((f32[32,256]{1,0:T(8,128)S(1)}, f32[32,256]{1,0:T(8,128)S(1)}, u32[]{:S(2)}, u32[]{:S(2)}) %collective-permute-start.9) | collective-permute-done | bytes 32800 | tf_op jit(solution)/shard_map/ppermute | solution.py:139
  28.2 0.6 %sum.1 = f32[32,256]{1,0:T(8,128)} custom-call(f32[32,256]{1,0:T(8,128)S(1)} %collective-permute-done.8.refs_0_, f32[32,256]{1,0:T(8,128)S(1)} %collective-permute-done.9.refs_1_, f32[32,256]{1,0:T(8,128)S(1)} %collective-permute-done.10.refs_2_, f32[32,256]{1,0:T(8,128)S(1)} %collective-permute-done.11.refs_3_), custom_call_target="tpu_custom_call" | custom-call | tf_op jit(solution)/shard_map/sum/pallas_call | solution.py:253
  (12 shorter events, 0.1 us)
Async XLA Ops:
  2.0 7.9 %collective-permute-start.2 = (bf16[32,1280]{1,0:T(8,128)(2,1)S(1)}, bf16[32,1280]{1,0:T(8,128)(2,1)S(1)}, u32[]{:S(2)}, u32[]{:S(2)}) collective-permute-start(bf16[32,1280]{1,0:T(8,128)(2,1)S(1)} %get-tuple-element.32), channel_id=1, source_target_pairs={{0,24},{1,25},{2,26},{3,27},{4,28},{5,29},{6,30},{7,31},{8,16},{9,... | collective-permute-start | bytes 245768 | tf_op jit(solution)/shard_map/ppermute | solution.py:139
  6.0 4.4 %collective-permute-start.1 = (bf16[32,1280]{1,0:T(8,128)(2,1)S(1)}, bf16[32,1280]{1,0:T(8,128)(2,1)S(1)}, u32[]{:S(2)}, u32[]{:S(2)}) collective-permute-start(bf16[32,1280]{1,0:T(8,128)(2,1)S(1)} %get-tuple-element.32), channel_id=1, source_target_pairs={{0,16},{1,17},{2,18},{3,19},{4,20},{5,21},{6,22},{7,23},{8,24},{9,... | collective-permute-start | bytes 245768 | tf_op jit(solution)/shard_map/ppermute | solution.py:139
  6.5 4.2 %collective-permute-start = (bf16[32,1280]{1,0:T(8,128)(2,1)S(1)}, bf16[32,1280]{1,0:T(8,128)(2,1)S(1)}, u32[]{:S(2)}, u32[]{:S(2)}) collective-permute-start(bf16[32,1280]{1,0:T(8,128)(2,1)S(1)} %get-tuple-element.32), channel_id=1, source_target_pairs={{0,12},{1,13},{2,14},{3,15},{4,8},{5,9},{6,10},{7,11},{8,4},{9,5},... | collective-permute-start | bytes 245768 | tf_op jit(solution)/shard_map/ppermute | solution.py:139
  10.7 1.7 %collective-permute-start.3 = (bf16[128,1280]{1,0:T(8,128)(2,1)S(1)}, bf16[128,1280]{1,0:T(8,128)(2,1)S(1)}, u32[]{:S(2)}, u32[]{:S(2)}) collective-permute-start(bf16[128,1280]{1,0:T(8,128)(2,1)S(1)} %constant_dynamic-update-slice_fusion.own_ref), channel_id=1, source_target_pairs={{0,4},{1,5},{2,6},{3,7},{4,0},{5,1},{6,2},{7,3},{8,12},{9,13},{10,... | collective-permute-start | bytes 983048 | tf_op jit(solution)/shard_map/ppermute | solution.py:139
  13.7 1.4 %collective-permute-start.4 = (f32[128,256]{1,0:T(8,128)S(1)}, f32[128,256]{1,0:T(8,128)S(1)}, u32[]{:S(2)}, u32[]{:S(2)}) collective-permute-start(f32[128,256]{1,0:T(8,128)S(1)} %get-tuple-element.37), channel_id=1, source_target_pairs={{0,4},{1,5},{2,6},{3,7},{4,0},{5,1},{6,2},{7,3},{8,12},{9,13},{10,... | collective-permute-start | bytes 393224 | tf_op jit(solution)/shard_map/ppermute | solution.py:139
  15.1 4.3 %collective-permute-start.7 = (f32[32,256]{1,0:T(8,128)S(1)}, f32[32,256]{1,0:T(8,128)S(1)}, u32[]{:S(2)}, u32[]{:S(2)}) collective-permute-start(f32[32,256]{1,0:T(8,128)S(1)} %get-tuple-element.44), channel_id=1, source_target_pairs={{0,28},{1,29},{2,30},{3,31},{4,24},{5,25},{6,26},{7,27},{8,20},{9,... | collective-permute-start | bytes 98312 | tf_op jit(solution)/shard_map/ppermute | solution.py:139
  17.2 3.3 %collective-permute-start.6 = (f32[32,256]{1,0:T(8,128)S(1)}, f32[32,256]{1,0:T(8,128)S(1)}, u32[]{:S(2)}, u32[]{:S(2)}) collective-permute-start(f32[32,256]{1,0:T(8,128)S(1)} %get-tuple-element.45), channel_id=1, source_target_pairs={{0,20},{1,21},{2,22},{3,23},{4,16},{5,17},{6,18},{7,19},{8,28},{9,... | collective-permute-start | bytes 98312 | tf_op jit(solution)/shard_map/ppermute | solution.py:139
  17.5 3.3 %collective-permute-start.5 = (f32[32,256]{1,0:T(8,128)S(1)}, f32[32,256]{1,0:T(8,128)S(1)}, u32[]{:S(2)}, u32[]{:S(2)}) collective-permute-start(f32[32,256]{1,0:T(8,128)S(1)} %get-tuple-element.46), channel_id=1, source_target_pairs={{0,12},{1,13},{2,14},{3,15},{4,8},{5,9},{6,10},{7,11},{8,4},{9,5},... | collective-permute-start | bytes 98312 | tf_op jit(solution)/shard_map/ppermute | solution.py:139
  20.9 5.4 %collective-permute-start.11 = (f32[32,256]{1,0:T(8,128)S(1)}, f32[32,256]{1,0:T(8,128)S(1)}, u32[]{:S(2)}, u32[]{:S(2)}) collective-permute-start(f32[32,256]{1,0:T(8,128)S(1)} %add_add_fusion), channel_id=1, source_target_pairs={{0,5},{1,6},{2,7},{3,4},{4,1},{5,2},{6,3},{7,0},{8,13},{9,14},{10,... | collective-permute-start | bytes 98312 | tf_op jit(solution)/shard_map/ppermute | solution.py:139
  22.4 4.6 %collective-permute-start.10 = (f32[32,256]{1,0:T(8,128)S(1)}, f32[32,256]{1,0:T(8,128)S(1)}, u32[]{:S(2)}, u32[]{:S(2)}) collective-permute-start(f32[32,256]{1,0:T(8,128)S(1)} %add_add_fusion), channel_id=1, source_target_pairs={{0,6},{1,7},{2,4},{3,5},{4,2},{5,3},{6,0},{7,1},{8,14},{9,15},{10,... | collective-permute-start | bytes 98312 | tf_op jit(solution)/shard_map/ppermute | solution.py:139
  24.8 3.3 %collective-permute-start.9 = (f32[32,256]{1,0:T(8,128)S(1)}, f32[32,256]{1,0:T(8,128)S(1)}, u32[]{:S(2)}, u32[]{:S(2)}) collective-permute-start(f32[32,256]{1,0:T(8,128)S(1)} %add_add_fusion), channel_id=1, source_target_pairs={{0,7},{1,4},{2,5},{3,6},{4,3},{5,0},{6,1},{7,2},{8,15},{9,12},{10,... | collective-permute-start | bytes 98312 | tf_op jit(solution)/shard_map/ppermute | solution.py:139
  26.0 2.2 %collective-permute-start.8 = (f32[32,256]{1,0:T(8,128)S(1)}, f32[32,256]{1,0:T(8,128)S(1)}, u32[]{:S(2)}, u32[]{:S(2)}) collective-permute-start(f32[32,256]{1,0:T(8,128)S(1)} %add_add_fusion), channel_id=1, source_target_pairs={{0,4},{1,5},{2,6},{3,7},{4,0},{5,1},{6,2},{7,3},{8,12},{9,13},{10,... | collective-permute-start | bytes 98312 | tf_op jit(solution)/shard_map/ppermute | solution.py:139

commit v6 on v4

--- a/solution.py
+++ b/solution.py
@@ -105,13 +105,18 @@
         residual_ref[at, :] = left
         rounded[at, :] = left.astype(BF16)
     grad = dot(kernel[...], rounded[...], ((0,), (0,)))
+    even = lax.rem(lax.axis_index("blk"), 2) == 0
     step = half // far
     for f in range(far):
-        at = f * step
-        kept_ref[at : at + each, :] = grad[half + at : half + at + each]
-        kept_ref[at + each : at + step, :] = grad[at + each : at + step]
-        sent_ref[at : at + each, :] = grad[at : at + each]
-        sent_ref[at + each : at + step, :] = grad[half + at + each : half + at + step]
+        own, first, second, last, other, third, fourth, final = (
+            grad[at + i * each : at + (i + 1) * each] for at in (f * step, half + f * step) for i in range(4)
+        )
+        kept = other, jnp.where(even, third, fourth), jnp.where(even, fourth, third), last
+        sent = own, jnp.where(even, second, first), jnp.where(even, first, second), final
+        for i in range(4):
+            at = f * step + i * each
+            kept_ref[at : at + each, :] = kept[i]
+            sent_ref[at : at + each, :] = sent[i]
 
 
 def write_kernel(source, target, sem):
@@ -129,11 +134,12 @@
 
 def send(x, sizes, flip, shift=0, step=1, size=1):
     blk, rep = sizes
+    flips = flip if isinstance(flip, tuple) else (flip, flip)
     pairs = []
     for b in range(blk):
         for r in range(rep):
             digit = r // step % size
-            pairs.append((b * rep + r, (b ^ flip) * rep + r + ((digit + shift) % size - digit) * step))
+            pairs.append((b * rep + r, (b ^ flips[b % 2]) * rep + r + ((digit + shift) % size - digit) * step))
     return lax.ppermute(x, ("blk", "rep"), pairs)
 
 
@@ -178,9 +184,13 @@
 
     chips = [[d << low for d in range(1, 1 << (high - low))] for low, high in digits(sizes[0], 1)]
     reps = digits(sizes[1], 0)
-    block = piece
-    near = [0] + chips[0]
-    parts = [block] + [to(block, flip=d) for d in near[1:]]
+    across, along, diagonal = chips[0]
+    parts = [
+        piece,
+        to(piece, flip=(across ^ 1, along ^ 1)),
+        to(piece, flip=(along ^ 1, across ^ 1)),
+        to(piece, flip=diagonal),
+    ]
     points, point_norm, goals = pl.pallas_call(
         points_kernel,
         out_shape=(
@@ -206,7 +216,7 @@
     for group in chips[1:]:
         block = jnp.concatenate([block] + [to(block, flip=d) for d in group], axis=0)
     half = block.shape[0]
-    far = half // (len(near) * each)
+    far = half // (len(parts) * each)
     residual, kept, sent = pl.pallas_call(
         functools.partial(residual_kernel, far, each),
         out_shape=(
@@ -226,13 +236,13 @@
         name="residual",
     )(points, point_norm, goals, block, to(block, flip=1))
 
-    total = (kept + to(sent, flip=1)).reshape(far, len(near), each, outs)
+    total = (kept + to(sent, flip=1)).reshape(far, len(parts), each, outs)
     for group in reversed(chips[1:]):
         low = total.shape[0] // (len(group) + 1)
         blocks = [total[i * low : (i + 1) * low] for i in range(len(group) + 1)]
         total = pair_sum(blocks[:1] + [to(x, flip=d) for x, d in zip(blocks[1:], group)])
-    rows = {d: total[0, i] for i, d in enumerate(near)}
-    parts = [rows[0]] + [to(rows[d], flip=d ^ 1) for d in chips[0]]
+    mine, *others = total[0]
+    parts = [mine] + [to(x, flip=d ^ 1) for x, d in zip(others, chips[0])]
     residual = pl.pallas_call(
         write_kernel,
         out_shape=jax.ShapeDtypeStruct(residual.shape, F32),

time: 29.1 us -> 29 us (level)
  waiting for transfers between devices: 7.18 us -> 5.94 us
  starting transfers between devices: 13.3 us -> 14.4 us
    ppermute x12, waiting for transfers between devices: 7.18 us -> 5.94 us  [send(): return lax.ppermute(x, ('blk', 'rep'), pairs)]
    ppermute x12, starting transfers between devices: 13.3 us -> 14.4 us  [send(): return lax.ppermute(x, ('blk', 'rep'), pairs)]
  transfers between devices with their start and end apart: 12 -> 12, of which waited for: 9 -> 7; matrix products, arithmetic and copies ran while one was open for 0% -> 0% of each run, Pallas kernels for 15% -> 15%
where the time goes in v6:
time: 29 us; the launch traced here: 28.8 us
  starting transfers between devices  14.4 us (50%)
  Pallas kernels  7.64 us (26%)
  waiting for transfers between devices  5.94 us (20%)
  between operations  0.75 us (3%)
    ppermute x12, starting transfers between devices, send(): return lax.ppermute(x, ('blk', 'rep'), pairs)  14.4 us
    ppermute x12, waiting for transfers between devices, send(): return lax.ppermute(x, ('blk', 'rep'), pairs)  5.94 us
    pallas_call x1, Pallas kernels, per_device(): pl.pallas_call(points_kernel, out_shape=(pltpu.VMEM((count, width), BF16)...  3.42 us
    pallas_call x1, Pallas kernels, per_device(): pl.pallas_call(piece_kernel, out_shape=(pltpu.VMEM((each, width + outs),...  1.37 us
    pallas_call x1, Pallas kernels, per_device(): pl.pallas_call(functools.partial(residual_kernel, far, each), out_shape=(...  1.24 us
    pallas_call x1, Pallas kernels, per_device(): pl.pallas_call(write_kernel, out_shape=jax.ShapeDtypeStruct(residual.shap...  0.99 us
    pallas_call x1, Pallas kernels, per_device(): pl.pallas_call(sum_kernel, out_shape=jax.ShapeDtypeStruct(mine.shape, F32...  0.62 us
  transfers between devices with their start and end apart: 12, of which 7 were waited for; matrix products, arithmetic and copies ran while one was open for 0% of the time, Pallas kernels for 15%

profile of v6, /device:TPU:0, one launch (start us, length us, event | category | flops | bytes accessed | tf_op | source)
XLA Modules:
  0.0 28.8 jit_solution(6881247931076672862)
XLA Ops:
  0.6 1.4 %piece.1 = (bf16[32,1280]{1,0:T(8,128)(2,1)S(1)}, s32[8,128]{1,0:T(8,128)S(1)}, bf16[512,1024]{1,0:T(8,128)(2,1)S(1)}) custom-call(s32[1,32]{1,0:T(1,128)} %bitcast.3, bf16[64,1024]{1,0:T(8,128)(2,1)} %centers_hbm.1, bf16[32,256]{1,0:T(8,128)(2,1)} %coefs_hbm.1, s32[8,128]{1,0:T(8,128)} %bitcast.2, bf16[1280,1024]{1,0:T(8,128)(2,1)} %pool_hbm.3), custom_call_target="tpu_custom_call" | custom-call | tf_op jit(solution)/shard_map/piece/pallas_call | solution.py:166
  2.0 4.0 %collective-permute-start.2 = (bf16[32,1280]{1,0:T(8,128)(2,1)S(1)}, bf16[32,1280]{1,0:T(8,128)(2,1)S(1)}, u32[]{:S(2)}, u32[]{:S(2)}) collective-permute-start(bf16[32,1280]{1,0:T(8,128)(2,1)S(1)} %get-tuple-element.32), channel_id=1, source_target_pairs={{0,24},{1,25},{2,26},{3,27},{4,28},{5,29},{6,30},{7,31},{8,16},{9,... | collective-permute-start | bytes 245768 | tf_op jit(solution)/shard_map/ppermute | solution.py:143
  6.0 0.0 collective-permute-start.1
  6.0 1.7 %collective-permute-start = (bf16[32,1280]{1,0:T(8,128)(2,1)S(1)}, bf16[32,1280]{1,0:T(8,128)(2,1)S(1)}, u32[]{:S(2)}, u32[]{:S(2)}) collective-permute-start(bf16[32,1280]{1,0:T(8,128)(2,1)S(1)} %get-tuple-element.32), channel_id=1, source_target_pairs={{0,12},{1,13},{2,14},{3,15},{4,16},{5,17},{6,18},{7,19},{8,4},{9,5... | collective-permute-start | bytes 245768 | tf_op jit(solution)/shard_map/ppermute | solution.py:143
  7.7 3.4 %points.1 = (bf16[1024,1024]{1,0:T(8,128)(2,1)S(1)}, f32[1024,1]{1,0:T(8,128)S(1)}, bf16[1024,256]{1,0:T(8,128)(2,1)S(1)}) custom-call(s32[8,128]{1,0:T(8,128)S(1)} %get-tuple-element.24.rows_ref, bf16[512,1024]{1,0:T(8,128)(2,1)S(1)} %get-tuple-element.25.first_ref, bf16[1280,1024]{1,0:T(8,128)(2,1)} %pool_hbm.3, bf16[1024,256]{1,0:T(8,128)(2,1)} %targets_hbm.1), custom_call_target="tpu_custom_call" | custom-call | flops 2147483648 | bytes 5242880 | tf_op jit(solution)/shard_map/points/pallas_call | solution.py:194
  11.2 0.1 collective-permute-start.3
  11.3 1.6 %collective-permute-done.3.other_ref = bf16[128,1280]{1,0:T(8,128)(2,1)S(1)} collective-permute-done((bf16[128,1280]{1,0:T(8,128)(2,1)S(1)}, bf16[128,1280]{1,0:T(8,128)(2,1)S(1)}, u32[]{:S(2)}, u32[]{:S(2)}) %collective-permute-start.3) | collective-permute-done | bytes 327712 | tf_op jit(solution)/shard_map/ppermute | solution.py:143
  12.9 1.2 %residual.1 = (f32[1024,256]{1,0:T(8,128)S(1)}, f32[128,256]{1,0:T(8,128)S(1)}, f32[128,256]{1,0:T(8,128)S(1)}) custom-call(bf16[1024,1024]{1,0:T(8,128)(2,1)S(1)} %get-tuple-element.29.points_ref, f32[1024,1]{1,0:T(8,128)S(1)} %get-tuple-element.30.norm_ref, bf16[1024,256]{1,0:T(8,128)(2,1)S(1)} %get-tuple-element.31.targets_ref, ...), custom_call_target="tpu_custom_call" | custom-call | tf_op jit(solution)/shard_map/residual/pallas_call | solution.py:220
  14.2 0.2 collective-permute-start.4
  14.4 1.2 %collective-permute-done.4 = f32[128,256]{1,0:T(8,128)S(1)} collective-permute-done((f32[128,256]{1,0:T(8,128)S(1)}, f32[128,256]{1,0:T(8,128)S(1)}, u32[]{:S(2)}, u32[]{:S(2)}) %collective-permute-start.4) | collective-permute-done | bytes 131104 | tf_op jit(solution)/shard_map/ppermute | solution.py:143
  15.6 1.4 %collective-permute-start.7 = (f32[32,256]{1,0:T(8,128)S(1)}, f32[32,256]{1,0:T(8,128)S(1)}, u32[]{:S(2)}, u32[]{:S(2)}) collective-permute-start(f32[32,256]{1,0:T(8,128)S(1)} %get-tuple-element.44), channel_id=1, source_target_pairs={{0,28},{1,29},{2,30},{3,31},{4,24},{5,25},{6,26},{7,27},{8,20},{9,... | collective-permute-start | bytes 98312 | tf_op jit(solution)/shard_map/ppermute | solution.py:143
  17.1 0.5 %collective-permute-start.6 = (f32[32,256]{1,0:T(8,128)S(1)}, f32[32,256]{1,0:T(8,128)S(1)}, u32[]{:S(2)}, u32[]{:S(2)}) collective-permute-start(f32[32,256]{1,0:T(8,128)S(1)} %get-tuple-element.45), channel_id=1, source_target_pairs={{0,20},{1,21},{2,22},{3,23},{4,16},{5,17},{6,18},{7,19},{8,28},{9,... | collective-permute-start | bytes 98312 | tf_op jit(solution)/shard_map/ppermute | solution.py:143
  17.6 1.1 %collective-permute-start.5 = (f32[32,256]{1,0:T(8,128)S(1)}, f32[32,256]{1,0:T(8,128)S(1)}, u32[]{:S(2)}, u32[]{:S(2)}) collective-permute-start(f32[32,256]{1,0:T(8,128)S(1)} %get-tuple-element.46), channel_id=1, source_target_pairs={{0,12},{1,13},{2,14},{3,15},{4,8},{5,9},{6,10},{7,11},{8,4},{9,5},... | collective-permute-start | bytes 98312 | tf_op jit(solution)/shard_map/ppermute | solution.py:143
  18.7 1.0 %write.1 = f32[1024,256]{1,0:T(8,128)} custom-call(f32[1024,256]{1,0:T(8,128)S(1)} %get-tuple-element.38.source), custom_call_target="tpu_custom_call" | custom-call | bytes 4194304 | tf_op jit(solution)/shard_map/write/pallas_call | solution.py:246
  19.7 0.3 collective-permute-done.7
  20.0 0.7 %collective-permute-done.6 = f32[32,256]{1,0:T(8,128)S(1)} collective-permute-done((f32[32,256]{1,0:T(8,128)S(1)}, f32[32,256]{1,0:T(8,128)S(1)}, u32[]{:S(2)}, u32[]{:S(2)}) %collective-permute-start.6) | collective-permute-done | bytes 32800 | tf_op jit(solution)/shard_map/ppermute | solution.py:143
  20.7 0.2 collective-permute-done.5
  20.9 1.4 %collective-permute-start.11 = (f32[32,256]{1,0:T(8,128)S(1)}, f32[32,256]{1,0:T(8,128)S(1)}, u32[]{:S(2)}, u32[]{:S(2)}) collective-permute-start(f32[32,256]{1,0:T(8,128)S(1)} %add_add_fusion), channel_id=1, source_target_pairs={{0,5},{1,6},{2,7},{3,4},{4,1},{5,2},{6,3},{7,0},{8,13},{9,14},{10,... | collective-permute-start | bytes 98312 | tf_op jit(solution)/shard_map/ppermute | solution.py:143
  22.3 2.5 %collective-permute-start.10 = (f32[32,256]{1,0:T(8,128)S(1)}, f32[32,256]{1,0:T(8,128)S(1)}, u32[]{:S(2)}, u32[]{:S(2)}) collective-permute-start(f32[32,256]{1,0:T(8,128)S(1)} %add_add_fusion), channel_id=1, source_target_pairs={{0,6},{1,7},{2,4},{3,5},{4,2},{5,3},{6,0},{7,1},{8,14},{9,15},{10,... | collective-permute-start | bytes 98312 | tf_op jit(solution)/shard_map/ppermute | solution.py:143
  24.9 1.1 %collective-permute-start.9 = (f32[32,256]{1,0:T(8,128)S(1)}, f32[32,256]{1,0:T(8,128)S(1)}, u32[]{:S(2)}, u32[]{:S(2)}) collective-permute-start(f32[32,256]{1,0:T(8,128)S(1)} %add_add_fusion), channel_id=1, source_target_pairs={{0,7},{1,4},{2,5},{3,6},{4,3},{5,0},{6,1},{7,2},{8,15},{9,12},{10,... | collective-permute-start | bytes 98312 | tf_op jit(solution)/shard_map/ppermute | solution.py:143
  26.0 0.3 %collective-permute-start.8 = (f32[32,256]{1,0:T(8,128)S(1)}, f32[32,256]{1,0:T(8,128)S(1)}, u32[]{:S(2)}, u32[]{:S(2)}) collective-permute-start(f32[32,256]{1,0:T(8,128)S(1)} %add_add_fusion), channel_id=1, source_target_pairs={{0,4},{1,5},{2,6},{3,7},{4,0},{5,1},{6,2},{7,3},{8,12},{9,13},{10,... | collective-permute-start | bytes 98312 | tf_op jit(solution)/shard_map/ppermute | solution.py:143
  26.3 0.6 %collective-permute-done.10.refs_2_ = f32[32,256]{1,0:T(8,128)S(1)} collective-permute-done((f32[32,256]{1,0:T(8,128)S(1)}, f32[32,256]{1,0:T(8,128)S(1)}, u32[]{:S(2)}, u32[]{:S(2)}) %collective-permute-start.10) | collective-permute-done | bytes 32800 | tf_op jit(solution)/shard_map/ppermute | solution.py:143
  26.9 1.3 %collective-permute-done.9.refs_1_ = f32[32,256]{1,0:T(8,128)S(1)} collective-permute-done((f32[32,256]{1,0:T(8,128)S(1)}, f32[32,256]{1,0:T(8,128)S(1)}, u32[]{:S(2)}, u32[]{:S(2)}) %collective-permute-start.9) | collective-permute-done | bytes 32800 | tf_op jit(solution)/shard_map/ppermute | solution.py:143
  28.2 0.6 %sum.1 = f32[32,256]{1,0:T(8,128)} custom-call(f32[32,256]{1,0:T(8,128)S(1)} %collective-permute-done.8.refs_0_, f32[32,256]{1,0:T(8,128)S(1)} %collective-permute-done.9.refs_1_, f32[32,256]{1,0:T(8,128)S(1)} %collective-permute-done.10.refs_2_, f32[32,256]{1,0:T(8,128)S(1)} %collective-permute-done.11.refs_3_), custom_call_target="tpu_custom_call" | custom-call | tf_op jit(solution)/shard_map/sum/pallas_call | solution.py:262
  (12 shorter events, 0.1 us)
Async XLA Ops:
  2.0 9.1 %collective-permute-start.2 = (bf16[32,1280]{1,0:T(8,128)(2,1)S(1)}, bf16[32,1280]{1,0:T(8,128)(2,1)S(1)}, u32[]{:S(2)}, u32[]{:S(2)}) collective-permute-start(bf16[32,1280]{1,0:T(8,128)(2,1)S(1)} %get-tuple-element.32), channel_id=1, source_target_pairs={{0,24},{1,25},{2,26},{3,27},{4,28},{5,29},{6,30},{7,31},{8,16},{9,... | collective-permute-start | bytes 245768 | tf_op jit(solution)/shard_map/ppermute | solution.py:143
  6.0 5.2 %collective-permute-start.1 = (bf16[32,1280]{1,0:T(8,128)(2,1)S(1)}, bf16[32,1280]{1,0:T(8,128)(2,1)S(1)}, u32[]{:S(2)}, u32[]{:S(2)}) collective-permute-start(bf16[32,1280]{1,0:T(8,128)(2,1)S(1)} %get-tuple-element.32), channel_id=1, source_target_pairs={{0,20},{1,21},{2,22},{3,23},{4,8},{5,9},{6,10},{7,11},{8,28},{9,29... | collective-permute-start | bytes 245768 | tf_op jit(solution)/shard_map/ppermute | solution.py:143
  6.0 5.2 %collective-permute-start = (bf16[32,1280]{1,0:T(8,128)(2,1)S(1)}, bf16[32,1280]{1,0:T(8,128)(2,1)S(1)}, u32[]{:S(2)}, u32[]{:S(2)}) collective-permute-start(bf16[32,1280]{1,0:T(8,128)(2,1)S(1)} %get-tuple-element.32), channel_id=1, source_target_pairs={{0,12},{1,13},{2,14},{3,15},{4,16},{5,17},{6,18},{7,19},{8,4},{9,5... | collective-permute-start | bytes 245768 | tf_op jit(solution)/shard_map/ppermute | solution.py:143
  11.2 1.7 %collective-permute-start.3 = (bf16[128,1280]{1,0:T(8,128)(2,1)S(1)}, bf16[128,1280]{1,0:T(8,128)(2,1)S(1)}, u32[]{:S(2)}, u32[]{:S(2)}) collective-permute-start(bf16[128,1280]{1,0:T(8,128)(2,1)S(1)} %constant_dynamic-update-slice_fusion.own_ref), channel_id=1, source_target_pairs={{0,4},{1,5},{2,6},{3,7},{4,0},{5,1},{6,2},{7,3},{8,12},{9,13},{10,... | collective-permute-start | bytes 983048 | tf_op jit(solution)/shard_map/ppermute | solution.py:143
  14.2 1.4 %collective-permute-start.4 = (f32[128,256]{1,0:T(8,128)S(1)}, f32[128,256]{1,0:T(8,128)S(1)}, u32[]{:S(2)}, u32[]{:S(2)}) collective-permute-start(f32[128,256]{1,0:T(8,128)S(1)} %get-tuple-element.37), channel_id=1, source_target_pairs={{0,4},{1,5},{2,6},{3,7},{4,0},{5,1},{6,2},{7,3},{8,12},{9,13},{10,... | collective-permute-start | bytes 393224 | tf_op jit(solution)/shard_map/ppermute | solution.py:143
  15.6 4.3 %collective-permute-start.7 = (f32[32,256]{1,0:T(8,128)S(1)}, f32[32,256]{1,0:T(8,128)S(1)}, u32[]{:S(2)}, u32[]{:S(2)}) collective-permute-start(f32[32,256]{1,0:T(8,128)S(1)} %get-tuple-element.44), channel_id=1, source_target_pairs={{0,28},{1,29},{2,30},{3,31},{4,24},{5,25},{6,26},{7,27},{8,20},{9,... | collective-permute-start | bytes 98312 | tf_op jit(solution)/shard_map/ppermute | solution.py:143
  17.1 3.6 %collective-permute-start.6 = (f32[32,256]{1,0:T(8,128)S(1)}, f32[32,256]{1,0:T(8,128)S(1)}, u32[]{:S(2)}, u32[]{:S(2)}) collective-permute-start(f32[32,256]{1,0:T(8,128)S(1)} %get-tuple-element.45), channel_id=1, source_target_pairs={{0,20},{1,21},{2,22},{3,23},{4,16},{5,17},{6,18},{7,19},{8,28},{9,... | collective-permute-start | bytes 98312 | tf_op jit(solution)/shard_map/ppermute | solution.py:143
  17.6 3.3 %collective-permute-start.5 = (f32[32,256]{1,0:T(8,128)S(1)}, f32[32,256]{1,0:T(8,128)S(1)}, u32[]{:S(2)}, u32[]{:S(2)}) collective-permute-start(f32[32,256]{1,0:T(8,128)S(1)} %get-tuple-element.46), channel_id=1, source_target_pairs={{0,12},{1,13},{2,14},{3,15},{4,8},{5,9},{6,10},{7,11},{8,4},{9,5},... | collective-permute-start | bytes 98312 | tf_op jit(solution)/shard_map/ppermute | solution.py:143
  20.9 5.4 %collective-permute-start.11 = (f32[32,256]{1,0:T(8,128)S(1)}, f32[32,256]{1,0:T(8,128)S(1)}, u32[]{:S(2)}, u32[]{:S(2)}) collective-permute-start(f32[32,256]{1,0:T(8,128)S(1)} %add_add_fusion), channel_id=1, source_target_pairs={{0,5},{1,6},{2,7},{3,4},{4,1},{5,2},{6,3},{7,0},{8,13},{9,14},{10,... | collective-permute-start | bytes 98312 | tf_op jit(solution)/shard_map/ppermute | solution.py:143
  22.3 4.6 %collective-permute-start.10 = (f32[32,256]{1,0:T(8,128)S(1)}, f32[32,256]{1,0:T(8,128)S(1)}, u32[]{:S(2)}, u32[]{:S(2)}) collective-permute-start(f32[32,256]{1,0:T(8,128)S(1)} %add_add_fusion), channel_id=1, source_target_pairs={{0,6},{1,7},{2,4},{3,5},{4,2},{5,3},{6,0},{7,1},{8,14},{9,15},{10,... | collective-permute-start | bytes 98312 | tf_op jit(solution)/shard_map/ppermute | solution.py:143
  24.9 3.3 %collective-permute-start.9 = (f32[32,256]{1,0:T(8,128)S(1)}, f32[32,256]{1,0:T(8,128)S(1)}, u32[]{:S(2)}, u32[]{:S(2)}) collective-permute-start(f32[32,256]{1,0:T(8,128)S(1)} %add_add_fusion), channel_id=1, source_target_pairs={{0,7},{1,4},{2,5},{3,6},{4,3},{5,0},{6,1},{7,2},{8,15},{9,12},{10,... | collective-permute-start | bytes 98312 | tf_op jit(solution)/shard_map/ppermute | solution.py:143
  26.0 2.2 %collective-permute-start.8 = (f32[32,256]{1,0:T(8,128)S(1)}, f32[32,256]{1,0:T(8,128)S(1)}, u32[]{:S(2)}, u32[]{:S(2)}) collective-permute-start(f32[32,256]{1,0:T(8,128)S(1)} %add_add_fusion), channel_id=1, source_target_pairs={{0,4},{1,5},{2,6},{3,7},{4,0},{5,1},{6,2},{7,3},{8,12},{9,13},{10,... | collective-permute-start | bytes 98312 | tf_op jit(solution)/shard_map/ppermute | solution.py:143

commit v7 on v6

--- a/solution.py
+++ b/solution.py
@@ -82,12 +82,16 @@
         copy.wait()
 
 
-def residual_kernel(far, each, points_ref, norm_ref, targets_ref, own_ref, other_ref, residual_ref, kept_ref, sent_ref, centers, coefs, kernel, rounded):
-    half = own_ref.shape[0]
+def residual_kernel(far, each, blocks, points_ref, norm_ref, targets_ref, *refs):
+    residual_ref, kept_ref, sent_ref, centers, coefs, kernel, rounded = refs[blocks:]
+    half = kept_ref.shape[0]
     count, width = points_ref.shape
-    for i, ref in enumerate((own_ref, other_ref)):
-        centers[i * half : (i + 1) * half, :] = ref[:, :width]
-        coefs[i * half : (i + 1) * half, :] = ref[:, width:]
+    start = 0
+    for ref in refs[:blocks]:
+        at = slice(start, start + ref.shape[0])
+        centers[at, :] = ref[:, :width]
+        coefs[at, :] = ref[:, width:]
+        start += ref.shape[0]
     squares = jnp.zeros((2 * half, 128), F32)
     for g in range(width // 128):
         part = centers[:, g * 128 : (g + 1) * 128].astype(F32)
@@ -191,6 +195,7 @@
         to(piece, flip=(along ^ 1, across ^ 1)),
         to(piece, flip=diagonal),
     ]
+    other = to(piece, flip=1)
     points, point_norm, goals = pl.pallas_call(
         points_kernel,
         out_shape=(
@@ -211,20 +216,25 @@
         cost_estimate=pl.CostEstimate(flops=2 << 30, bytes_accessed=5 << 20, transcendentals=0),
         name="points",
     )(rows, resident, pool, in_hbm(targets))
-    parts, points, point_norm, goals = lax.optimization_barrier((parts, points, point_norm, goals))
-    block = jnp.concatenate(parts, axis=0)
+    other, parts, points, point_norm, goals = lax.optimization_barrier((other, parts, points, point_norm, goals))
+    own = [parts[0], jnp.concatenate(parts[1:], axis=0)]
+    others = [other, to(own[1], flip=1)]
     for group in chips[1:]:
-        block = jnp.concatenate([block] + [to(block, flip=d) for d in group], axis=0)
-    half = block.shape[0]
+        own, others = (
+            [jnp.concatenate(blocks + [to(block, flip=d) for d in group for block in blocks], axis=0)]
+            for blocks in (own, others)
+        )
+    blocks = own + others
+    half = sum(block.shape[0] for block in own)
     far = half // (len(parts) * each)
     residual, kept, sent = pl.pallas_call(
-        functools.partial(residual_kernel, far, each),
+        functools.partial(residual_kernel, far, each, len(blocks)),
         out_shape=(
             pltpu.VMEM((count, outs), F32),
             pltpu.VMEM((half, outs), F32),
             pltpu.VMEM((half, outs), F32),
         ),
-        in_specs=[VMEM] * 5,
+        in_specs=[VMEM] * (3 + len(blocks)),
         out_specs=(VMEM,) * 3,
         scratch_shapes=[
             pltpu.VMEM((2 * half, width), BF16),
@@ -234,7 +244,7 @@
         ],
         compiler_params=pltpu.CompilerParams(vmem_limit_bytes=32 << 20),
         name="residual",
-    )(points, point_norm, goals, block, to(block, flip=1))
+    )(points, point_norm, goals, *blocks)
 
     total = (kept + to(sent, flip=1)).reshape(far, len(parts), each, outs)
     for group in reversed(chips[1:]):

time: 29 us -> 28.9 us (level)
  waiting for transfers between devices: 5.94 us -> 4.93 us
  starting transfers between devices: 14.4 us -> 15.4 us
    ppermute x12 -> x13, waiting for transfers between devices: 5.94 us -> 4.93 us  [send(): return lax.ppermute(x, ('blk', 'rep'), pairs)]
    ppermute x12 -> x13, starting transfers between devices: 14.4 us -> 15.4 us  [send(): return lax.ppermute(x, ('blk', 'rep'), pairs)]
  transfers between devices with their start and end apart: 12 -> 13, of which waited for: 7 -> 6; matrix products, arithmetic and copies ran while one was open for 0% -> 0% of each run, Pallas kernels for 15% -> 15%
where the time goes in v7:
time: 28.9 us; the launch traced here: 28.7 us
  starting transfers between devices  15.4 us (53%)
  Pallas kernels  7.63 us (26%)
  waiting for transfers between devices  4.93 us (17%)
  between operations  0.74 us (3%)
    ppermute x13, starting transfers between devices, send(): return lax.ppermute(x, ('blk', 'rep'), pairs)  15.4 us
    ppermute x13, waiting for transfers between devices, send(): return lax.ppermute(x, ('blk', 'rep'), pairs)  4.93 us
    pallas_call x1, Pallas kernels, per_device(): pl.pallas_call(points_kernel, out_shape=(pltpu.VMEM((count, width), BF16)...  3.41 us
    pallas_call x1, Pallas kernels, per_device(): pl.pallas_call(piece_kernel, out_shape=(pltpu.VMEM((each, width + outs),...  1.37 us
    pallas_call x1, Pallas kernels, per_device(): pl.pallas_call(functools.partial(residual_kernel, far, each, len(blocks))...  1.23 us
    pallas_call x1, Pallas kernels, per_device(): pl.pallas_call(write_kernel, out_shape=jax.ShapeDtypeStruct(residual.shap...  0.99 us
    pallas_call x1, Pallas kernels, per_device(): pl.pallas_call(sum_kernel, out_shape=jax.ShapeDtypeStruct(mine.shape, F32...  0.62 us
  transfers between devices with their start and end apart: 13, of which 6 were waited for; matrix products, arithmetic and copies ran while one was open for 0% of the time, Pallas kernels for 15%

profile of v7, /device:TPU:0, one launch (start us, length us, event | category | flops | bytes accessed | tf_op | source)
XLA Modules:
  0.0 28.7 jit_solution(2651153273852673864)
XLA Ops:
  0.6 1.4 %piece.1 = (bf16[32,1280]{1,0:T(8,128)(2,1)S(1)}, s32[8,128]{1,0:T(8,128)S(1)}, bf16[512,1024]{1,0:T(8,128)(2,1)S(1)}) custom-call(s32[1,32]{1,0:T(1,128)} %bitcast.3, bf16[64,1024]{1,0:T(8,128)(2,1)} %centers_hbm.1, bf16[32,256]{1,0:T(8,128)(2,1)} %coefs_hbm.1, s32[8,128]{1,0:T(8,128)} %bitcast.2, bf16[1280,1024]{1,0:T(8,128)(2,1)} %pool_hbm.3), custom_call_target="tpu_custom_call" | custom-call | tf_op jit(solution)/shard_map/piece/pallas_call | solution.py:170
  2.0 4.0 %collective-permute-start.3 = (bf16[32,1280]{1,0:T(8,128)(2,1)S(1)}, bf16[32,1280]{1,0:T(8,128)(2,1)S(1)}, u32[]{:S(2)}, u32[]{:S(2)}) collective-permute-start(bf16[32,1280]{1,0:T(8,128)(2,1)S(1)} %get-tuple-element.33.refs_0_), channel_id=1, source_target_pairs={{0,24},{1,25},{2,26},{3,27},{4,28},{5,29},{6,30},{7,31},{8,16},{9,... | collective-permute-start | bytes 245768 | tf_op jit(solution)/shard_map/ppermute | solution.py:147
  6.0 1.7 %collective-permute-start.1 = (bf16[32,1280]{1,0:T(8,128)(2,1)S(1)}, bf16[32,1280]{1,0:T(8,128)(2,1)S(1)}, u32[]{:S(2)}, u32[]{:S(2)}) collective-permute-start(bf16[32,1280]{1,0:T(8,128)(2,1)S(1)} %get-tuple-element.33.refs_0_), channel_id=1, source_target_pairs={{0,12},{1,13},{2,14},{3,15},{4,16},{5,17},{6,18},{7,19},{8,4},{9,5... | collective-permute-start | bytes 245768 | tf_op jit(solution)/shard_map/ppermute | solution.py:147
  7.7 3.4 %points.1 = (bf16[1024,1024]{1,0:T(8,128)(2,1)S(1)}, f32[1024,1]{1,0:T(8,128)S(1)}, bf16[1024,256]{1,0:T(8,128)(2,1)S(1)}) custom-call(s32[8,128]{1,0:T(8,128)S(1)} %get-tuple-element.25.rows_ref, bf16[512,1024]{1,0:T(8,128)(2,1)S(1)} %get-tuple-element.26.first_ref, bf16[1280,1024]{1,0:T(8,128)(2,1)} %pool_hbm.3, bf16[1024,256]{1,0:T(8,128)(2,1)} %targets_hbm.1), custom_call_target="tpu_custom_call" | custom-call | flops 2147483648 | bytes 5242880 | tf_op jit(solution)/shard_map/points/pallas_call | solution.py:199
  11.2 0.0 collective-permute-done.1
  11.2 0.0 collective-permute-done.refs_2_
  11.2 0.6 %collective-permute-start.4 = (bf16[96,1280]{1,0:T(8,128)(2,1)S(1)}, bf16[96,1280]{1,0:T(8,128)(2,1)S(1)}, u32[]{:S(2)}, u32[]{:S(2)}) collective-permute-start(bf16[96,1280]{1,0:T(8,128)(2,1)S(1)} %constant_dynamic-update-slice_fusion.refs_1_), channel_id=1, source_target_pairs={{0,4},{1,5},{2,6},{3,7},{4,0},{5,1},{6,2},{7,3},{8,12},{9,13},{10,... | collective-permute-start | bytes 737288 | tf_op jit(solution)/shard_map/ppermute | solution.py:147
  11.8 1.1 %collective-permute-done.4.refs_3_ = bf16[96,1280]{1,0:T(8,128)(2,1)S(1)} collective-permute-done((bf16[96,1280]{1,0:T(8,128)(2,1)S(1)}, bf16[96,1280]{1,0:T(8,128)(2,1)S(1)}, u32[]{:S(2)}, u32[]{:S(2)}) %collective-permute-start.4) | collective-permute-done | bytes 245792 | tf_op jit(solution)/shard_map/ppermute | solution.py:147
  12.9 1.2 %residual.1 = (f32[1024,256]{1,0:T(8,128)S(1)}, f32[128,256]{1,0:T(8,128)S(1)}, f32[128,256]{1,0:T(8,128)S(1)}) custom-call(bf16[1024,1024]{1,0:T(8,128)(2,1)S(1)} %get-tuple-element.30.points_ref, f32[1024,1]{1,0:T(8,128)S(1)} %get-tuple-element.31.norm_ref, bf16[1024,256]{1,0:T(8,128)(2,1)S(1)} %get-tuple-element.32.targets_ref, ...), custom_call_target="tpu_custom_call" | custom-call | tf_op jit(solution)/shard_map/residual/pallas_call | solution.py:230
  14.2 0.4 %collective-permute-start.5 = (f32[128,256]{1,0:T(8,128)S(1)}, f32[128,256]{1,0:T(8,128)S(1)}, u32[]{:S(2)}, u32[]{:S(2)}) collective-permute-start(f32[128,256]{1,0:T(8,128)S(1)} %get-tuple-element.39), channel_id=1, source_target_pairs={{0,4},{1,5},{2,6},{3,7},{4,0},{5,1},{6,2},{7,3},{8,12},{9,13},{10,... | collective-permute-start | bytes 393224 | tf_op jit(solution)/shard_map/ppermute | solution.py:147
  14.6 1.0 %collective-permute-done.5 = f32[128,256]{1,0:T(8,128)S(1)} collective-permute-done((f32[128,256]{1,0:T(8,128)S(1)}, f32[128,256]{1,0:T(8,128)S(1)}, u32[]{:S(2)}, u32[]{:S(2)}) %collective-permute-start.5) | collective-permute-done | bytes 131104 | tf_op jit(solution)/shard_map/ppermute | solution.py:147
  15.6 1.3 %collective-permute-start.8 = (f32[32,256]{1,0:T(8,128)S(1)}, f32[32,256]{1,0:T(8,128)S(1)}, u32[]{:S(2)}, u32[]{:S(2)}) collective-permute-start(f32[32,256]{1,0:T(8,128)S(1)} %get-tuple-element.46), channel_id=1, source_target_pairs={{0,28},{1,29},{2,30},{3,31},{4,24},{5,25},{6,26},{7,27},{8,20},{9,... | collective-permute-start | bytes 98312 | tf_op jit(solution)/shard_map/ppermute | solution.py:147
  16.9 0.5 %collective-permute-start.7 = (f32[32,256]{1,0:T(8,128)S(1)}, f32[32,256]{1,0:T(8,128)S(1)}, u32[]{:S(2)}, u32[]{:S(2)}) collective-permute-start(f32[32,256]{1,0:T(8,128)S(1)} %get-tuple-element.47), channel_id=1, source_target_pairs={{0,20},{1,21},{2,22},{3,23},{4,16},{5,17},{6,18},{7,19},{8,28},{9,... | collective-permute-start | bytes 98312 | tf_op jit(solution)/shard_map/ppermute | solution.py:147
  17.4 1.4 %collective-permute-start.6 = (f32[32,256]{1,0:T(8,128)S(1)}, f32[32,256]{1,0:T(8,128)S(1)}, u32[]{:S(2)}, u32[]{:S(2)}) collective-permute-start(f32[32,256]{1,0:T(8,128)S(1)} %get-tuple-element.48), channel_id=1, source_target_pairs={{0,12},{1,13},{2,14},{3,15},{4,8},{5,9},{6,10},{7,11},{8,4},{9,5},... | collective-permute-start | bytes 98312 | tf_op jit(solution)/shard_map/ppermute | solution.py:147
  18.9 1.0 %write.1 = f32[1024,256]{1,0:T(8,128)} custom-call(f32[1024,256]{1,0:T(8,128)S(1)} %get-tuple-element.40.source), custom_call_target="tpu_custom_call" | custom-call | bytes 4194304 | tf_op jit(solution)/shard_map/write/pallas_call | solution.py:256
  19.9 0.1 collective-permute-done.8
  20.0 0.8 %collective-permute-done.7 = f32[32,256]{1,0:T(8,128)S(1)} collective-permute-done((f32[32,256]{1,0:T(8,128)S(1)}, f32[32,256]{1,0:T(8,128)S(1)}, u32[]{:S(2)}, u32[]{:S(2)}) %collective-permute-start.7) | collective-permute-done | bytes 32800 | tf_op jit(solution)/shard_map/ppermute | solution.py:147
  20.8 1.6 %collective-permute-start.12 = (f32[32,256]{1,0:T(8,128)S(1)}, f32[32,256]{1,0:T(8,128)S(1)}, u32[]{:S(2)}, u32[]{:S(2)}) collective-permute-start(f32[32,256]{1,0:T(8,128)S(1)} %add_add_fusion), channel_id=1, source_target_pairs={{0,5},{1,6},{2,7},{3,4},{4,1},{5,2},{6,3},{7,0},{8,13},{9,14},{10,... | collective-permute-start | bytes 98312 | tf_op jit(solution)/shard_map/ppermute | solution.py:147
  22.4 2.4 %collective-permute-start.11 = (f32[32,256]{1,0:T(8,128)S(1)}, f32[32,256]{1,0:T(8,128)S(1)}, u32[]{:S(2)}, u32[]{:S(2)}) collective-permute-start(f32[32,256]{1,0:T(8,128)S(1)} %add_add_fusion), channel_id=1, source_target_pairs={{0,6},{1,7},{2,4},{3,5},{4,2},{5,3},{6,0},{7,1},{8,14},{9,15},{10,... | collective-permute-start | bytes 98312 | tf_op jit(solution)/shard_map/ppermute | solution.py:147
  24.8 1.3 %collective-permute-start.10 = (f32[32,256]{1,0:T(8,128)S(1)}, f32[32,256]{1,0:T(8,128)S(1)}, u32[]{:S(2)}, u32[]{:S(2)}) collective-permute-start(f32[32,256]{1,0:T(8,128)S(1)} %add_add_fusion), channel_id=1, source_target_pairs={{0,7},{1,4},{2,5},{3,6},{4,3},{5,0},{6,1},{7,2},{8,15},{9,12},{10,... | collective-permute-start | bytes 98312 | tf_op jit(solution)/shard_map/ppermute | solution.py:147
  26.0 0.2 collective-permute-start.9
  26.2 0.9 %collective-permute-done.11.refs_2_ = f32[32,256]{1,0:T(8,128)S(1)} collective-permute-done((f32[32,256]{1,0:T(8,128)S(1)}, f32[32,256]{1,0:T(8,128)S(1)}, u32[]{:S(2)}, u32[]{:S(2)}) %collective-permute-start.11) | collective-permute-done | bytes 32800 | tf_op jit(solution)/shard_map/ppermute | solution.py:147
  27.1 1.0 %collective-permute-done.10.refs_1_ = f32[32,256]{1,0:T(8,128)S(1)} collective-permute-done((f32[32,256]{1,0:T(8,128)S(1)}, f32[32,256]{1,0:T(8,128)S(1)}, u32[]{:S(2)}, u32[]{:S(2)}) %collective-permute-start.10) | collective-permute-done | bytes 32800 | tf_op jit(solution)/shard_map/ppermute | solution.py:147
  28.1 0.6 %sum.1 = f32[32,256]{1,0:T(8,128)} custom-call(f32[32,256]{1,0:T(8,128)S(1)} %collective-permute-done.9.refs_0_, f32[32,256]{1,0:T(8,128)S(1)} %collective-permute-done.10.refs_1_, f32[32,256]{1,0:T(8,128)S(1)} %collective-permute-done.11.refs_2_, f32[32,256]{1,0:T(8,128)S(1)} %collective-permute-done.12.refs_3_), custom_call_target="tpu_custom_call" | custom-call | tf_op jit(solution)/shard_map/sum/pallas_call | solution.py:272
  (13 shorter events, 0.1 us)
Async XLA Ops:
  2.0 9.1 %collective-permute-start.3 = (bf16[32,1280]{1,0:T(8,128)(2,1)S(1)}, bf16[32,1280]{1,0:T(8,128)(2,1)S(1)}, u32[]{:S(2)}, u32[]{:S(2)}) collective-permute-start(bf16[32,1280]{1,0:T(8,128)(2,1)S(1)} %get-tuple-element.33.refs_0_), channel_id=1, source_target_pairs={{0,24},{1,25},{2,26},{3,27},{4,28},{5,29},{6,30},{7,31},{8,16},{9,... | collective-permute-start | bytes 245768 | tf_op jit(solution)/shard_map/ppermute | solution.py:147
  6.0 5.2 %collective-permute-start.2 = (bf16[32,1280]{1,0:T(8,128)(2,1)S(1)}, bf16[32,1280]{1,0:T(8,128)(2,1)S(1)}, u32[]{:S(2)}, u32[]{:S(2)}) collective-permute-start(bf16[32,1280]{1,0:T(8,128)(2,1)S(1)} %get-tuple-element.33.refs_0_), channel_id=1, source_target_pairs={{0,20},{1,21},{2,22},{3,23},{4,8},{5,9},{6,10},{7,11},{8,28},{9,29... | collective-permute-start | bytes 245768 | tf_op jit(solution)/shard_map/ppermute | solution.py:147
  6.0 5.2 %collective-permute-start.1 = (bf16[32,1280]{1,0:T(8,128)(2,1)S(1)}, bf16[32,1280]{1,0:T(8,128)(2,1)S(1)}, u32[]{:S(2)}, u32[]{:S(2)}) collective-permute-start(bf16[32,1280]{1,0:T(8,128)(2,1)S(1)} %get-tuple-element.33.refs_0_), channel_id=1, source_target_pairs={{0,12},{1,13},{2,14},{3,15},{4,16},{5,17},{6,18},{7,19},{8,4},{9,5... | collective-permute-start | bytes 245768 | tf_op jit(solution)/shard_map/ppermute | solution.py:147
  7.7 3.5 %collective-permute-start = (bf16[32,1280]{1,0:T(8,128)(2,1)S(1)}, bf16[32,1280]{1,0:T(8,128)(2,1)S(1)}, u32[]{:S(2)}, u32[]{:S(2)}) collective-permute-start(bf16[32,1280]{1,0:T(8,128)(2,1)S(1)} %get-tuple-element.33.refs_0_), channel_id=1, source_target_pairs={{0,4},{1,5},{2,6},{3,7},{4,0},{5,1},{6,2},{7,3},{8,12},{9,13},{10,... | collective-permute-start | bytes 245768 | tf_op jit(solution)/shard_map/ppermute | solution.py:147
  11.2 1.7 %collective-permute-start.4 = (bf16[96,1280]{1,0:T(8,128)(2,1)S(1)}, bf16[96,1280]{1,0:T(8,128)(2,1)S(1)}, u32[]{:S(2)}, u32[]{:S(2)}) collective-permute-start(bf16[96,1280]{1,0:T(8,128)(2,1)S(1)} %constant_dynamic-update-slice_fusion.refs_1_), channel_id=1, source_target_pairs={{0,4},{1,5},{2,6},{3,7},{4,0},{5,1},{6,2},{7,3},{8,12},{9,13},{10,... | collective-permute-start | bytes 737288 | tf_op jit(solution)/shard_map/ppermute | solution.py:147
  14.2 1.4 %collective-permute-start.5 = (f32[128,256]{1,0:T(8,128)S(1)}, f32[128,256]{1,0:T(8,128)S(1)}, u32[]{:S(2)}, u32[]{:S(2)}) collective-permute-start(f32[128,256]{1,0:T(8,128)S(1)} %get-tuple-element.39), channel_id=1, source_target_pairs={{0,4},{1,5},{2,6},{3,7},{4,0},{5,1},{6,2},{7,3},{8,12},{9,13},{10,... | collective-permute-start | bytes 393224 | tf_op jit(solution)/shard_map/ppermute | solution.py:147
  15.6 4.3 %collective-permute-start.8 = (f32[32,256]{1,0:T(8,128)S(1)}, f32[32,256]{1,0:T(8,128)S(1)}, u32[]{:S(2)}, u32[]{:S(2)}) collective-permute-start(f32[32,256]{1,0:T(8,128)S(1)} %get-tuple-element.46), channel_id=1, source_target_pairs={{0,28},{1,29},{2,30},{3,31},{4,24},{5,25},{6,26},{7,27},{8,20},{9,... | collective-permute-start | bytes 98312 | tf_op jit(solution)/shard_map/ppermute | solution.py:147
  16.9 3.9 %collective-permute-start.7 = (f32[32,256]{1,0:T(8,128)S(1)}, f32[32,256]{1,0:T(8,128)S(1)}, u32[]{:S(2)}, u32[]{:S(2)}) collective-permute-start(f32[32,256]{1,0:T(8,128)S(1)} %get-tuple-element.47), channel_id=1, source_target_pairs={{0,20},{1,21},{2,22},{3,23},{4,16},{5,17},{6,18},{7,19},{8,28},{9,... | collective-permute-start | bytes 98312 | tf_op jit(solution)/shard_map/ppermute | solution.py:147
  17.4 3.4 %collective-permute-start.6 = (f32[32,256]{1,0:T(8,128)S(1)}, f32[32,256]{1,0:T(8,128)S(1)}, u32[]{:S(2)}, u32[]{:S(2)}) collective-permute-start(f32[32,256]{1,0:T(8,128)S(1)} %get-tuple-element.48), channel_id=1, source_target_pairs={{0,12},{1,13},{2,14},{3,15},{4,8},{5,9},{6,10},{7,11},{8,4},{9,5},... | collective-permute-start | bytes 98312 | tf_op jit(solution)/shard_map/ppermute | solution.py:147
  20.8 5.4 %collective-permute-start.12 = (f32[32,256]{1,0:T(8,128)S(1)}, f32[32,256]{1,0:T(8,128)S(1)}, u32[]{:S(2)}, u32[]{:S(2)}) collective-permute-start(f32[32,256]{1,0:T(8,128)S(1)} %add_add_fusion), channel_id=1, source_target_pairs={{0,5},{1,6},{2,7},{3,4},{4,1},{5,2},{6,3},{7,0},{8,13},{9,14},{10,... | collective-permute-start | bytes 98312 | tf_op jit(solution)/shard_map/ppermute | solution.py:147
  22.4 4.7 %collective-permute-start.11 = (f32[32,256]{1,0:T(8,128)S(1)}, f32[32,256]{1,0:T(8,128)S(1)}, u32[]{:S(2)}, u32[]{:S(2)}) collective-permute-start(f32[32,256]{1,0:T(8,128)S(1)} %add_add_fusion), channel_id=1, source_target_pairs={{0,6},{1,7},{2,4},{3,5},{4,2},{5,3},{6,0},{7,1},{8,14},{9,15},{10,... | collective-permute-start | bytes 98312 | tf_op jit(solution)/shard_map/ppermute | solution.py:147
  24.8 3.3 %collective-permute-start.10 = (f32[32,256]{1,0:T(8,128)S(1)}, f32[32,256]{1,0:T(8,128)S(1)}, u32[]{:S(2)}, u32[]{:S(2)}) collective-permute-start(f32[32,256]{1,0:T(8,128)S(1)} %add_add_fusion), channel_id=1, source_target_pairs={{0,7},{1,4},{2,5},{3,6},{4,3},{5,0},{6,1},{7,2},{8,15},{9,12},{10,... | collective-permute-start | bytes 98312 | tf_op jit(solution)/shard_map/ppermute | solution.py:147
  26.0 2.1 %collective-permute-start.9 = (f32[32,256]{1,0:T(8,128)S(1)}, f32[32,256]{1,0:T(8,128)S(1)}, u32[]{:S(2)}, u32[]{:S(2)}) collective-permute-start(f32[32,256]{1,0:T(8,128)S(1)} %add_add_fusion), channel_id=1, source_target_pairs={{0,4},{1,5},{2,6},{3,7},{4,0},{5,1},{6,2},{7,3},{8,12},{9,13},{10,... | collective-permute-start | bytes 98312 | tf_op jit(solution)/shard_map/ppermute | solution.py:147

commit v8 on v7

--- a/solution.py
+++ b/solution.py
@@ -246,13 +246,6 @@
         name="residual",
     )(points, point_norm, goals, *blocks)
 
-    total = (kept + to(sent, flip=1)).reshape(far, len(parts), each, outs)
-    for group in reversed(chips[1:]):
-        low = total.shape[0] // (len(group) + 1)
-        blocks = [total[i * low : (i + 1) * low] for i in range(len(group) + 1)]
-        total = pair_sum(blocks[:1] + [to(x, flip=d) for x, d in zip(blocks[1:], group)])
-    mine, *others = total[0]
-    parts = [mine] + [to(x, flip=d ^ 1) for x, d in zip(others, chips[0])]
     residual = pl.pallas_call(
         write_kernel,
         out_shape=jax.ShapeDtypeStruct(residual.shape, F32),
@@ -263,7 +256,14 @@
         cost_estimate=pl.CostEstimate(flops=0, bytes_accessed=4 << 20, transcendentals=0),
         name="write",
     )(residual)
-    parts, residual = lax.optimization_barrier((parts, residual))
+    got, residual = lax.optimization_barrier((to(sent, flip=1), residual))
+    total = (kept + got).reshape(far, len(parts), each, outs)
+    for group in reversed(chips[1:]):
+        low = total.shape[0] // (len(group) + 1)
+        blocks = [total[i * low : (i + 1) * low] for i in range(len(group) + 1)]
+        total = pair_sum(blocks[:1] + [to(x, flip=d) for x, d in zip(blocks[1:], group)])
+    mine, *others = total[0]
+    parts = [mine] + [to(x, flip=d ^ 1) for x, d in zip(others, chips[0])]
     mine = pair_sum(parts)
     flip = 1
     for low, high in reps:

time: 28.9 us -> 28.9 us (level)
  transfers between devices with their start and end apart: 13 -> 13, of which waited for: 6 -> 5; matrix products, arithmetic and copies ran while one was open for 0% -> 0% of each run, Pallas kernels for 15% -> 15%
where the time goes in v8:
time: 28.9 us; the launch traced here: 28.8 us
  starting transfers between devices  15.3 us (53%)
  Pallas kernels  7.63 us (26%)
  waiting for transfers between devices  4.98 us (17%)
  between operations  0.75 us (3%)
    ppermute x13, starting transfers between devices, send(): return lax.ppermute(x, ('blk', 'rep'), pairs)  15.3 us
    ppermute x13, waiting for transfers between devices, send(): return lax.ppermute(x, ('blk', 'rep'), pairs)  4.98 us
    pallas_call x1, Pallas kernels, per_device(): pl.pallas_call(points_kernel, out_shape=(pltpu.VMEM((count, width), BF16)...  3.41 us
    pallas_call x1, Pallas kernels, per_device(): pl.pallas_call(piece_kernel, out_shape=(pltpu.VMEM((each, width + outs),...  1.37 us
    pallas_call x1, Pallas kernels, per_device(): pl.pallas_call(functools.partial(residual_kernel, far, each, len(blocks))...  1.23 us
    pallas_call x1, Pallas kernels, per_device(): pl.pallas_call(write_kernel, out_shape=jax.ShapeDtypeStruct(residual.shap...  0.99 us
    pallas_call x1, Pallas kernels, per_device(): pl.pallas_call(sum_kernel, out_shape=jax.ShapeDtypeStruct(mine.shape, F32...  0.62 us
  transfers between devices with their start and end apart: 13, of which 5 were waited for; matrix products, arithmetic and copies ran while one was open for 0% of the time, Pallas kernels for 15%

profile of v8, /device:TPU:0, one launch (start us, length us, event | category | flops | bytes accessed | tf_op | source)
XLA Modules:
  0.0 28.8 jit_solution(1784748544194419570)
XLA Ops:
  0.6 1.4 %piece.1 = (bf16[32,1280]{1,0:T(8,128)(2,1)S(1)}, s32[8,128]{1,0:T(8,128)S(1)}, bf16[512,1024]{1,0:T(8,128)(2,1)S(1)}) custom-call(s32[1,32]{1,0:T(1,128)} %bitcast.3, bf16[64,1024]{1,0:T(8,128)(2,1)} %centers_hbm.1, bf16[32,256]{1,0:T(8,128)(2,1)} %coefs_hbm.1, s32[8,128]{1,0:T(8,128)} %bitcast.2, bf16[1280,1024]{1,0:T(8,128)(2,1)} %pool_hbm.3), custom_call_target="tpu_custom_call" | custom-call | tf_op jit(solution)/shard_map/piece/pallas_call | solution.py:170
  2.0 4.0 %collective-permute-start.3 = (bf16[32,1280]{1,0:T(8,128)(2,1)S(1)}, bf16[32,1280]{1,0:T(8,128)(2,1)S(1)}, u32[]{:S(2)}, u32[]{:S(2)}) collective-permute-start(bf16[32,1280]{1,0:T(8,128)(2,1)S(1)} %get-tuple-element.30.refs_0_), channel_id=1, source_target_pairs={{0,24},{1,25},{2,26},{3,27},{4,28},{5,29},{6,30},{7,31},{8,16},{9,... | collective-permute-start | bytes 245768 | tf_op jit(solution)/shard_map/ppermute | solution.py:147
  6.0 0.0 collective-permute-start.2
  6.0 1.7 %collective-permute-start.1 = (bf16[32,1280]{1,0:T(8,128)(2,1)S(1)}, bf16[32,1280]{1,0:T(8,128)(2,1)S(1)}, u32[]{:S(2)}, u32[]{:S(2)}) collective-permute-start(bf16[32,1280]{1,0:T(8,128)(2,1)S(1)} %get-tuple-element.30.refs_0_), channel_id=1, source_target_pairs={{0,12},{1,13},{2,14},{3,15},{4,16},{5,17},{6,18},{7,19},{8,4},{9,5... | collective-permute-start | bytes 245768 | tf_op jit(solution)/shard_map/ppermute | solution.py:147
  7.7 0.0 collective-permute-start
  7.7 3.4 %points.1 = (bf16[1024,1024]{1,0:T(8,128)(2,1)S(1)}, f32[1024,1]{1,0:T(8,128)S(1)}, bf16[1024,256]{1,0:T(8,128)(2,1)S(1)}) custom-call(s32[8,128]{1,0:T(8,128)S(1)} %get-tuple-element.22.rows_ref, bf16[512,1024]{1,0:T(8,128)(2,1)S(1)} %get-tuple-element.23.first_ref, bf16[1280,1024]{1,0:T(8,128)(2,1)} %pool_hbm.3, bf16[1024,256]{1,0:T(8,128)(2,1)} %targets_hbm.1), custom_call_target="tpu_custom_call" | custom-call | flops 2147483648 | bytes 5242880 | tf_op jit(solution)/shard_map/points/pallas_call | solution.py:199
  11.1 0.0 collective-permute-done.3
  11.2 0.6 %collective-permute-start.4 = (bf16[96,1280]{1,0:T(8,128)(2,1)S(1)}, bf16[96,1280]{1,0:T(8,128)(2,1)S(1)}, u32[]{:S(2)}, u32[]{:S(2)}) collective-permute-start(bf16[96,1280]{1,0:T(8,128)(2,1)S(1)} %constant_dynamic-update-slice_fusion.refs_1_), channel_id=1, source_target_pairs={{0,4},{1,5},{2,6},{3,7},{4,0},{5,1},{6,2},{7,3},{8,12},{9,13},{10,... | collective-permute-start | bytes 737288 | tf_op jit(solution)/shard_map/ppermute | solution.py:147
  11.8 1.1 %collective-permute-done.4.refs_3_ = bf16[96,1280]{1,0:T(8,128)(2,1)S(1)} collective-permute-done((bf16[96,1280]{1,0:T(8,128)(2,1)S(1)}, bf16[96,1280]{1,0:T(8,128)(2,1)S(1)}, u32[]{:S(2)}, u32[]{:S(2)}) %collective-permute-start.4) | collective-permute-done | bytes 245792 | tf_op jit(solution)/shard_map/ppermute | solution.py:147
  12.9 1.2 %residual.1 = (f32[1024,256]{1,0:T(8,128)S(1)}, f32[128,256]{1,0:T(8,128)S(1)}, f32[128,256]{1,0:T(8,128)S(1)}) custom-call(bf16[1024,1024]{1,0:T(8,128)(2,1)S(1)} %get-tuple-element.27.points_ref, f32[1024,1]{1,0:T(8,128)S(1)} %get-tuple-element.28.norm_ref, bf16[1024,256]{1,0:T(8,128)(2,1)S(1)} %get-tuple-element.29.targets_ref, ...), custom_call_target="tpu_custom_call" | custom-call | tf_op jit(solution)/shard_map/residual/pallas_call | solution.py:230
  14.2 0.4 %collective-permute-start.5 = (f32[128,256]{1,0:T(8,128)S(1)}, f32[128,256]{1,0:T(8,128)S(1)}, u32[]{:S(2)}, u32[]{:S(2)}) collective-permute-start(f32[128,256]{1,0:T(8,128)S(1)} %get-tuple-element.35), channel_id=1, source_target_pairs={{0,4},{1,5},{2,6},{3,7},{4,0},{5,1},{6,2},{7,3},{8,12},{9,13},{10,... | collective-permute-start | bytes 393224 | tf_op jit(solution)/shard_map/ppermute | solution.py:147
  14.6 1.0 %write.1 = f32[1024,256]{1,0:T(8,128)} custom-call(f32[1024,256]{1,0:T(8,128)S(1)} %get-tuple-element.36.source), custom_call_target="tpu_custom_call" | custom-call | bytes 4194304 | tf_op jit(solution)/shard_map/write/pallas_call | solution.py:249
  15.7 1.3 %collective-permute-start.8 = (f32[32,256]{1,0:T(8,128)S(1)}, f32[32,256]{1,0:T(8,128)S(1)}, u32[]{:S(2)}, u32[]{:S(2)}) collective-permute-start(f32[32,256]{1,0:T(8,128)S(1)} %get-tuple-element.40), channel_id=1, source_target_pairs={{0,28},{1,29},{2,30},{3,31},{4,24},{5,25},{6,26},{7,27},{8,20},{9,... | collective-permute-start | bytes 98312 | tf_op jit(solution)/shard_map/ppermute | solution.py:147
  17.0 0.5 %collective-permute-start.7 = (f32[32,256]{1,0:T(8,128)S(1)}, f32[32,256]{1,0:T(8,128)S(1)}, u32[]{:S(2)}, u32[]{:S(2)}) collective-permute-start(f32[32,256]{1,0:T(8,128)S(1)} %get-tuple-element.41), channel_id=1, source_target_pairs={{0,20},{1,21},{2,22},{3,23},{4,16},{5,17},{6,18},{7,19},{8,28},{9,... | collective-permute-start | bytes 98312 | tf_op jit(solution)/shard_map/ppermute | solution.py:147
  17.5 1.4 %collective-permute-start.6 = (f32[32,256]{1,0:T(8,128)S(1)}, f32[32,256]{1,0:T(8,128)S(1)}, u32[]{:S(2)}, u32[]{:S(2)}) collective-permute-start(f32[32,256]{1,0:T(8,128)S(1)} %get-tuple-element.42), channel_id=1, source_target_pairs={{0,12},{1,13},{2,14},{3,15},{4,8},{5,9},{6,10},{7,11},{8,4},{9,5},... | collective-permute-start | bytes 98312 | tf_op jit(solution)/shard_map/ppermute | solution.py:147
  18.9 1.1 %collective-permute-done.8 = f32[32,256]{1,0:T(8,128)S(1)} collective-permute-done((f32[32,256]{1,0:T(8,128)S(1)}, f32[32,256]{1,0:T(8,128)S(1)}, u32[]{:S(2)}, u32[]{:S(2)}) %collective-permute-start.8) | collective-permute-done | bytes 32800 | tf_op jit(solution)/shard_map/ppermute | solution.py:147
  20.0 0.9 %collective-permute-done.7 = f32[32,256]{1,0:T(8,128)S(1)} collective-permute-done((f32[32,256]{1,0:T(8,128)S(1)}, f32[32,256]{1,0:T(8,128)S(1)}, u32[]{:S(2)}, u32[]{:S(2)}) %collective-permute-start.7) | collective-permute-done | bytes 32800 | tf_op jit(solution)/shard_map/ppermute | solution.py:147
  20.9 1.5 %collective-permute-start.12 = (f32[32,256]{1,0:T(8,128)S(1)}, f32[32,256]{1,0:T(8,128)S(1)}, u32[]{:S(2)}, u32[]{:S(2)}) collective-permute-start(f32[32,256]{1,0:T(8,128)S(1)} %fusion), channel_id=1, source_target_pairs={{0,5},{1,6},{2,7},{3,4},{4,1},{5,2},{6,3},{7,0},{8,13},{9,14},{10,... | collective-permute-start | bytes 98312 | tf_op jit(solution)/shard_map/ppermute | solution.py:147
  22.4 2.4 %collective-permute-start.11 = (f32[32,256]{1,0:T(8,128)S(1)}, f32[32,256]{1,0:T(8,128)S(1)}, u32[]{:S(2)}, u32[]{:S(2)}) collective-permute-start(f32[32,256]{1,0:T(8,128)S(1)} %fusion), channel_id=1, source_target_pairs={{0,6},{1,7},{2,4},{3,5},{4,2},{5,3},{6,0},{7,1},{8,14},{9,15},{10,... | collective-permute-start | bytes 98312 | tf_op jit(solution)/shard_map/ppermute | solution.py:147
  24.8 1.2 %collective-permute-start.10 = (f32[32,256]{1,0:T(8,128)S(1)}, f32[32,256]{1,0:T(8,128)S(1)}, u32[]{:S(2)}, u32[]{:S(2)}) collective-permute-start(f32[32,256]{1,0:T(8,128)S(1)} %fusion), channel_id=1, source_target_pairs={{0,7},{1,4},{2,5},{3,6},{4,3},{5,0},{6,1},{7,2},{8,15},{9,12},{10,... | collective-permute-start | bytes 98312 | tf_op jit(solution)/shard_map/ppermute | solution.py:147
  26.0 0.2 collective-permute-start.9
  26.3 0.8 %collective-permute-done.11.refs_2_ = f32[32,256]{1,0:T(8,128)S(1)} collective-permute-done((f32[32,256]{1,0:T(8,128)S(1)}, f32[32,256]{1,0:T(8,128)S(1)}, u32[]{:S(2)}, u32[]{:S(2)}) %collective-permute-start.11) | collective-permute-done | bytes 32800 | tf_op jit(solution)/shard_map/ppermute | solution.py:147
  27.1 1.1 %collective-permute-done.10.refs_1_ = f32[32,256]{1,0:T(8,128)S(1)} collective-permute-done((f32[32,256]{1,0:T(8,128)S(1)}, f32[32,256]{1,0:T(8,128)S(1)}, u32[]{:S(2)}, u32[]{:S(2)}) %collective-permute-start.10) | collective-permute-done | bytes 32800 | tf_op jit(solution)/shard_map/ppermute | solution.py:147
  28.1 0.6 %sum.1 = f32[32,256]{1,0:T(8,128)} custom-call(f32[32,256]{1,0:T(8,128)S(1)} %collective-permute-done.9.refs_0_, f32[32,256]{1,0:T(8,128)S(1)} %collective-permute-done.10.refs_1_, f32[32,256]{1,0:T(8,128)S(1)} %collective-permute-done.11.refs_2_, f32[32,256]{1,0:T(8,128)S(1)} %collective-permute-done.12.refs_3_), custom_call_target="tpu_custom_call" | custom-call | tf_op jit(solution)/shard_map/sum/pallas_call | solution.py:272
  (13 shorter events, 0.1 us)
Async XLA Ops:
  2.0 9.1 %collective-permute-start.3 = (bf16[32,1280]{1,0:T(8,128)(2,1)S(1)}, bf16[32,1280]{1,0:T(8,128)(2,1)S(1)}, u32[]{:S(2)}, u32[]{:S(2)}) collective-permute-start(bf16[32,1280]{1,0:T(8,128)(2,1)S(1)} %get-tuple-element.30.refs_0_), channel_id=1, source_target_pairs={{0,24},{1,25},{2,26},{3,27},{4,28},{5,29},{6,30},{7,31},{8,16},{9,... | collective-permute-start | bytes 245768 | tf_op jit(solution)/shard_map/ppermute | solution.py:147
  6.0 5.2 %collective-permute-start.2 = (bf16[32,1280]{1,0:T(8,128)(2,1)S(1)}, bf16[32,1280]{1,0:T(8,128)(2,1)S(1)}, u32[]{:S(2)}, u32[]{:S(2)}) collective-permute-start(bf16[32,1280]{1,0:T(8,128)(2,1)S(1)} %get-tuple-element.30.refs_0_), channel_id=1, source_target_pairs={{0,20},{1,21},{2,22},{3,23},{4,8},{5,9},{6,10},{7,11},{8,28},{9,29... | collective-permute-start | bytes 245768 | tf_op jit(solution)/shard_map/ppermute | solution.py:147
  6.0 5.2 %collective-permute-start.1 = (bf16[32,1280]{1,0:T(8,128)(2,1)S(1)}, bf16[32,1280]{1,0:T(8,128)(2,1)S(1)}, u32[]{:S(2)}, u32[]{:S(2)}) collective-permute-start(bf16[32,1280]{1,0:T(8,128)(2,1)S(1)} %get-tuple-element.30.refs_0_), channel_id=1, source_target_pairs={{0,12},{1,13},{2,14},{3,15},{4,16},{5,17},{6,18},{7,19},{8,4},{9,5... | collective-permute-start | bytes 245768 | tf_op jit(solution)/shard_map/ppermute | solution.py:147
  7.7 3.5 %collective-permute-start = (bf16[32,1280]{1,0:T(8,128)(2,1)S(1)}, bf16[32,1280]{1,0:T(8,128)(2,1)S(1)}, u32[]{:S(2)}, u32[]{:S(2)}) collective-permute-start(bf16[32,1280]{1,0:T(8,128)(2,1)S(1)} %get-tuple-element.30.refs_0_), channel_id=1, source_target_pairs={{0,4},{1,5},{2,6},{3,7},{4,0},{5,1},{6,2},{7,3},{8,12},{9,13},{10,... | collective-permute-start | bytes 245768 | tf_op jit(solution)/shard_map/ppermute | solution.py:147
  11.2 1.7 %collective-permute-start.4 = (bf16[96,1280]{1,0:T(8,128)(2,1)S(1)}, bf16[96,1280]{1,0:T(8,128)(2,1)S(1)}, u32[]{:S(2)}, u32[]{:S(2)}) collective-permute-start(bf16[96,1280]{1,0:T(8,128)(2,1)S(1)} %constant_dynamic-update-slice_fusion.refs_1_), channel_id=1, source_target_pairs={{0,4},{1,5},{2,6},{3,7},{4,0},{5,1},{6,2},{7,3},{8,12},{9,13},{10,... | collective-permute-start | bytes 737288 | tf_op jit(solution)/shard_map/ppermute | solution.py:147
  14.2 1.4 %collective-permute-start.5 = (f32[128,256]{1,0:T(8,128)S(1)}, f32[128,256]{1,0:T(8,128)S(1)}, u32[]{:S(2)}, u32[]{:S(2)}) collective-permute-start(f32[128,256]{1,0:T(8,128)S(1)} %get-tuple-element.35), channel_id=1, source_target_pairs={{0,4},{1,5},{2,6},{3,7},{4,0},{5,1},{6,2},{7,3},{8,12},{9,13},{10,... | collective-permute-start | bytes 393224 | tf_op jit(solution)/shard_map/ppermute | solution.py:147
  15.7 4.3 %collective-permute-start.8 = (f32[32,256]{1,0:T(8,128)S(1)}, f32[32,256]{1,0:T(8,128)S(1)}, u32[]{:S(2)}, u32[]{:S(2)}) collective-permute-start(f32[32,256]{1,0:T(8,128)S(1)} %get-tuple-element.40), channel_id=1, source_target_pairs={{0,28},{1,29},{2,30},{3,31},{4,24},{5,25},{6,26},{7,27},{8,20},{9,... | collective-permute-start | bytes 98312 | tf_op jit(solution)/shard_map/ppermute | solution.py:147
  17.0 3.9 %collective-permute-start.7 = (f32[32,256]{1,0:T(8,128)S(1)}, f32[32,256]{1,0:T(8,128)S(1)}, u32[]{:S(2)}, u32[]{:S(2)}) collective-permute-start(f32[32,256]{1,0:T(8,128)S(1)} %get-tuple-element.41), channel_id=1, source_target_pairs={{0,20},{1,21},{2,22},{3,23},{4,16},{5,17},{6,18},{7,19},{8,28},{9,... | collective-permute-start | bytes 98312 | tf_op jit(solution)/shard_map/ppermute | solution.py:147
  17.5 3.4 %collective-permute-start.6 = (f32[32,256]{1,0:T(8,128)S(1)}, f32[32,256]{1,0:T(8,128)S(1)}, u32[]{:S(2)}, u32[]{:S(2)}) collective-permute-start(f32[32,256]{1,0:T(8,128)S(1)} %get-tuple-element.42), channel_id=1, source_target_pairs={{0,12},{1,13},{2,14},{3,15},{4,8},{5,9},{6,10},{7,11},{8,4},{9,5},... | collective-permute-start | bytes 98312 | tf_op jit(solution)/shard_map/ppermute | solution.py:147
  20.9 5.4 %collective-permute-start.12 = (f32[32,256]{1,0:T(8,128)S(1)}, f32[32,256]{1,0:T(8,128)S(1)}, u32[]{:S(2)}, u32[]{:S(2)}) collective-permute-start(f32[32,256]{1,0:T(8,128)S(1)} %fusion), channel_id=1, source_target_pairs={{0,5},{1,6},{2,7},{3,4},{4,1},{5,2},{6,3},{7,0},{8,13},{9,14},{10,... | collective-permute-start | bytes 98312 | tf_op jit(solution)/shard_map/ppermute | solution.py:147
  22.4 4.7 %collective-permute-start.11 = (f32[32,256]{1,0:T(8,128)S(1)}, f32[32,256]{1,0:T(8,128)S(1)}, u32[]{:S(2)}, u32[]{:S(2)}) collective-permute-start(f32[32,256]{1,0:T(8,128)S(1)} %fusion), channel_id=1, source_target_pairs={{0,6},{1,7},{2,4},{3,5},{4,2},{5,3},{6,0},{7,1},{8,14},{9,15},{10,... | collective-permute-start | bytes 98312 | tf_op jit(solution)/shard_map/ppermute | solution.py:147
  24.8 3.3 %collective-permute-start.10 = (f32[32,256]{1,0:T(8,128)S(1)}, f32[32,256]{1,0:T(8,128)S(1)}, u32[]{:S(2)}, u32[]{:S(2)}) collective-permute-start(f32[32,256]{1,0:T(8,128)S(1)} %fusion), channel_id=1, source_target_pairs={{0,7},{1,4},{2,5},{3,6},{4,3},{5,0},{6,1},{7,2},{8,15},{9,12},{10,... | collective-permute-start | bytes 98312 | tf_op jit(solution)/shard_map/ppermute | solution.py:147
  26.0 2.1 %collective-permute-start.9 = (f32[32,256]{1,0:T(8,128)S(1)}, f32[32,256]{1,0:T(8,128)S(1)}, u32[]{:S(2)}, u32[]{:S(2)}) collective-permute-start(f32[32,256]{1,0:T(8,128)S(1)} %fusion), channel_id=1, source_target_pairs={{0,4},{1,5},{2,6},{3,7},{4,0},{5,1},{6,2},{7,3},{8,12},{9,13},{10,... | collective-permute-start | bytes 98312 | tf_op jit(solution)/shard_map/ppermute | solution.py:147
